TPU v7x, 512 devices: a whole 4x4x16 slice. The times are simulated.
512 devices in a mesh: px: 16 (over y, x), py: 32 (over z, core).
Axes of the slice: x: 4, y: 4, z: 16, core: 2. Of those that a mesh axis runs over, the one named last changes fastest.
Arguments:
- offsets: float32 [3, 64, 256, 128], P(None, 'px', 'py'), may hold values from -0.12 to 0.12
- block: float32 [48, 64, 256, 128], P(None, 'px', 'py')
- prior: float32 [48, 64, 256, 128], P(None, 'px', 'py')
Outputs:
- new_block: float32 [48, 64, 256, 128], P(None, 'px', 'py')
- search: float32 [48, 64, 256, 128], P(None, 'px', 'py')
All inputs are finite; a program needn't handle non-finite values. Where the computation divides by a largest or mean magnitude, that divisor is 1e-20 or more.
Results may differ from a plain program's by a relative error of at most 0.0003.
Values sent between devices are 32-bit elements; how exact they have to be, the bound alone decides.
No kernel may reach another device: no remote copies, remote signals or barrier semaphores. Data moves between devices by JAX's collectives and lax.ppermute only.
A program may use at most 128 MiB of HBM per device.

v0:
```python
import jax
import jax.numpy as jnp
from jax import lax
from jax.sharding import PartitionSpec as P


def padded_2(cells, sides, width):
    for axis, dim in sides:
        count = lax.axis_size(axis)
        ends = count - 1
        head = lax.slice_in_dim(cells, 0, width, axis=dim)
        tail = lax.slice_in_dim(cells, cells.shape[dim] - width, cells.shape[dim], axis=dim)
        cells = jnp.concatenate(
            [
                lax.ppermute(tail, axis, [(i, (i + 1) % count) for i in range(ends)]),
                cells,
                lax.ppermute(head, axis, [((i + 1) % count, i) for i in range(ends)]),
            ],
            axis=dim,
        )
    return cells


def kuhn_tetrahedra():
    orders = [(0, 1, 2), (0, 2, 1), (1, 0, 2), (1, 2, 0), (2, 0, 1), (2, 1, 0)]
    tetrahedra = []
    for ordering in orders:
        corner = [0, 0, 0]
        corners = [(0, 0, 0)]
        for axis_step in ordering:
            corner[axis_step] = 1
            corners.append((corner[0], corner[1], corner[2]))
        tetrahedra.append(corners)
    return tetrahedra


def stencil_offsets():
    distinct = []
    for corners in kuhn_tetrahedra():
        for first_corner in corners:
            for second_corner in corners:
                shift_key = (
                    second_corner[0] - first_corner[0],
                    second_corner[1] - first_corner[1],
                    second_corner[2] - first_corner[2],
                )
                if shift_key not in distinct:
                    distinct.append(shift_key)
    return sorted(distinct)


def corner_slice(positions, corner):
    cells_a = positions.shape[1] - 1
    cells_b = positions.shape[2] - 1
    depth = positions.shape[3]
    return positions[
        :,
        corner[0] : corner[0] + cells_a,
        corner[1] : corner[1] + cells_b,
        corner[2] : corner[2] + depth - 1,
    ]


def placed_at(entry_value, corner):
    return jnp.pad(
        entry_value,
        ((corner[0], 1 - corner[0]), (corner[1], 1 - corner[1]), (corner[2], 1 - corner[2])),
    )


def assemble(positions, cell_valid):
    offsets_list = stencil_offsets()
    full_shape = positions.shape[1:]
    inside = cell_valid[:, :, None]
    entry_sums = {}
    mass_sums = {}
    for corners in kuhn_tetrahedra():
        anchor = corner_slice(positions, corners[0])
        edge_one = corner_slice(positions, corners[1]) - anchor
        edge_two = corner_slice(positions, corners[2]) - anchor
        edge_three = corner_slice(positions, corners[3]) - anchor
        grad_one = jnp.cross(edge_two, edge_three, axis=0)
        grad_two = jnp.cross(edge_three, edge_one, axis=0)
        grad_three = jnp.cross(edge_one, edge_two, axis=0)
        gradients = [-(grad_one + grad_two + grad_three), grad_one, grad_two, grad_three]
        determinant = jnp.sum(edge_one * grad_one, axis=0)
        volume_six = jnp.where(inside, jnp.abs(determinant), 1.0)
        weight = jnp.where(inside, 1.0 / (6.0 * volume_six), 0.0)
        for first in range(4):
            for second in range(4):
                entry_value = jnp.sum(gradients[first] * gradients[second], axis=0) * weight
                shift_key = (
                    corners[second][0] - corners[first][0],
                    corners[second][1] - corners[first][1],
                    corners[second][2] - corners[first][2],
                )
                slot_key = (corners[first], offsets_list.index(shift_key))
                if slot_key in entry_sums:
                    entry_sums[slot_key] = entry_sums[slot_key] + entry_value
                else:
                    entry_sums[slot_key] = entry_value
        portion = jnp.where(inside, volume_six / 24.0, 0.0)
        for corner in corners:
            if corner in mass_sums:
                mass_sums[corner] = mass_sums[corner] + portion
            else:
                mass_sums[corner] = portion
    totals = [jnp.zeros(full_shape, jnp.float32) for entry in offsets_list]
    for slot_key in entry_sums:
        totals[slot_key[1]] = totals[slot_key[1]] + placed_at(entry_sums[slot_key], slot_key[0])
    mass_total = jnp.zeros(full_shape, jnp.float32)
    for corner in mass_sums:
        mass_total = mass_total + placed_at(mass_sums[corner], corner)
    coefs = jnp.stack([entry[1:-1, 1:-1, :] for entry in totals])
    return (coefs, mass_total[1:-1, 1:-1, :])


def window_positions(extended_offsets, index_a, index_b):
    depth = extended_offsets.shape[3]
    grid_a = jnp.broadcast_to(
        index_a.astype(jnp.float32)[:, None, None], extended_offsets.shape[1:]
    )
    grid_b = jnp.broadcast_to(
        index_b.astype(jnp.float32)[None, :, None], extended_offsets.shape[1:]
    )
    grid_c = jnp.broadcast_to(
        jnp.arange(depth, dtype=jnp.int32).astype(jnp.float32)[None, None, :],
        extended_offsets.shape[1:],
    )
    return jnp.stack([grid_a, grid_b, grid_c]) + extended_offsets


def stiffness_apply(extended, coefs):
    offsets_list = stencil_offsets()
    rows_a = extended.shape[1] - 2
    rows_b = extended.shape[2] - 2
    depth = extended.shape[3]
    padded = jnp.pad(extended, ((0, 0), (0, 0), (0, 0), (1, 1)))
    result = jnp.zeros((extended.shape[0], rows_a, rows_b, depth), jnp.float32)
    for position, shift_key in enumerate(offsets_list):
        result = (
            result
            + coefs[position]
            * padded[
                :,
                1 + shift_key[0] : 1 + shift_key[0] + rows_a,
                1 + shift_key[1] : 1 + shift_key[1] + rows_b,
                1 + shift_key[2] : 1 + shift_key[2] + depth,
            ]
        )
    return result


def ritz(gram_k, gram_m, vecs):
    lower = jnp.linalg.cholesky(gram_m)
    half = jax.scipy.linalg.solve_triangular(lower, gram_k, lower=True)
    reduced = jax.scipy.linalg.solve_triangular(lower, half.T, lower=True)
    bound = jnp.max(jnp.sum(jnp.abs(reduced), axis=1))
    shifted = jnp.eye(reduced.shape[0], dtype=jnp.float32) - reduced / bound
    filtered = jnp.dot(shifted, shifted[:, :vecs], precision=lax.Precision.HIGHEST)
    return jax.scipy.linalg.solve_triangular(lower, filtered, lower=True, trans=1)


def local_grams(vectors, k_vectors, mass):
    flat = vectors.reshape(vectors.shape[0], -1)
    k_flat = k_vectors.reshape(vectors.shape[0], -1)
    m_flat = flat * mass.reshape(1, -1)
    gram_k = lax.dot_general(
        flat, k_flat, (((1,), (1,)), ((), ())), precision=lax.Precision.HIGHEST
    )
    gram_m = lax.dot_general(
        flat, m_flat, (((1,), (1,)), ((), ())), precision=lax.Precision.HIGHEST
    )
    return (gram_k, gram_m)


def shards(offsets, block, prior):
    vecs = block.shape[0]
    rows_a = block.shape[1]
    rows_b = block.shape[2]
    depth = block.shape[3]
    total_a = rows_a * lax.axis_size("px")
    total_b = rows_b * lax.axis_size("py")
    start_a = lax.axis_index("px") * rows_a
    start_b = lax.axis_index("py") * rows_b
    extended_offsets = padded_2(offsets, (("px", 1), ("py", 2)), 2)
    index_a = start_a - 2 + jnp.arange(rows_a + 4, dtype=jnp.int32)
    index_b = start_b - 2 + jnp.arange(rows_b + 4, dtype=jnp.int32)
    positions = window_positions(extended_offsets, index_a, index_b)
    cells_a = index_a[:-1]
    cells_b = index_b[:-1]
    valid_a = (cells_a >= 0) & (cells_a <= total_a - 2)
    valid_b = (cells_b >= 0) & (cells_b <= total_b - 2)
    coefs_wide, mass_wide = assemble(positions, valid_a[:, None] & valid_b[None, :])
    coefs = coefs_wide[:, 1:-1, 1:-1, :]
    mass = mass_wide[1:-1, 1:-1, :]
    centre = stencil_offsets().index((0, 0, 0))
    diagonal = coefs[centre]
    first_rim = padded_2(block, (("px", 1), ("py", 2)), 1)
    k_block = stiffness_apply(first_rim, coefs)
    m_block = mass * block
    numer, denom = lax.psum(
        (jnp.sum(block * k_block, axis=(1, 2, 3)), jnp.sum(block * m_block, axis=(1, 2, 3))),
        ("px", "py"),
    )
    quotient = numer / denom
    search = (k_block - quotient[:, None, None, None] * m_block) / diagonal
    second_rim = padded_2(jnp.concatenate([search, prior]), (("px", 1), ("py", 2)), 1)
    applied = stiffness_apply(second_rim, coefs)
    k_search = applied[:vecs]
    k_prior = applied[vecs:]
    basis = jnp.concatenate([block, search, prior])
    k_basis = jnp.concatenate([k_block, k_search, k_prior])
    gram_k, gram_m = lax.psum(local_grams(basis, k_basis, mass), ("px", "py"))
    coeffs = ritz(gram_k, gram_m, vecs)
    scale = jnp.sqrt(jnp.float32(total_a * total_b * depth))
    flat_basis = basis.reshape(basis.shape[0], -1)
    new_block = scale * lax.dot_general(
        coeffs, flat_basis, (((0,), (0,)), ((), ())), precision=lax.Precision.HIGHEST
    )
    return (new_block.reshape(block.shape), search)


def solution(mesh):
    in_specs = (P(None, "px", "py", None), P(None, "px", "py", None), P(None, "px", "py", None))
    out_specs = (P(None, "px", "py", None), P(None, "px", "py", None))
    return jax.shard_map(shards, mesh=mesh, in_specs=in_specs, out_specs=out_specs, check_vma=False)
```

profile of v0, /device:TPU:1, one launch (start us, length us, event | category | flops | bytes accessed | tf_op | source)
XLA Modules:
  0.0 725.1 jit_solution(15556272561452814514)
XLA Ops:
  8.1 3.9 collective-permute-start
  14.9 4.0 collective-permute-start.4
  20.5 4.9 collective-permute-start.2
  25.4 3.0 collective-permute-start.3
  36.1 1.9 collective-permute-start.6
  38.0 2.4 collective-permute-start.7
  40.5 3.9 collective-permute-done.7
  45.4 3.9 fusion.37
  49.3 114.8 %all-reduce.61 = (f32[48]{0:T(128)S(1)}, f32[48]{0:T(128)S(1)}) all-reduce(f32[48]{0:T(128)S(1)} %get-tuple-element.55, f32[48]{0:T(128)S(1)} %get-tuple-element.54), channel_id=1, replica_groups=mesh['px'=16,'py'=32] {'px','py'}, use_global_device_ids=true, to_apply=%region_61.63 | all-reduce | flops 96 | bytes 768 | tf_op jit(solution)/shard_map/psum | solution.py:202
  165.8 2.9 collective-permute-start.8
  170.1 6.4 collective-permute-done.8
  176.5 3.8 collective-permute-done.9
  180.4 2.2 collective-permute-start.10
  182.6 3.1 collective-permute-start.11
  185.6 2.8 fusion.34
  188.4 2.2 collective-permute-done.11
  191.6 4.3 select_maximum_fusion
  196.0 3.2 fusion.18
  199.3 2.7 fusion.31
  204.1 456.7 %all-reduce.65.cloned.1.call-done = (f32[144,144]{1,0:T(8,128)}, f32[144,144]{0,1:T(8,128)}) async-done(((f32[144,144]{1,0:T(8,128)}, f32[144,144]{0,1:T(8,128)}), (f32[144,144]{1,0:T(8,128)}, f32[144,144]{0,1:T(8,128)})) %all-reduce.65.cloned.1.call-update) | async-done | bytes 165904 | tf_op jit(solution)/shard_map/psum | solution.py:214
  662.7 11.7 %cholesky.51 = f32[128,128]{1,0:T(8,128)S(1)} custom-call(f32[128,128]{1,0:T(8,128)S(1)} %cholesky.124), custom_call_target="Cholesky" | custom-call | tf_op jit(solution)/shard_map/jit(cholesky)/cholesky | solution.py:155
  674.5 9.8 %custom-call.18 = f32[1,128,128]{1,2,0:T(8,128)S(1)} custom-call(f32[1,128,128]{2,1,0:T(8,128)S(1)} %get-tuple-element.248), custom_call_target="InvertDiagBlocksLowerTriangular" | custom-call | tf_op jit(solution)/shard_map/jit(cholesky)/cholesky | solution.py:155
  689.0 19.9 %custom-call.19 = f32[2,128,128]{1,2,0:T(8,128)S(1)} custom-call(f32[2,128,128]{2,1,0:T(8,128)S(1)} %pad_maximum_fusion.28), custom_call_target="InvertDiagBlocksLowerTriangular" | custom-call | tf_op jit(solution)/shard_map/jit(_solve_triangular)/triangular_solve | solution.py:161
  714.5 2.7 fusion.27
  (187 shorter events, 31.3 us)
Async XLA Ops:
  7.2 13.2 %copy-start.3 = (f32[3,4,8,128]{3,2,1,0:T(8,128)S(1)}, f32[3,4,8,128]{3,2,1,0:T(8,128)}, u32[]{:S(2)}) copy-start(f32[3,4,8,128]{3,2,1,0:T(8,128)} %param.7) | copy-start | bytes 147460
  7.2 21.3 %copy-start.2 = (f32[48,4,8,128]{3,2,1,0:T(8,128)S(1)}, f32[48,4,8,128]{3,2,1,0:T(8,128)}, u32[]{:S(2)}) copy-start(f32[48,4,8,128]{3,2,1,0:T(8,128)} %param.9) | copy-start | bytes 2359300
  7.2 653.6 %all-reduce.65.cloned.1.call-start = ((), (), s32[]{:S(2)}) async-start(), calls=%async_computation | async-start | bytes 589824 | tf_op jit(solution)/shard_map/psum | solution.py:214
  8.1 12.3 %collective-permute-start = (f32[3,2,8,128]{3,2,1,0:T(8,128)S(1)}, f32[3,2,8,128]{3,2,1,0:T(8,128)S(1)}, u32[]{:S(2)}, u32[]{:S(2)}) collective-permute-start(f32[3,2,8,128]{3,2,1,0:T(8,128)S(1)} %get-tuple-element.264), channel_id=1, source_target_pairs={{0,32},{32,64},{64,96},{96,128},{128,160},{160,192},{192,224},{224... | collective-permute-start | bytes 73736 | tf_op jit(solution)/shard_map/ppermute | solution.py:15
  12.0 8.4 %collective-permute-start.1 = (f32[3,2,8,128]{3,2,1,0:T(8,128)S(1)}, f32[3,2,8,128]{3,2,1,0:T(8,128)S(1)}, u32[]{:S(2)}, u32[]{:S(2)}) collective-permute-start(f32[3,2,8,128]{3,2,1,0:T(8,128)S(1)} %get-tuple-element.263), channel_id=1, source_target_pairs={{32,0},{64,32},{96,64},{128,96},{160,128},{192,160},{224,192},{256... | collective-permute-start | bytes 73736 | tf_op jit(solution)/shard_map/ppermute | solution.py:17
  14.9 20.6 %collective-permute-start.4 = (f32[48,1,8,128]{3,0,2,1:T(8,128)S(1)}, f32[48,1,8,128]{3,0,2,1:T(8,128)S(1)}, u32[]{:S(2)}, u32[]{:S(2)}) collective-permute-start(f32[48,1,8,128]{3,0,2,1:T(8,128)S(1)} %get-tuple-element.137), channel_id=1, source_target_pairs={{0,32},{32,64},{64,96},{96,128},{128,160},{160,192},{192,224},{224... | collective-permute-start | bytes 589832 | tf_op jit(solution)/shard_map/ppermute | solution.py:15
  18.9 17.1 %collective-permute-start.5 = (f32[48,1,8,128]{3,0,2,1:T(8,128)S(1)}, f32[48,1,8,128]{3,0,2,1:T(8,128)S(1)}, u32[]{:S(2)}, u32[]{:S(2)}) collective-permute-start(f32[48,1,8,128]{3,0,2,1:T(8,128)S(1)} %get-tuple-element.136), channel_id=1, source_target_pairs={{32,0},{64,32},{96,64},{128,96},{160,128},{192,160},{224,192},{256... | collective-permute-start | bytes 589832 | tf_op jit(solution)/shard_map/ppermute | solution.py:17
  20.5 8.5 %collective-permute-start.2 = (f32[3,8,2,128]{3,2,1,0:T(2,128)S(1)}, f32[3,8,2,128]{3,2,1,0:T(2,128)S(1)}, u32[]{:S(2)}, u32[]{:S(2)}) collective-permute-start(f32[3,8,2,128]{3,2,1,0:T(2,128)S(1)} %get-tuple-element.245), channel_id=1, source_target_pairs={{0,1},{1,2},{2,3},{3,4},{4,5},{5,6},{6,7},{7,8},{8,9},{9,10},{10,1... | collective-permute-start | bytes 73736 | tf_op jit(solution)/shard_map/ppermute | solution.py:15
  25.4 5.4 collective-permute-start.3
  34.8 10.4 %copy-start.4 = (f32[4,8,128]{2,1,0:T(8,128)}, f32[4,8,128]{2,1,0:T(8,128)S(1)}, u32[]{:S(2)}) copy-start(f32[4,8,128]{2,1,0:T(8,128)S(1)} %slice_bitcast_fusion.10) | copy-start | bytes 49156
  34.9 10.4 %copy-start.6 = (f32[4,8,128]{2,1,0:T(8,128)}, f32[4,8,128]{2,1,0:T(8,128)S(1)}, u32[]{:S(2)}) copy-start(f32[4,8,128]{2,1,0:T(8,128)S(1)} %slice_bitcast_fusion.14) | copy-start | bytes 49156
  34.9 10.4 %copy-start.8 = (f32[4,8,128]{2,1,0:T(8,128)}, f32[4,8,128]{2,1,0:T(8,128)S(1)}, u32[]{:S(2)}) copy-start(f32[4,8,128]{2,1,0:T(8,128)S(1)} %slice_bitcast_fusion.16) | copy-start | bytes 49156
  34.9 10.4 %copy-start.10 = (f32[4,8,128]{2,1,0:T(8,128)}, f32[4,8,128]{2,1,0:T(8,128)S(1)}, u32[]{:S(2)}) copy-start(f32[4,8,128]{2,1,0:T(8,128)S(1)} %slice_bitcast_fusion.8) | copy-start | bytes 49156
  35.1 10.3 %copy-start.12 = (f32[4,8,128]{2,1,0:T(8,128)}, f32[4,8,128]{2,1,0:T(8,128)S(1)}, u32[]{:S(2)}) copy-start(f32[4,8,128]{2,1,0:T(8,128)S(1)} %slice_bitcast_fusion.17) | copy-start | bytes 49156
  35.1 10.2 %copy-start.14 = (f32[4,8,128]{2,1,0:T(8,128)}, f32[4,8,128]{2,1,0:T(8,128)S(1)}, u32[]{:S(2)}) copy-start(f32[4,8,128]{2,1,0:T(8,128)S(1)} %slice_bitcast_fusion.18) | copy-start | bytes 49156
  35.1 10.2 %copy-start.16 = (f32[4,8,128]{2,1,0:T(8,128)}, f32[4,8,128]{2,1,0:T(8,128)S(1)}, u32[]{:S(2)}) copy-start(f32[4,8,128]{2,1,0:T(8,128)S(1)} %slice_bitcast_fusion.6) | copy-start | bytes 49156
  35.1 10.2 %copy-start.18 = (f32[4,8,128]{2,1,0:T(8,128)}, f32[4,8,128]{2,1,0:T(8,128)S(1)}, u32[]{:S(2)}) copy-start(f32[4,8,128]{2,1,0:T(8,128)S(1)} %slice_bitcast_fusion.7) | copy-start | bytes 49156
  35.3 10.1 %copy-start.20 = (f32[4,8,128]{2,1,0:T(8,128)}, f32[4,8,128]{2,1,0:T(8,128)S(1)}, u32[]{:S(2)}) copy-start(f32[4,8,128]{2,1,0:T(8,128)S(1)} %slice_bitcast_fusion.11) | copy-start | bytes 49156
  36.1 4.5 collective-permute-start.6
  38.0 6.5 collective-permute-start.7
  165.8 10.6 %collective-permute-start.8 = (f32[96,1,8,128]{3,0,2,1:T(8,128)S(1)}, f32[96,1,8,128]{3,0,2,1:T(8,128)S(1)}, u32[]{:S(2)}, u32[]{:S(2)}) collective-permute-start(f32[96,1,8,128]{3,0,2,1:T(8,128)S(1)} %get-tuple-element.132), channel_id=1, source_target_pairs={{0,32},{32,64},{64,96},{96,128},{128,160},{160,192},{192,224},{224... | collective-permute-start | bytes 1179656 | tf_op jit(solution)/shard_map/ppermute | solution.py:15
  168.7 11.5 %collective-permute-start.9 = (f32[96,1,8,128]{3,0,2,1:T(8,128)S(1)}, f32[96,1,8,128]{3,0,2,1:T(8,128)S(1)}, u32[]{:S(2)}, u32[]{:S(2)}) collective-permute-start(f32[96,1,8,128]{3,0,2,1:T(8,128)S(1)} %get-tuple-element.133), channel_id=1, source_target_pairs={{32,0},{64,32},{96,64},{128,96},{160,128},{192,160},{224,192},{256... | collective-permute-start | bytes 1179656 | tf_op jit(solution)/shard_map/ppermute | solution.py:17
  180.4 8.1 %collective-permute-start.10 = (f32[96,6,1,128]{3,0,2,1:T(8,128)S(1)}, f32[96,6,1,128]{3,0,2,1:T(8,128)S(1)}, u32[]{:S(2)}, u32[]{:S(2)}) collective-permute-start(f32[96,6,1,128]{3,0,2,1:T(8,128)S(1)} %get-tuple-element.130), channel_id=1, source_target_pairs={{0,1},{1,2},{2,3},{3,4},{4,5},{5,6},{6,7},{7,8},{8,9},{9,10},{10,1... | collective-permute-start | bytes 884744 | tf_op jit(solution)/shard_map/ppermute | solution.py:15
  182.6 8.0 %collective-permute-start.11 = (f32[96,6,1,128]{3,0,2,1:T(8,128)S(1)}, f32[96,6,1,128]{3,0,2,1:T(8,128)S(1)}, u32[]{:S(2)}, u32[]{:S(2)}) collective-permute-start(f32[96,6,1,128]{3,0,2,1:T(8,128)S(1)} %get-tuple-element.131), channel_id=1, source_target_pairs={{1,0},{2,1},{3,2},{4,3},{5,4},{6,5},{7,6},{8,7},{9,8},{10,9},{11,1... | collective-permute-start | bytes 884744 | tf_op jit(solution)/shard_map/ppermute | solution.py:17
  (19 other events, 101.6 us)
Sparse Core Ops, SparseCore 0:
  202.2 458.5 all-reduce.64
where the time goes:
time: 726 us; the launch traced here: 725 us
  waiting for transfers between devices  475 us (65%)
  blocking collectives  115 us (16%)
  other arithmetic  65.9 us (9%)
  starting transfers between devices  32.3 us (4%)
  between operations  16.6 us (2%)
  matrix products  12.8 us (2%)
  local copies, waits for them, and re-layouts  7.75 us (1%)
    psum x1, waiting for transfers between devices, shards(): gram_k, gram_m = lax.psum(local_grams(basis, k_basis, mass), ('px', 'py'))  457 us
    psum x1, blocking collectives, shards(): lax.psum((jnp.sum(block * k_block, axis=(1, 2, 3)), jnp.sum(block * m_blo...  115 us
    another operation x7, other arithmetic, ritz(): lower = jnp.linalg.cholesky(gram_m)  24.4 us
    another operation x6, other arithmetic, ritz(): jax.scipy.linalg.solve_triangular(lower, filtered, lower=True, trans=1)  20 us
    ppermute x6, starting transfers between devices, padded_2(): lax.ppermute(tail, axis, [(i, (i + 1) % count) for i in range(ends)])  19.9 us
  transfers between devices with their start and end apart: 13, of which 6 were waited for; matrix products, arithmetic and copies ran while one was open for 2% of the time, Pallas kernels for 0%

commit v1 on v0

--- a/solution.py
+++ b/solution.py
@@ -1,6 +1,7 @@
 import jax
 import jax.numpy as jnp
 from jax import lax
+from jax.sharding import Mesh
 from jax.sharding import PartitionSpec as P
 
 
@@ -174,16 +175,54 @@
     return (gram_k, gram_m)
 
 
+def spread_sum(rows):
+    plane = ("px", "pc")
+    count = lax.axis_size("px") * lax.axis_size("pc")
+    depth = lax.axis_size("pz")
+    pieces = rows.reshape(count, -1, rows.shape[1])
+    part = jnp.sum(lax.all_to_all(pieces, plane, 0, 0), axis=0)
+    part = jnp.sum(
+        lax.all_to_all(jnp.broadcast_to(part[None], (depth,) + part.shape), "pz", 0, 0), axis=0
+    )
+    whole = lax.all_to_all(jnp.broadcast_to(part[None], (count,) + part.shape), plane, 0, 0)
+    return whole.reshape(rows.shape)
+
+
+def copied_sum(part):
+    for axes in (("px", "pc"), ("pz",)):
+        count = 1
+        for axis in axes:
+            count = count * lax.axis_size(axis)
+        part = jnp.sum(
+            lax.all_to_all(jnp.broadcast_to(part[None], (count,) + part.shape), axes, 0, 0), axis=0
+        )
+    return part
+
+
+def packed_grams(gram_k, gram_m):
+    order = gram_k.shape[0]
+    upper = jnp.triu(gram_k) + jnp.tril(gram_m, -1)
+    flat = jnp.concatenate([upper.reshape(-1), jnp.diagonal(gram_m)])
+    size = -(-flat.shape[0] // 32768) * 32768
+    flat = jnp.pad(flat, (0, size - flat.shape[0]))
+    total = spread_sum(flat.reshape(-1, 128)).reshape(-1)
+    square = total[: order * order].reshape(order, order)
+    diagonal = total[order * order : order * order + order]
+    high = jnp.triu(square)
+    low = jnp.tril(square, -1)
+    return (high + jnp.triu(square, 1).T, low + low.T + jnp.diag(diagonal))
+
+
 def shards(offsets, block, prior):
     vecs = block.shape[0]
     rows_a = block.shape[1]
     rows_b = block.shape[2]
     depth = block.shape[3]
     total_a = rows_a * lax.axis_size("px")
-    total_b = rows_b * lax.axis_size("py")
+    total_b = rows_b * lax.axis_size(("pz", "pc"))
     start_a = lax.axis_index("px") * rows_a
-    start_b = lax.axis_index("py") * rows_b
-    extended_offsets = padded_2(offsets, (("px", 1), ("py", 2)), 2)
+    start_b = lax.axis_index(("pz", "pc")) * rows_b
+    extended_offsets = padded_2(offsets, (("px", 1), (("pz", "pc"), 2)), 2)
     index_a = start_a - 2 + jnp.arange(rows_a + 4, dtype=jnp.int32)
     index_b = start_b - 2 + jnp.arange(rows_b + 4, dtype=jnp.int32)
     positions = window_positions(extended_offsets, index_a, index_b)
@@ -196,22 +235,24 @@
     mass = mass_wide[1:-1, 1:-1, :]
     centre = stencil_offsets().index((0, 0, 0))
     diagonal = coefs[centre]
-    first_rim = padded_2(block, (("px", 1), ("py", 2)), 1)
+    first_rim = padded_2(block, (("px", 1), (("pz", "pc"), 2)), 1)
     k_block = stiffness_apply(first_rim, coefs)
     m_block = mass * block
-    numer, denom = lax.psum(
-        (jnp.sum(block * k_block, axis=(1, 2, 3)), jnp.sum(block * m_block, axis=(1, 2, 3))),
-        ("px", "py"),
-    )
+    sums = jnp.stack(
+        [jnp.sum(block * k_block, axis=(1, 2, 3)), jnp.sum(block * m_block, axis=(1, 2, 3))]
+    )
+    sums = copied_sum(jnp.pad(sums, ((0, 6), (0, 128 - vecs))))
+    numer = sums[0, :vecs]
+    denom = sums[1, :vecs]
     quotient = numer / denom
     search = (k_block - quotient[:, None, None, None] * m_block) / diagonal
-    second_rim = padded_2(jnp.concatenate([search, prior]), (("px", 1), ("py", 2)), 1)
+    second_rim = padded_2(jnp.concatenate([search, prior]), (("px", 1), (("pz", "pc"), 2)), 1)
     applied = stiffness_apply(second_rim, coefs)
     k_search = applied[:vecs]
     k_prior = applied[vecs:]
     basis = jnp.concatenate([block, search, prior])
     k_basis = jnp.concatenate([k_block, k_search, k_prior])
-    gram_k, gram_m = lax.psum(local_grams(basis, k_basis, mass), ("px", "py"))
+    gram_k, gram_m = packed_grams(*local_grams(basis, k_basis, mass))
     coeffs = ritz(gram_k, gram_m, vecs)
     scale = jnp.sqrt(jnp.float32(total_a * total_b * depth))
     flat_basis = basis.reshape(basis.shape[0], -1)
@@ -222,6 +263,10 @@
 
 
 def solution(mesh):
-    in_specs = (P(None, "px", "py", None), P(None, "px", "py", None), P(None, "px", "py", None))
-    out_specs = (P(None, "px", "py", None), P(None, "px", "py", None))
-    return jax.shard_map(shards, mesh=mesh, in_specs=in_specs, out_specs=out_specs, check_vma=False)
+    grid = Mesh(
+        mesh.devices.reshape(mesh.shape["px"], mesh.shape["py"] // 2, 2), ("px", "pz", "pc")
+    )
+    spec = P(None, "px", ("pz", "pc"), None)
+    return jax.shard_map(
+        shards, mesh=grid, in_specs=(spec, spec, spec), out_specs=(spec, spec), check_vma=False
+    )

time: 726 us -> 234 us (0.32)
  waiting for transfers between devices: 475 us -> 44.6 us
  blocking collectives: 115 us -> 32.7 us
  starting transfers between devices: 32.3 us -> 61.4 us
  between operations: 16.6 us -> 3.48 us
    psum x1 -> x0, waiting for transfers between devices: 457 us -> none  [shards(): gram_k, gram_m = lax.psum(local_grams(basis, k_basis, mass), ('px', 'py'))]
    psum x1 -> x0, blocking collectives: 115 us -> none  [shards(): lax.psum((jnp.sum(block * k_block, axis=(1, 2, 3)), jnp.sum(block * m_blo...]
    all_to_all x0 -> x2, blocking collectives: none -> 32.7 us  [the longest x1 17.5 us: copied_sum(): lax.all_to_all(jnp.broadcast_to(part[None], (count,) + part.shape), axes,...]
    all_to_all x0 -> x3, waiting for transfers between devices: none -> 28.3 us  [the longest x1 11.1 us: copied_sum(): lax.all_to_all(jnp.broadcast_to(part[None], (count,) + part.shape), axes,...]
    all_to_all x0 -> x3, starting transfers between devices: none -> 27 us  [the longest x1 15.7 us: copied_sum(): lax.all_to_all(jnp.broadcast_to(part[None], (count,) + part.shape), axes,...]
  transfers between devices with their start and end apart: 13 -> 15, of which waited for: 6 -> 8; matrix products, arithmetic and copies ran while one was open for 2% -> 6% of each run, Pallas kernels for 0% -> 0%
where the time goes in v1:
time: 234 us; the launch traced here: 233 us
  other arithmetic  68.8 us (29%)
  starting transfers between devices  61.4 us (26%)
  waiting for transfers between devices  44.6 us (19%)
  blocking collectives  32.7 us (14%)
  local copies, waits for them, and re-layouts  12.5 us (5%)
  matrix products  9.6 us (4%)
  between operations  3.48 us (1%)
    another operation x7, other arithmetic, ritz(): lower = jnp.linalg.cholesky(gram_m)  24.4 us
    ppermute x6, starting transfers between devices, padded_2(): lax.ppermute(tail, axis, [(i, (i + 1) % count) for i in range(ends)])  23 us
    another operation x6, other arithmetic, ritz(): jax.scipy.linalg.solve_triangular(lower, filtered, lower=True, trans=1)  20.1 us
    all_to_all x1, blocking collectives, copied_sum(): lax.all_to_all(jnp.broadcast_to(part[None], (count,) + part.shape), axes,...  17.5 us
    all_to_all x1, starting transfers between devices, copied_sum(): lax.all_to_all(jnp.broadcast_to(part[None], (count,) + part.shape), axes,...  15.7 us
    all_to_all x1, blocking collectives, spread_sum(): part = jnp.sum(lax.all_to_all(pieces, plane, 0, 0), axis=0)  15.1 us
    ppermute x6, starting transfers between devices, padded_2(): lax.ppermute(head, axis, [((i + 1) % count, i) for i in range(ends)])  11.4 us
    ppermute x6, waiting for transfers between devices, padded_2(): lax.ppermute(head, axis, [((i + 1) % count, i) for i in range(ends)])  11.3 us
  transfers between devices with their start and end apart: 15, of which 8 were waited for; matrix products, arithmetic and copies ran while one was open for 6% of the time, Pallas kernels for 0%

profile of v1, /device:TPU:1, one launch (start us, length us, event | category | flops | bytes accessed | tf_op | source)
XLA Modules:
  0.0 233.1 jit_solution(13190232814367837328)
XLA Ops:
  1.4 3.9 %collective-permute-start = (f32[3,2,8,128]{3,2,1,0:T(8,128)S(1)}, f32[3,2,8,128]{3,2,1,0:T(8,128)S(1)}, u32[]{:S(2)}, u32[]{:S(2)}) collective-permute-start(f32[3,2,8,128]{3,2,1,0:T(8,128)S(1)} %get-tuple-element.264), channel_id=1, source_target_pairs={{0,32},{32,64},{64,96},{96,128},{128,160},{160,192},{192,224},{224... | collective-permute-start | bytes 73736 | tf_op jit(solution)/shard_map/ppermute | solution.py:16
  8.3 4.0 %collective-permute-start.4 = (f32[48,1,8,128]{3,0,2,1:T(8,128)S(1)}, f32[48,1,8,128]{3,0,2,1:T(8,128)S(1)}, u32[]{:S(2)}, u32[]{:S(2)}) collective-permute-start(f32[48,1,8,128]{3,0,2,1:T(8,128)S(1)} %get-tuple-element.135), channel_id=1, source_target_pairs={{0,32},{32,64},{64,96},{96,128},{128,160},{160,192},{192,224},{224... | collective-permute-start | bytes 589832 | tf_op jit(solution)/shard_map/ppermute | solution.py:16
  13.9 4.9 %collective-permute-start.2 = (f32[3,8,2,128]{3,2,1,0:T(2,128)S(1)}, f32[3,8,2,128]{3,2,1,0:T(2,128)S(1)}, u32[]{:S(2)}, u32[]{:S(2)}) collective-permute-start(f32[3,8,2,128]{3,2,1,0:T(2,128)S(1)} %get-tuple-element.245), channel_id=1, source_target_pairs={{0,1},{1,2},{2,3},{3,4},{4,5},{5,6},{6,7},{7,8},{8,9},{9,10},{10,1... | collective-permute-start | bytes 73736 | tf_op jit(solution)/shard_map/ppermute | solution.py:16
  18.8 3.0 %collective-permute-start.3 = (f32[3,8,2,128]{3,2,1,0:T(2,128)S(1)}, f32[3,8,2,128]{3,2,1,0:T(2,128)S(1)}, u32[]{:S(2)}, u32[]{:S(2)}) collective-permute-start(f32[3,8,2,128]{3,2,1,0:T(2,128)S(1)} %get-tuple-element.246), channel_id=1, source_target_pairs={{1,0},{2,1},{3,2},{4,3},{5,4},{6,5},{7,6},{8,7},{9,8},{10,9},{11,1... | collective-permute-start | bytes 73736 | tf_op jit(solution)/shard_map/ppermute | solution.py:18
  33.9 3.9 %collective-permute-done.7 = f32[48,6,1,128]{3,0,2,1:T(8,128)S(1)} collective-permute-done((f32[48,6,1,128]{3,0,2,1:T(8,128)S(1)}, f32[48,6,1,128]{3,0,2,1:T(8,128)S(1)}, u32[]{:S(2)}, u32[]{:S(2)}) %collective-permute-start.7) | collective-permute-done | bytes 147488 | tf_op jit(solution)/shard_map/ppermute | solution.py:18
  38.8 3.9 %multiply_reduce_fusion = (f32[48]{0:T(128)S(1)}, f32[48]{0:T(128)S(1)}, f32[48,4,8,128]{3,0,2,1:T(8,128)}) fusion(f32[48,4,8,128]{3,2,1,0:T(8,128)S(1)} %copy-done, f32[4,8,128]{2,1,0:T(8,128)S(1)} %fusion.128, f32[48,6,10,130]{3,0,2,1:T(8,128)S(1)} %select_maximum_fusion.5, f32[4,8,128]{2,1,0:T(8,128)S(1)} %slice_bitcast_fusion.5, ...), kind=kLoop, calls=%fused_computation.117 | loop fusion | flops 7864224 | bytes 10781056 | tf_op jit(solution)/shard_map/reduce_sum | solution.py:242
  42.8 17.5 %all_to_all.25 = f32[32,8,128]{2,1,0:T(8,128)S(1)} all-to-all(f32[32,8,128]{2,1,0:T(8,128)S(1)} %broadcast_in_dim.150), channel_id=1, replica_groups=mesh['px'=16,'pz'=16,'pc'=2] {'px','pc'}, dimensions={0} | all-to-all | bytes 262144 | tf_op jit(solution)/shard_map/all_to_all | solution.py:197
  61.0 15.7 %all-to-all-start.1 = ((f32[16,8,128]{2,1,0:T(8,128)}), f32[16,8,128]{2,1,0:T(8,128)S(1)}, u32[]{:S(2)}, u32[]{:S(2)}) async-start(f32[16,8,128]{2,1,0:T(8,128)} %broadcast_in_dim.151), calls=%async_computation.1 | async-start | bytes 131072 | tf_op jit(solution)/shard_map/all_to_all | solution.py:197
  77.1 11.1 %all-to-all-done.1 = f32[16,8,128]{2,1,0:T(8,128)S(1)} async-done(((f32[16,8,128]{2,1,0:T(8,128)}), f32[16,8,128]{2,1,0:T(8,128)S(1)}, u32[]{:S(2)}, u32[]{:S(2)}) %all-to-all-start.1) | async-done | bytes 65568 | tf_op jit(solution)/shard_map/all_to_all | solution.py:197
  93.8 5.0 %collective-permute-done.8 = f32[96,1,8,128]{3,0,2,1:T(8,128)S(1)} collective-permute-done((f32[96,1,8,128]{3,0,2,1:T(8,128)S(1)}, f32[96,1,8,128]{3,0,2,1:T(8,128)S(1)}, u32[]{:S(2)}, u32[]{:S(2)}) %collective-permute-start.8) | collective-permute-done | bytes 393248 | tf_op jit(solution)/shard_map/ppermute | solution.py:16
  98.8 3.9 %collective-permute-done.9 = f32[96,1,8,128]{3,0,2,1:T(8,128)S(1)} collective-permute-done((f32[96,1,8,128]{3,0,2,1:T(8,128)S(1)}, f32[96,1,8,128]{3,0,2,1:T(8,128)S(1)}, u32[]{:S(2)}, u32[]{:S(2)}) %collective-permute-start.9) | collective-permute-done | bytes 393248 | tf_op jit(solution)/shard_map/ppermute | solution.py:18
  103.5 5.8 %collective-permute-start.10 = (f32[96,6,1,128]{3,0,2,1:T(8,128)}, f32[96,6,1,128]{3,0,2,1:T(8,128)}, u32[]{:S(2)}, u32[]{:S(2)}) collective-permute-start(f32[96,6,1,128]{3,0,2,1:T(8,128)} %get-tuple-element.128), channel_id=1, source_target_pairs={{0,1},{1,2},{2,3},{3,4},{4,5},{5,6},{6,7},{7,8},{8,9},{9,10},{10,1... | collective-permute-start | bytes 884744 | tf_op jit(solution)/shard_map/ppermute | solution.py:16
  113.6 2.8 %gather_fusion = f32[144]{0:T(256)S(1)} fusion(f32[144,144]{1,0:T(8,128)S(1)} %fusion.34, s32[144]{0:T(256)S(1)} %bitcast.243), kind=kCustom, calls=%fused_computation | custom fusion | bytes 2304 | tf_op jit(solution)/shard_map/jit(diagonal)/cond/branch_0_fun/gather | solution.py:205
  119.6 5.3 %select_maximum_fusion = f32[96,6,10,130]{3,0,2,1:T(8,128)S(1)} fusion(f32[96,6,1,128]{3,0,2,1:T(8,128)} %collective-permute-done.11, f32[96,6,1,128]{3,0,2,1:T(8,128)} %collective-permute-done.10, f32[96,1,8,128]{3,0,2,1:T(8,128)S(1)} %collective-permute-done.9, f32[96,1,8,128]{3,0,2,1:T(8,128)S(1)} %collective-permute-done.8, ...), kind=kLoop, calls=%fused_computation.3 | loop fusion | flops 10483200 | bytes 5944320 | tf_op jit(solution)/shard_map/concatenate | solution.py:14
  125.1 3.9 %fusion.18 = f32[96,4,8,128]{3,0,2,1:T(8,128)S(1)} fusion(f32[48,4,8,128]{3,0,2,1:T(8,128)S(1)} %copy.74, f32[48,4,8,128]{3,0,2,1:T(8,128)S(1)} %fusion.45, f32[96,6,10,130]{3,0,2,1:T(8,128)S(1)} %select_maximum_fusion, f32[96,6,9,128]{3,0,2,1:T(8,128)S(1)} %get-tuple-element.127, f32[96,1,8,128]{3,0,2,1:T(8,128)S(1)} %collective-permute-done.9, ...), kind=kLoop, calls=%fused_computation.39 | loop fusion | flops 13369344 | bytes 23052288 | tf_op jit(solution)/shard_map/add | solution.py:143
  131.4 15.1 %all_to_all.26 = f32[32,8,128]{2,1,0:T(8,128)S(1)} all-to-all(f32[32,8,128]{2,1,0:T(8,128)S(1)} %fusion.79), channel_id=1, replica_groups=mesh['px'=16,'pz'=16,'pc'=2] {'px','pc'}, dimensions={0} | all-to-all | bytes 262144 | tf_op jit(solution)/shard_map/all_to_all | solution.py:183
  147.2 5.7 %all-to-all-start.3 = ((f32[16,8,128]{2,1,0:T(8,128)}), f32[16,8,128]{2,1,0:T(8,128)S(1)}, u32[]{:S(2)}, u32[]{:S(2)}) async-start(f32[16,8,128]{2,1,0:T(8,128)} %broadcast_in_dim.152), calls=%async_computation.3 | async-start | bytes 131072 | tf_op jit(solution)/shard_map/all_to_all | solution.py:185
  154.0 10.4 %all-to-all-done.3 = f32[16,8,128]{2,1,0:T(8,128)S(1)} async-done(((f32[16,8,128]{2,1,0:T(8,128)}), f32[16,8,128]{2,1,0:T(8,128)S(1)}, u32[]{:S(2)}, u32[]{:S(2)}) %all-to-all-start.3) | async-done | bytes 65568 | tf_op jit(solution)/shard_map/all_to_all | solution.py:185
  165.2 5.6 %all-to-all-start.4 = ((f32[32,8,128]{2,1,0:T(8,128)}), f32[32,8,128]{2,1,0:T(8,128)S(1)}, u32[]{:S(2)}, u32[]{:S(2)}) async-start(f32[32,8,128]{2,1,0:T(8,128)} %broadcast_in_dim.153), calls=%async_computation.4 | async-start | bytes 262144 | tf_op jit(solution)/shard_map/all_to_all | solution.py:187
  171.8 6.8 %all-to-all-done.4 = f32[32,8,128]{2,1,0:T(8,128)S(1)} async-done(((f32[32,8,128]{2,1,0:T(8,128)}), f32[32,8,128]{2,1,0:T(8,128)S(1)}, u32[]{:S(2)}, u32[]{:S(2)}) %all-to-all-start.4) | async-done | bytes 131104 | tf_op jit(solution)/shard_map/all_to_all | solution.py:187
  179.2 11.7 %cholesky.50 = f32[128,128]{1,0:T(8,128)S(1)} custom-call(f32[128,128]{1,0:T(8,128)S(1)} %copy.86), custom_call_target="Cholesky" | custom-call | tf_op jit(solution)/shard_map/jit(cholesky)/cholesky | solution.py:156
  191.0 9.8 %custom-call.18 = f32[1,128,128]{1,2,0:T(8,128)S(1)} custom-call(f32[1,128,128]{2,1,0:T(8,128)S(1)} %get-tuple-element.248), custom_call_target="InvertDiagBlocksLowerTriangular" | custom-call | tf_op jit(solution)/shard_map/jit(cholesky)/cholesky | solution.py:156
  205.6 19.9 %custom-call.19 = f32[2,128,128]{1,2,0:T(8,128)S(1)} custom-call(f32[2,128,128]{2,1,0:T(8,128)S(1)} %pad_maximum_fusion.28), custom_call_target="InvertDiagBlocksLowerTriangular" | custom-call | tf_op jit(solution)/shard_map/jit(_solve_triangular)/triangular_solve | solution.py:162
  229.4 2.7 %fusion.27 = f32[6,8,32,128]{3,1,2,0:T(8,128)S(1)} fusion(f32[18,8,32,128]{3,2,1,0:T(8,128)S(1)} %bitcast.242, f32[16,48]{0,1:T(8,128)S(1)} %copy.94, f32[128,48]{0,1:T(8,128)S(1)} %fusion.86), kind=kOutput, calls=%fused_computation.68 | convolution fusion | flops 339942144 | bytes 3173376 | tf_op jit(solution)/shard_map/dot_general | solution.py:259
  (229 shorter events, 47.2 us)
Async XLA Ops:
  0.6 13.2 %copy-start.3 = (f32[3,4,8,128]{3,2,1,0:T(8,128)S(1)}, f32[3,4,8,128]{3,2,1,0:T(8,128)}, u32[]{:S(2)}) copy-start(f32[3,4,8,128]{3,2,1,0:T(8,128)} %param.7) | copy-start | bytes 147460
  1.4 12.3 %collective-permute-start = (f32[3,2,8,128]{3,2,1,0:T(8,128)S(1)}, f32[3,2,8,128]{3,2,1,0:T(8,128)S(1)}, u32[]{:S(2)}, u32[]{:S(2)}) collective-permute-start(f32[3,2,8,128]{3,2,1,0:T(8,128)S(1)} %get-tuple-element.264), channel_id=1, source_target_pairs={{0,32},{32,64},{64,96},{96,128},{128,160},{160,192},{192,224},{224... | collective-permute-start | bytes 73736 | tf_op jit(solution)/shard_map/ppermute | solution.py:16
  5.4 8.4 %collective-permute-start.1 = (f32[3,2,8,128]{3,2,1,0:T(8,128)S(1)}, f32[3,2,8,128]{3,2,1,0:T(8,128)S(1)}, u32[]{:S(2)}, u32[]{:S(2)}) collective-permute-start(f32[3,2,8,128]{3,2,1,0:T(8,128)S(1)} %get-tuple-element.263), channel_id=1, source_target_pairs={{32,0},{64,32},{96,64},{128,96},{160,128},{192,160},{224,192},{256... | collective-permute-start | bytes 73736 | tf_op jit(solution)/shard_map/ppermute | solution.py:18
  8.3 20.6 %collective-permute-start.4 = (f32[48,1,8,128]{3,0,2,1:T(8,128)S(1)}, f32[48,1,8,128]{3,0,2,1:T(8,128)S(1)}, u32[]{:S(2)}, u32[]{:S(2)}) collective-permute-start(f32[48,1,8,128]{3,0,2,1:T(8,128)S(1)} %get-tuple-element.135), channel_id=1, source_target_pairs={{0,32},{32,64},{64,96},{96,128},{128,160},{160,192},{192,224},{224... | collective-permute-start | bytes 589832 | tf_op jit(solution)/shard_map/ppermute | solution.py:16
  12.3 17.1 %collective-permute-start.5 = (f32[48,1,8,128]{3,0,2,1:T(8,128)S(1)}, f32[48,1,8,128]{3,0,2,1:T(8,128)S(1)}, u32[]{:S(2)}, u32[]{:S(2)}) collective-permute-start(f32[48,1,8,128]{3,0,2,1:T(8,128)S(1)} %get-tuple-element.134), channel_id=1, source_target_pairs={{32,0},{64,32},{96,64},{128,96},{160,128},{192,160},{224,192},{256... | collective-permute-start | bytes 589832 | tf_op jit(solution)/shard_map/ppermute | solution.py:18
  13.9 8.0 %collective-permute-start.2 = (f32[3,8,2,128]{3,2,1,0:T(2,128)S(1)}, f32[3,8,2,128]{3,2,1,0:T(2,128)S(1)}, u32[]{:S(2)}, u32[]{:S(2)}) collective-permute-start(f32[3,8,2,128]{3,2,1,0:T(2,128)S(1)} %get-tuple-element.245), channel_id=1, source_target_pairs={{0,1},{1,2},{2,3},{3,4},{4,5},{5,6},{6,7},{7,8},{8,9},{9,10},{10,1... | collective-permute-start | bytes 73736 | tf_op jit(solution)/shard_map/ppermute | solution.py:16
  18.8 5.4 %collective-permute-start.3 = (f32[3,8,2,128]{3,2,1,0:T(2,128)S(1)}, f32[3,8,2,128]{3,2,1,0:T(2,128)S(1)}, u32[]{:S(2)}, u32[]{:S(2)}) collective-permute-start(f32[3,8,2,128]{3,2,1,0:T(2,128)S(1)} %get-tuple-element.246), channel_id=1, source_target_pairs={{1,0},{2,1},{3,2},{4,3},{5,4},{6,5},{7,6},{8,7},{9,8},{10,9},{11,1... | collective-permute-start | bytes 73736 | tf_op jit(solution)/shard_map/ppermute | solution.py:18
  28.2 10.4 %copy-start.6 = (f32[4,8,128]{2,1,0:T(8,128)}, f32[4,8,128]{2,1,0:T(8,128)S(1)}, u32[]{:S(2)}) copy-start(f32[4,8,128]{2,1,0:T(8,128)S(1)} %slice_bitcast_fusion.10) | copy-start | bytes 49156
  28.3 10.4 %copy-start.8 = (f32[4,8,128]{2,1,0:T(8,128)}, f32[4,8,128]{2,1,0:T(8,128)S(1)}, u32[]{:S(2)}) copy-start(f32[4,8,128]{2,1,0:T(8,128)S(1)} %slice_bitcast_fusion.14) | copy-start | bytes 49156
  28.3 10.4 %copy-start.10 = (f32[4,8,128]{2,1,0:T(8,128)}, f32[4,8,128]{2,1,0:T(8,128)S(1)}, u32[]{:S(2)}) copy-start(f32[4,8,128]{2,1,0:T(8,128)S(1)} %slice_bitcast_fusion.16) | copy-start | bytes 49156
  28.3 10.4 %copy-start.12 = (f32[4,8,128]{2,1,0:T(8,128)}, f32[4,8,128]{2,1,0:T(8,128)S(1)}, u32[]{:S(2)}) copy-start(f32[4,8,128]{2,1,0:T(8,128)S(1)} %slice_bitcast_fusion.8) | copy-start | bytes 49156
  29.4 4.5 %collective-permute-start.6 = (f32[48,6,1,128]{3,0,2,1:T(8,128)S(1)}, f32[48,6,1,128]{3,0,2,1:T(8,128)S(1)}, u32[]{:S(2)}, u32[]{:S(2)}) collective-permute-start(f32[48,6,1,128]{3,0,2,1:T(8,128)S(1)} %get-tuple-element.132), channel_id=1, source_target_pairs={{0,1},{1,2},{2,3},{3,4},{4,5},{5,6},{6,7},{7,8},{8,9},{9,10},{10,1... | collective-permute-start | bytes 442376 | tf_op jit(solution)/shard_map/ppermute | solution.py:16
  31.4 6.5 %collective-permute-start.7 = (f32[48,6,1,128]{3,0,2,1:T(8,128)S(1)}, f32[48,6,1,128]{3,0,2,1:T(8,128)S(1)}, u32[]{:S(2)}, u32[]{:S(2)}) collective-permute-start(f32[48,6,1,128]{3,0,2,1:T(8,128)S(1)} %get-tuple-element.133), channel_id=1, source_target_pairs={{1,0},{2,1},{3,2},{4,3},{5,4},{6,5},{7,6},{8,7},{9,8},{10,9},{11,1... | collective-permute-start | bytes 442376 | tf_op jit(solution)/shard_map/ppermute | solution.py:18
  33.9 54.4 %copy-start.4 = (f32[4,8,128]{2,1,0:T(8,128)}, f32[4,8,128]{2,1,0:T(8,128)S(1)}, u32[]{:S(2)}) copy-start(f32[4,8,128]{2,1,0:T(8,128)S(1)} %fusion.128) | copy-start | bytes 49156
  38.8 37.9 %copy-start.2 = (f32[48,4,8,128]{3,2,1,0:T(8,128)S(1)}, f32[48,4,8,128]{3,2,1,0:T(8,128)}, u32[]{:S(2)}) copy-start(f32[48,4,8,128]{3,2,1,0:T(8,128)} %param.9) | copy-start | bytes 2359300
  61.0 27.3 %all-to-all-start.1 = ((f32[16,8,128]{2,1,0:T(8,128)}), f32[16,8,128]{2,1,0:T(8,128)S(1)}, u32[]{:S(2)}, u32[]{:S(2)}) async-start(f32[16,8,128]{2,1,0:T(8,128)} %broadcast_in_dim.151), calls=%async_computation.1 | async-start | bytes 131072 | tf_op jit(solution)/shard_map/all_to_all | solution.py:197
  89.9 21.4 %copy-start.5 = (f32[4,8,128]{2,1,0:T(8,128)S(1)}, f32[4,8,128]{2,1,0:T(8,128)}, u32[]{:S(2)}) copy-start(f32[4,8,128]{2,1,0:T(8,128)} %copy-done.4) | copy-start | bytes 49156
  90.0 8.7 %collective-permute-start.8 = (f32[96,1,8,128]{3,0,2,1:T(8,128)S(1)}, f32[96,1,8,128]{3,0,2,1:T(8,128)S(1)}, u32[]{:S(2)}, u32[]{:S(2)}) collective-permute-start(f32[96,1,8,128]{3,0,2,1:T(8,128)S(1)} %get-tuple-element.130), channel_id=1, source_target_pairs={{0,32},{32,64},{64,96},{96,128},{128,160},{160,192},{192,224},{224... | collective-permute-start | bytes 1179656 | tf_op jit(solution)/shard_map/ppermute | solution.py:16
  92.4 10.2 %collective-permute-start.9 = (f32[96,1,8,128]{3,0,2,1:T(8,128)S(1)}, f32[96,1,8,128]{3,0,2,1:T(8,128)S(1)}, u32[]{:S(2)}, u32[]{:S(2)}) collective-permute-start(f32[96,1,8,128]{3,0,2,1:T(8,128)S(1)} %get-tuple-element.131), channel_id=1, source_target_pairs={{32,0},{64,32},{96,64},{128,96},{160,128},{192,160},{224,192},{256... | collective-permute-start | bytes 1179656 | tf_op jit(solution)/shard_map/ppermute | solution.py:18
  93.8 35.3 %copy-start.34 = (s32[144]{0:T(256)}, s32[144]{0:T(256)S(1)}, u32[]{:S(2)}) copy-start(s32[144]{0:T(256)S(1)} %iota_add_fusion) | copy-start | bytes 1732
  103.5 12.9 %collective-permute-start.10 = (f32[96,6,1,128]{3,0,2,1:T(8,128)}, f32[96,6,1,128]{3,0,2,1:T(8,128)}, u32[]{:S(2)}, u32[]{:S(2)}) collective-permute-start(f32[96,6,1,128]{3,0,2,1:T(8,128)} %get-tuple-element.128), channel_id=1, source_target_pairs={{0,1},{1,2},{2,3},{3,4},{4,5},{5,6},{6,7},{7,8},{8,9},{9,10},{10,1... | collective-permute-start | bytes 884744 | tf_op jit(solution)/shard_map/ppermute | solution.py:16
  109.3 8.4 %collective-permute-start.11 = (f32[96,6,1,128]{3,0,2,1:T(8,128)}, f32[96,6,1,128]{3,0,2,1:T(8,128)}, u32[]{:S(2)}, u32[]{:S(2)}) collective-permute-start(f32[96,6,1,128]{3,0,2,1:T(8,128)} %get-tuple-element.129), channel_id=1, source_target_pairs={{1,0},{2,1},{3,2},{4,3},{5,4},{6,5},{7,6},{8,7},{9,8},{10,9},{11,1... | collective-permute-start | bytes 884744 | tf_op jit(solution)/shard_map/ppermute | solution.py:18
  147.2 17.3 %all-to-all-start.3 = ((f32[16,8,128]{2,1,0:T(8,128)}), f32[16,8,128]{2,1,0:T(8,128)S(1)}, u32[]{:S(2)}, u32[]{:S(2)}) async-start(f32[16,8,128]{2,1,0:T(8,128)} %broadcast_in_dim.152), calls=%async_computation.3 | async-start | bytes 131072 | tf_op jit(solution)/shard_map/all_to_all | solution.py:185
  165.2 13.4 %all-to-all-start.4 = ((f32[32,8,128]{2,1,0:T(8,128)}), f32[32,8,128]{2,1,0:T(8,128)S(1)}, u32[]{:S(2)}, u32[]{:S(2)}) async-start(f32[32,8,128]{2,1,0:T(8,128)} %broadcast_in_dim.153), calls=%async_computation.4 | async-start | bytes 262144 | tf_op jit(solution)/shard_map/all_to_all | solution.py:187
  (27 other events, 185.2 us)

commit v2 on v1

--- a/solution.py
+++ b/solution.py
@@ -188,29 +188,37 @@
     return whole.reshape(rows.shape)
 
 
-def copied_sum(part):
-    for axes in (("px", "pc"), ("pz",)):
-        count = 1
-        for axis in axes:
-            count = count * lax.axis_size(axis)
-        part = jnp.sum(
-            lax.all_to_all(jnp.broadcast_to(part[None], (count,) + part.shape), axes, 0, 0), axis=0
-        )
-    return part
-
-
-def packed_grams(gram_k, gram_m):
+def summed_grams(gram_k, gram_m):
     order = gram_k.shape[0]
-    upper = jnp.triu(gram_k) + jnp.tril(gram_m, -1)
-    flat = jnp.concatenate([upper.reshape(-1), jnp.diagonal(gram_m)])
-    size = -(-flat.shape[0] // 32768) * 32768
-    flat = jnp.pad(flat, (0, size - flat.shape[0]))
-    total = spread_sum(flat.reshape(-1, 128)).reshape(-1)
-    square = total[: order * order].reshape(order, order)
-    diagonal = total[order * order : order * order + order]
+    eye = jnp.eye(order, dtype=jnp.bool_)
+    square = jnp.triu(gram_k) + jnp.tril(gram_m, -1)
+    diagonal = jnp.sum(jnp.where(eye, gram_m, 0.0), axis=0)
+    rows = jnp.concatenate([square, jnp.broadcast_to(diagonal[None], (256 - order, order))])
+    total = spread_sum(jnp.pad(rows, ((0, 0), (0, 256 - order))))
+    square = total[:order, :order]
+    diagonal = total[order, :order]
     high = jnp.triu(square)
     low = jnp.tril(square, -1)
-    return (high + jnp.triu(square, 1).T, low + low.T + jnp.diag(diagonal))
+    return (high + jnp.triu(square, 1).T, low + low.T + jnp.where(eye, diagonal[None], 0.0))
+
+
+def combined(gram, quotient):
+    vecs = quotient.shape[0]
+    rows = jnp.concatenate(
+        [
+            gram[:vecs],
+            gram[vecs : 2 * vecs] - quotient[:, None] * gram[2 * vecs : 3 * vecs],
+            gram[3 * vecs :],
+        ]
+    )
+    return jnp.concatenate(
+        [
+            rows[:, :vecs],
+            rows[:, vecs : 2 * vecs] - quotient[None, :] * rows[:, 2 * vecs : 3 * vecs],
+            rows[:, 3 * vecs :],
+        ],
+        axis=1,
+    )
 
 
 def shards(offsets, block, prior):
@@ -222,7 +230,11 @@
     total_b = rows_b * lax.axis_size(("pz", "pc"))
     start_a = lax.axis_index("px") * rows_a
     start_b = lax.axis_index(("pz", "pc")) * rows_b
-    extended_offsets = padded_2(offsets, (("px", 1), (("pz", "pc"), 2)), 2)
+    sides = (("px", 1), (("pz", "pc"), 2))
+    wide = padded_2(jnp.concatenate([offsets, block]), sides, 2)
+    prior_wide = padded_2(prior, sides, 1)
+    extended_offsets = wide[: offsets.shape[0]]
+    block_wide = wide[offsets.shape[0] :]
     index_a = start_a - 2 + jnp.arange(rows_a + 4, dtype=jnp.int32)
     index_b = start_b - 2 + jnp.arange(rows_b + 4, dtype=jnp.int32)
     positions = window_positions(extended_offsets, index_a, index_b)
@@ -234,28 +246,26 @@
     coefs = coefs_wide[:, 1:-1, 1:-1, :]
     mass = mass_wide[1:-1, 1:-1, :]
     centre = stencil_offsets().index((0, 0, 0))
-    diagonal = coefs[centre]
-    first_rim = padded_2(block, (("px", 1), (("pz", "pc"), 2)), 1)
-    k_block = stiffness_apply(first_rim, coefs)
-    m_block = mass * block
-    sums = jnp.stack(
-        [jnp.sum(block * k_block, axis=(1, 2, 3)), jnp.sum(block * m_block, axis=(1, 2, 3))]
-    )
-    sums = copied_sum(jnp.pad(sums, ((0, 6), (0, 128 - vecs))))
-    numer = sums[0, :vecs]
-    denom = sums[1, :vecs]
-    quotient = numer / denom
-    search = (k_block - quotient[:, None, None, None] * m_block) / diagonal
-    second_rim = padded_2(jnp.concatenate([search, prior]), (("px", 1), (("pz", "pc"), 2)), 1)
-    applied = stiffness_apply(second_rim, coefs)
-    k_search = applied[:vecs]
-    k_prior = applied[vecs:]
-    basis = jnp.concatenate([block, search, prior])
-    k_basis = jnp.concatenate([k_block, k_search, k_prior])
-    gram_k, gram_m = packed_grams(*local_grams(basis, k_basis, mass))
-    coeffs = ritz(gram_k, gram_m, vecs)
+    vertex_a = index_a[1:-1]
+    vertex_b = index_b[1:-1]
+    inside_a = (vertex_a >= 0) & (vertex_a <= total_a - 1)
+    inside_b = (vertex_b >= 0) & (vertex_b <= total_b - 1)
+    inside = (inside_a[:, None] & inside_b[None, :])[:, :, None]
+    diagonal = jnp.where(inside, coefs_wide[centre], 1.0)
+    k_wide = stiffness_apply(block_wide, coefs_wide)
+    u_wide = k_wide / diagonal
+    w_wide = mass_wide * block_wide[:, 1:-1, 1:-1, :] / diagonal
+    applied = stiffness_apply(jnp.concatenate([u_wide, w_wide, prior_wide]), coefs)
+    u_part = u_wide[:, 1:-1, 1:-1, :]
+    w_part = w_wide[:, 1:-1, 1:-1, :]
+    basis = jnp.concatenate([block, u_part, w_part, prior])
+    k_basis = jnp.concatenate([k_wide[:, 1:-1, 1:-1, :], applied])
+    gram_k, gram_m = summed_grams(*local_grams(basis, k_basis, mass))
+    quotient = jnp.diagonal(gram_k[:vecs, :vecs]) / jnp.diagonal(gram_m[:vecs, :vecs])
+    search = u_part - quotient[:, None, None, None] * w_part
+    coeffs = ritz(combined(gram_k, quotient), combined(gram_m, quotient), vecs)
     scale = jnp.sqrt(jnp.float32(total_a * total_b * depth))
-    flat_basis = basis.reshape(basis.shape[0], -1)
+    flat_basis = jnp.concatenate([block, search, prior]).reshape(3 * vecs, -1)
     new_block = scale * lax.dot_general(
         coeffs, flat_basis, (((0,), (0,)), ((), ())), precision=lax.Precision.HIGHEST
     )

time: 234 us -> 218 us (0.932); the launches traced: 233 us -> 214 us
  waiting for transfers between devices: 44.6 us -> 11.3 us
  starting transfers between devices: 61.4 us -> 32.3 us
  other arithmetic: 68.8 us -> 87.1 us
  blocking collectives: 32.7 us -> 45.7 us
  local copies, waits for them, and re-layouts: 12.5 us -> 19.3 us
  matrix products: 9.6 us -> 14.8 us
    all_to_all x2 -> x0, waiting for transfers between devices: 21.5 us -> none  [the longest x1 11.1 us: copied_sum(): lax.all_to_all(jnp.broadcast_to(part[None], (count,) + part.shape), axes,...]
    all_to_all x2 -> x0, starting transfers between devices: 21.4 us -> none  [the longest x1 15.7 us: copied_sum(): lax.all_to_all(jnp.broadcast_to(part[None], (count,) + part.shape), axes,...]
    all_to_all x1, blocking collectives: 17.5 us -> 29.1 us  [spread_sum(): lax.all_to_all(jnp.broadcast_to(part[None], (depth,) + part.shape), 'pz',...]
    ppermute x6 -> x4, waiting for transfers between devices: 11.3 us -> 0.31 us  [padded_2(): lax.ppermute(head, axis, [((i + 1) % count, i) for i in range(ends)])]
    reduce_sum x8 -> x9, other arithmetic: 1.51 us -> 10.9 us  [assemble(): entry_value = jnp.sum(gradients[first] * gradients[second], axis=0) * weight]
    concatenate x3 -> x2, other arithmetic: 8 us -> 0.53 us  [padded_2(): jnp.concatenate([lax.ppermute(tail, axis, [(i, (i + 1) % count) for i in...]
    unnamed x80 -> x25, local copies, waits for them, and re-layouts: 4.84 us -> 9.75 us
    ppermute x6 -> x4, starting transfers between devices: 11.4 us -> 6.94 us  [padded_2(): lax.ppermute(head, axis, [((i + 1) % count, i) for i in range(ends)])]
  transfers between devices with their start and end apart: 15 -> 9, of which waited for: 8 -> 3; matrix products, arithmetic and copies ran while one was open for 6% -> 14% of each run, Pallas kernels for 0% -> 0%
where the time goes in v2:
time: 218 us; the launch traced here: 214 us
  other arithmetic  87.1 us (40%)
  blocking collectives  45.7 us (21%)
  starting transfers between devices  32.3 us (15%)
  local copies, waits for them, and re-layouts  19.3 us (9%)
  matrix products  14.8 us (7%)
  waiting for transfers between devices  11.3 us (5%)
  between operations  3.4 us (2%)
    all_to_all x1, blocking collectives, spread_sum(): lax.all_to_all(jnp.broadcast_to(part[None], (depth,) + part.shape), 'pz',...  29.1 us
    another operation x7, other arithmetic, ritz(): lower = jnp.linalg.cholesky(gram_m)  27.9 us
    another operation x6, other arithmetic, ritz(): jax.scipy.linalg.solve_triangular(lower, filtered, lower=True, trans=1)  22.1 us
    ppermute x4, starting transfers between devices, padded_2(): lax.ppermute(tail, axis, [(i, (i + 1) % count) for i in range(ends)])  18.5 us
    all_to_all x1, blocking collectives, spread_sum(): part = jnp.sum(lax.all_to_all(pieces, plane, 0, 0), axis=0)  16.6 us
    reduce_sum x9, other arithmetic, assemble(): entry_value = jnp.sum(gradients[first] * gradients[second], axis=0) * weight  10.9 us
    unnamed x25, local copies, waits for them, and re-layouts  9.75 us
    all_to_all x1, waiting for transfers between devices, spread_sum(): lax.all_to_all(jnp.broadcast_to(part[None], (count,) + part.shape), plane...  8.23 us
  transfers between devices with their start and end apart: 9, of which 3 were waited for; matrix products, arithmetic and copies ran while one was open for 14% of the time, Pallas kernels for 0%

profile of v2, /device:TPU:1, one launch (start us, length us, event | category | flops | bytes accessed | tf_op | source)
XLA Modules:
  0.0 213.8 jit_solution(1895736307202314210)
XLA Ops:
  0.6 1.7 copy.40
  3.2 4.0 %collective-permute-start = (f32[51,2,8,128]{3,0,2,1:T(8,128)S(1)}, f32[51,2,8,128]{3,0,2,1:T(8,128)S(1)}, u32[]{:S(2)}, u32[]{:S(2)}) collective-permute-start(f32[51,2,8,128]{3,0,2,1:T(8,128)S(1)} %get-tuple-element.125), channel_id=1, source_target_pairs={{0,32},{32,64},{64,96},{96,128},{128,160},{160,192},{192,224},{224... | collective-permute-start | bytes 1253384 | tf_op jit(solution)/shard_map/ppermute | solution.py:16
  10.6 4.7 %collective-permute-start.4 = (f32[48,1,8,128]{3,0,2,1:T(8,128)}, f32[48,1,8,128]{3,0,2,1:T(8,128)}, u32[]{:S(2)}, u32[]{:S(2)}) collective-permute-start(f32[48,1,8,128]{3,0,2,1:T(8,128)} %get-tuple-element.128), channel_id=1, source_target_pairs={{0,32},{32,64},{64,96},{96,128},{128,160},{160,192},{192,224},{224... | collective-permute-start | bytes 589832 | tf_op jit(solution)/shard_map/ppermute | solution.py:16
  17.0 2.7 %collective-permute-done.4 = f32[48,1,8,128]{3,0,2,1:T(8,128)} collective-permute-done((f32[48,1,8,128]{3,0,2,1:T(8,128)}, f32[48,1,8,128]{3,0,2,1:T(8,128)}, u32[]{:S(2)}, u32[]{:S(2)}) %collective-permute-start.4) | collective-permute-done | bytes 196640 | tf_op jit(solution)/shard_map/ppermute | solution.py:16
  20.7 6.3 %collective-permute-start.2 = (f32[51,8,2,128]{3,0,2,1:T(8,128)S(1)}, f32[51,8,2,128]{3,0,2,1:T(8,128)S(1)}, u32[]{:S(2)}, u32[]{:S(2)}) collective-permute-start(f32[51,8,2,128]{3,0,2,1:T(8,128)S(1)} %get-tuple-element.121), channel_id=1, source_target_pairs={{0,1},{1,2},{2,3},{3,4},{4,5},{5,6},{6,7},{7,8},{8,9},{9,10},{10,1... | collective-permute-start | bytes 1253384 | tf_op jit(solution)/shard_map/ppermute | solution.py:16
  27.0 1.9 collective-permute-start.3
  30.4 3.6 %collective-permute-start.6 = (f32[48,6,1,128]{3,0,2,1:T(8,128)S(1)}, f32[48,6,1,128]{3,0,2,1:T(8,128)S(1)}, u32[]{:S(2)}, u32[]{:S(2)}) collective-permute-start(f32[48,6,1,128]{3,0,2,1:T(8,128)S(1)} %get-tuple-element.123), channel_id=1, source_target_pairs={{0,1},{1,2},{2,3},{3,4},{4,5},{5,6},{6,7},{7,8},{8,9},{9,10},{10,1... | collective-permute-start | bytes 442376 | tf_op jit(solution)/shard_map/ppermute | solution.py:16
  34.1 2.4 %collective-permute-start.7 = (f32[48,6,1,128]{3,0,2,1:T(8,128)S(1)}, f32[48,6,1,128]{3,0,2,1:T(8,128)S(1)}, u32[]{:S(2)}, u32[]{:S(2)}) collective-permute-start(f32[48,6,1,128]{3,0,2,1:T(8,128)S(1)} %get-tuple-element.124), channel_id=1, source_target_pairs={{1,0},{2,1},{3,2},{4,3},{5,4},{6,5},{7,6},{8,7},{9,8},{10,9},{11,1... | collective-permute-start | bytes 442376 | tf_op jit(solution)/shard_map/ppermute | solution.py:18
  47.6 1.6 multiply_reduce_fusion.39
  49.2 1.6 multiply_reduce_fusion.19
  54.9 4.3 %broadcast_divide_fusion = (f32[48,6,10,128]{3,0,2,1:T(8,128)S(1)}, f32[48,6,10,128]{3,0,2,1:T(8,128)S(1)}) fusion(f32[6,10,128]{2,1,0:T(8,128)S(1)} %get-tuple-element.115, f32[6,10,128]{2,1,0:T(8,128)S(1)} %get-tuple-element.269, f32[51,8,10,128]{3,0,2,1:T(8,128)S(1)} %get-tuple-element.120, f32[6,10,128]{2,1,0:T(8,128)S(1)} %get-tuple-element.266, ...), kind=kLoop, calls=%fused_computation.102 | loop fusion | flops 11059200 | bytes 16121856 | tf_op jit(solution)/shard_map/div | solution.py:256
  60.9 2.9 %select_reduce_fusion = (f32[192]{0:T(256)S(1)}, f32[192,192]{0,1:T(8,128)S(1)}) fusion(f32[48,4,8,128]{3,0,2,1:T(8,128)S(1)} %copy-done.2, f32[48,4,8,128]{3,0,2,1:T(8,128)S(1)} %slice.812, f32[48,4,8,128]{3,0,2,1:T(8,128)S(1)} %slice.810, f32[48,4,8,128]{3,0,2,1:T(8,128)S(1)} %copy.40, f32[4,8,128]{2,1,0:T(8,128)S(1)} %slice.840), kind=kOutput, calls=%fused_computation.121 | convolution fusion | flops 1817554688 | bytes 3310336 | tf_op jit(solution)/shard_map/dot_general | solution.py:172
  64.2 5.8 %fusion.20 = f32[144,4,8,128]{3,0,2,1:T(8,128)S(1)} fusion(f32[144,6,10,128]{3,0,2,1:T(8,128)S(1)} %maximum_maximum_fusion, f32[4,8,128]{2,1,0:T(8,128)S(1)} %slice_bitcast_fusion.5, f32[4,8,128]{2,1,0:T(8,128)S(1)} %slice_bitcast_fusion.6, f32[4,8,128]{2,1,0:T(8,128)S(1)} %slice_bitcast_fusion.7, f32[4,8,128]{2,1,0:T(8,128)S(1)} %slice_bitcast_fusion.8, ...), kind=kLoop, calls=%fused_computation.42 | loop fusion | flops 17104896 | bytes 23543808 | tf_op jit(solution)/shard_map/add | solution.py:143
  70.0 2.7 %fusion.65 = f32[192,192]{0,1:T(8,128)S(1)} fusion(f32[144,4,8,128]{3,0,2,1:T(8,128)S(1)} %fusion.20, f32[48,4,8,128]{3,0,2,1:T(8,128)S(1)} %slice.813, f32[48,4,8,128]{3,0,2,1:T(8,128)S(1)} %copy-done.2, f32[48,4,8,128]{3,0,2,1:T(8,128)S(1)} %slice.812, f32[48,4,8,128]{3,0,2,1:T(8,128)S(1)} %slice.810, f32[48,4,8,128]{3,0,2,1:T(8,128)S(1)} %copy.40, ...), kind=kOutput, calls=%fused_computation.104 | convolution fusion | flops 1815232512 | bytes 6587136 | tf_op jit(solution)/shard_map/dot_general | solution.py:169
  73.0 16.6 %all_to_all.15 = f32[32,8,256]{2,1,0:T(8,128)S(1)} all-to-all(f32[32,8,256]{2,1,0:T(8,128)S(1)} %pad_bitcast_fusion), channel_id=1, replica_groups=mesh['px'=16,'pz'=16,'pc'=2] {'px','pc'}, dimensions={0} | all-to-all | bytes 524288 | tf_op jit(solution)/shard_map/all_to_all | solution.py:183
  89.7 29.1 %all_to_all.16 = f32[16,8,256]{2,1,0:T(8,128)S(1)} all-to-all(f32[16,8,256]{2,1,0:T(8,128)S(1)} %broadcast_in_dim.168), channel_id=1, replica_groups=mesh['px'=16,'pz'=16,'pc'=2] {'pz'}, dimensions={0} | all-to-all | bytes 262144 | tf_op jit(solution)/shard_map/all_to_all | solution.py:185
  119.5 6.8 %all-to-all-start.2 = ((f32[32,8,256]{2,1,0:T(8,128)}), f32[32,8,256]{2,1,0:T(8,128)S(1)}, u32[]{:S(2)}, u32[]{:S(2)}) async-start(f32[32,8,256]{2,1,0:T(8,128)} %broadcast_in_dim.169), calls=%async_computation.2 | async-start | bytes 524288 | tf_op jit(solution)/shard_map/all_to_all | solution.py:187
  127.0 8.2 %all-to-all-done.2 = f32[32,8,256]{2,1,0:T(8,128)S(1)} async-done(((f32[32,8,256]{2,1,0:T(8,128)}), f32[32,8,256]{2,1,0:T(8,128)S(1)}, u32[]{:S(2)}, u32[]{:S(2)}) %all-to-all-start.2) | async-done | bytes 262176 | tf_op jit(solution)/shard_map/all_to_all | solution.py:187
  136.2 1.6 fusion.70
  137.8 1.7 copy.47
  144.7 12.3 %cholesky.51 = f32[128,128]{1,0:T(8,128)} custom-call(f32[128,128]{1,0:T(8,128)S(1)} %cholesky.124), custom_call_target="Cholesky" | custom-call | tf_op jit(solution)/shard_map/jit(cholesky)/cholesky | solution.py:156
  159.4 11.3 %custom-call.18 = f32[1,128,128]{1,2,0:T(8,128)} custom-call(f32[1,128,128]{2,1,0:T(8,128)} %get-tuple-element.243), custom_call_target="InvertDiagBlocksLowerTriangular" | custom-call | tf_op jit(solution)/shard_map/jit(cholesky)/cholesky | solution.py:156
  177.6 20.5 %custom-call.19 = f32[2,128,128]{1,2,0:T(8,128)} custom-call(f32[2,128,128]{2,1,0:T(8,128)S(1)} %pad_maximum_fusion.37), custom_call_target="InvertDiagBlocksLowerTriangular" | custom-call | tf_op jit(solution)/shard_map/jit(_solve_triangular)/triangular_solve | solution.py:162
  209.7 2.7 %fusion.53 = f32[6,8,32,128]{3,1,2,0:T(8,128)S(1)} fusion(f32[18,8,32,128]{3,2,1,0:T(8,128)S(1)} %bitcast.229, f32[16,48]{0,1:T(8,128)S(1)} %copy.53, f32[128,48]{0,1:T(8,128)S(1)} %fusion.85), kind=kOutput, calls=%fused_computation.92 | convolution fusion | flops 339942144 | bytes 3173376 | tf_op jit(solution)/shard_map/dot_general | solution.py:269
  (173 shorter events, 53.4 us)
Async XLA Ops:
  0.6 7.9 %copy-start.3 = (f32[48,4,8,128]{3,2,1,0:T(8,128)S(1)}, f32[48,4,8,128]{3,2,1,0:T(8,128)}, u32[]{:S(2)}) copy-start(f32[48,4,8,128]{3,2,1,0:T(8,128)} %param.9) | copy-start | bytes 2359300
  3.2 17.4 %collective-permute-start = (f32[51,2,8,128]{3,0,2,1:T(8,128)S(1)}, f32[51,2,8,128]{3,0,2,1:T(8,128)S(1)}, u32[]{:S(2)}, u32[]{:S(2)}) collective-permute-start(f32[51,2,8,128]{3,0,2,1:T(8,128)S(1)} %get-tuple-element.125), channel_id=1, source_target_pairs={{0,32},{32,64},{64,96},{96,128},{128,160},{160,192},{192,224},{224... | collective-permute-start | bytes 1253384 | tf_op jit(solution)/shard_map/ppermute | solution.py:16
  7.2 13.4 %collective-permute-start.1 = (f32[51,2,8,128]{3,0,2,1:T(8,128)S(1)}, f32[51,2,8,128]{3,0,2,1:T(8,128)S(1)}, u32[]{:S(2)}, u32[]{:S(2)}) collective-permute-start(f32[51,2,8,128]{3,0,2,1:T(8,128)S(1)} %get-tuple-element.126), channel_id=1, source_target_pairs={{32,0},{64,32},{96,64},{128,96},{160,128},{192,160},{224,192},{256... | collective-permute-start | bytes 1253384 | tf_op jit(solution)/shard_map/ppermute | solution.py:18
  9.0 0.9 copy-start.1
  10.6 9.1 %collective-permute-start.4 = (f32[48,1,8,128]{3,0,2,1:T(8,128)}, f32[48,1,8,128]{3,0,2,1:T(8,128)}, u32[]{:S(2)}, u32[]{:S(2)}) collective-permute-start(f32[48,1,8,128]{3,0,2,1:T(8,128)} %get-tuple-element.128), channel_id=1, source_target_pairs={{0,32},{32,64},{64,96},{96,128},{128,160},{160,192},{192,224},{224... | collective-permute-start | bytes 589832 | tf_op jit(solution)/shard_map/ppermute | solution.py:16
  15.3 14.1 %collective-permute-start.5 = (f32[48,1,8,128]{3,0,2,1:T(8,128)}, f32[48,1,8,128]{3,0,2,1:T(8,128)}, u32[]{:S(2)}, u32[]{:S(2)}) collective-permute-start(f32[48,1,8,128]{3,0,2,1:T(8,128)} %get-tuple-element.127), channel_id=1, source_target_pairs={{32,0},{64,32},{96,64},{128,96},{160,128},{192,160},{224,192},{256... | collective-permute-start | bytes 589832 | tf_op jit(solution)/shard_map/ppermute | solution.py:18
  20.7 15.8 %collective-permute-start.2 = (f32[51,8,2,128]{3,0,2,1:T(8,128)S(1)}, f32[51,8,2,128]{3,0,2,1:T(8,128)S(1)}, u32[]{:S(2)}, u32[]{:S(2)}) collective-permute-start(f32[51,8,2,128]{3,0,2,1:T(8,128)S(1)} %get-tuple-element.121), channel_id=1, source_target_pairs={{0,1},{1,2},{2,3},{3,4},{4,5},{5,6},{6,7},{7,8},{8,9},{9,10},{10,1... | collective-permute-start | bytes 1253384 | tf_op jit(solution)/shard_map/ppermute | solution.py:16
  27.0 9.8 %collective-permute-start.3 = (f32[51,8,2,128]{3,0,2,1:T(8,128)S(1)}, f32[51,8,2,128]{3,0,2,1:T(8,128)S(1)}, u32[]{:S(2)}, u32[]{:S(2)}) collective-permute-start(f32[51,8,2,128]{3,0,2,1:T(8,128)S(1)} %get-tuple-element.122), channel_id=1, source_target_pairs={{1,0},{2,1},{3,2},{4,3},{5,4},{6,5},{7,6},{8,7},{9,8},{10,9},{11,1... | collective-permute-start | bytes 1253384 | tf_op jit(solution)/shard_map/ppermute | solution.py:18
  30.4 33.4 %collective-permute-start.6 = (f32[48,6,1,128]{3,0,2,1:T(8,128)S(1)}, f32[48,6,1,128]{3,0,2,1:T(8,128)S(1)}, u32[]{:S(2)}, u32[]{:S(2)}) collective-permute-start(f32[48,6,1,128]{3,0,2,1:T(8,128)S(1)} %get-tuple-element.123), channel_id=1, source_target_pairs={{0,1},{1,2},{2,3},{3,4},{4,5},{5,6},{6,7},{7,8},{8,9},{9,10},{10,1... | collective-permute-start | bytes 442376 | tf_op jit(solution)/shard_map/ppermute | solution.py:16
  34.1 29.8 %collective-permute-start.7 = (f32[48,6,1,128]{3,0,2,1:T(8,128)S(1)}, f32[48,6,1,128]{3,0,2,1:T(8,128)S(1)}, u32[]{:S(2)}, u32[]{:S(2)}) collective-permute-start(f32[48,6,1,128]{3,0,2,1:T(8,128)S(1)} %get-tuple-element.124), channel_id=1, source_target_pairs={{1,0},{2,1},{3,2},{4,3},{5,4},{6,5},{7,6},{8,7},{9,8},{10,9},{11,1... | collective-permute-start | bytes 442376 | tf_op jit(solution)/shard_map/ppermute | solution.py:18
  59.2 4.6 %copy-start = (f32[48,6,10,128]{3,0,2,1:T(8,128)}, f32[48,6,10,128]{3,0,2,1:T(8,128)S(1)}, u32[]{:S(2)}) copy-start(f32[48,6,10,128]{3,0,2,1:T(8,128)S(1)} %get-tuple-element.113) | copy-start | bytes 4423684
  59.3 1.7 copy-start.2
  119.5 15.7 %all-to-all-start.2 = ((f32[32,8,256]{2,1,0:T(8,128)}), f32[32,8,256]{2,1,0:T(8,128)S(1)}, u32[]{:S(2)}, u32[]{:S(2)}) async-start(f32[32,8,256]{2,1,0:T(8,128)} %broadcast_in_dim.169), calls=%async_computation.2 | async-start | bytes 524288 | tf_op jit(solution)/shard_map/all_to_all | solution.py:187
  143.0 0.6 copy-start.4
  143.0 0.6 copy-start.5
  143.0 0.6 copy-start.6
  199.3 6.3 %copy-start.7 = (f32[2,128,128]{1,2,0:T(8,128)S(1)}, f32[2,128,128]{1,2,0:T(8,128)}, u32[]{:S(2)}) copy-start(f32[2,128,128]{1,2,0:T(8,128)} %custom-call.19) | copy-start | bytes 393220

commit v3 on v2

--- a/solution.py
+++ b/solution.py
@@ -1,8 +1,107 @@
 import jax
 import jax.numpy as jnp
 from jax import lax
+from jax.experimental import pallas as pl
+from jax.experimental.pallas import tpu as pltpu
 from jax.sharding import Mesh
 from jax.sharding import PartitionSpec as P
+
+
+VECS = 48
+HI = lax.Precision.HIGHEST
+
+
+def dots(a, b, dims):
+    return lax.dot_general(a, b, (dims, ((), ())), precision=HI, preferred_element_type=jnp.float32)
+
+
+def eliminated(gram):
+    order = gram.shape[0]
+    third = order // 3
+    rows = lax.broadcasted_iota(jnp.int32, gram.shape, 0)
+    cols = lax.broadcasted_iota(jnp.int32, gram.shape, 1)
+    inverse = jnp.where(rows == cols, 1.0, 0.0).astype(jnp.float32)
+    place = lax.broadcasted_iota(jnp.int32, (third, 128), 0)
+    done = []
+    for j in range(3):
+        left = gram[:third]
+        right = inverse[:third]
+        gram = gram[third:]
+        inverse = inverse[third:]
+        pivots = jnp.ones((third, 128), jnp.float32)
+        for k in range(third):
+            c = third * j + k
+            column = jnp.broadcast_to(left[:, c : c + 1], (third, 128))
+            pivot = column[k : k + 1, :]
+            pivots = jnp.where(place == k, pivot, pivots)
+            factor = jnp.where(place > k, column * (1.0 / pivot), 0.0)
+            factor = jnp.concatenate([factor, factor], axis=1)
+            left, right = (
+                left - factor * left[k : k + 1, :],
+                right - factor * right[k : k + 1, :],
+            )
+        scale = 1.0 / jnp.sqrt(pivots)
+        scale = jnp.concatenate([scale, scale], axis=1)
+        left = left * scale
+        right = right * scale
+        done.append(right)
+        if j < 2:
+            flipped = left.T[third * (j + 1) : order]
+            gram = gram - dots(flipped, left, ((1,), (0,)))
+            inverse = inverse - dots(flipped, right, ((1,), (0,)))
+    return jnp.concatenate(done, axis=0)
+
+
+def ritz_core(total):
+    vecs = VECS
+    order = 3 * vecs
+    full = 4 * vecs
+    rows = lax.broadcasted_iota(jnp.int32, total.shape, 0)
+    cols = lax.broadcasted_iota(jnp.int32, total.shape, 1)
+    flipped = total.T
+    diagonal = total[full : full + 1, :]
+    gram_k = jnp.where(rows <= cols, total, flipped)
+    gram_m = jnp.where(rows > cols, total, jnp.where(rows == cols, diagonal, flipped))
+    eye = rows == cols
+    top = lambda g: jnp.sum(jnp.where(eye, g, 0.0)[:vecs], axis=1, keepdims=True)
+    quotient = top(gram_k) / top(gram_m)
+
+    def joined(g):
+        mid = g[vecs : 2 * vecs] - quotient * g[2 * vecs : 3 * vecs]
+        return jnp.concatenate([g[:vecs], mid, g[3 * vecs : full]], axis=0)
+
+    gram_k = joined(joined(gram_k).T)
+    gram_m = joined(joined(gram_m).T)
+    gram_m = jnp.concatenate([gram_m, jnp.zeros((order, 256 - order), jnp.float32)], axis=1)
+    inverse = eliminated(gram_m)[:, :order]
+    half = dots(inverse, gram_k, ((1,), (0,)))
+    reduced = dots(half, inverse, ((1,), (1,)))
+    bound = jnp.max(jnp.sum(jnp.abs(reduced), axis=1, keepdims=True), axis=0, keepdims=True)
+    eye = lax.broadcasted_iota(jnp.int32, (order, order), 0) == lax.broadcasted_iota(
+        jnp.int32, (order, order), 1
+    )
+    shifted = jnp.where(eye, 1.0, 0.0) - reduced / bound
+    filtered = dots(shifted[:vecs], shifted, ((1,), (0,)))
+    return dots(filtered, inverse, ((1,), (0,))), quotient
+
+
+def ritz_kernel(total_ref, coeffs_ref, quotient_ref):
+    coeffs, quotient = ritz_core(total_ref[...])
+    coeffs_ref[...] = coeffs
+    quotient_ref[...] = jnp.broadcast_to(quotient, quotient_ref.shape)
+
+
+def ritz_call(total):
+    return pl.pallas_call(
+        ritz_kernel,
+        out_shape=(
+            jax.ShapeDtypeStruct((VECS, 3 * VECS), jnp.float32),
+            jax.ShapeDtypeStruct((VECS, 128), jnp.float32),
+        ),
+        in_specs=[pl.BlockSpec(memory_space=pltpu.VMEM)],
+        out_specs=(pl.BlockSpec(memory_space=pltpu.VMEM),) * 2,
+        compiler_params=pltpu.CompilerParams(vmem_limit_bytes=32 * 2**20),
+    )(total)
 
 
 def padded_2(cells, sides, width):
@@ -152,16 +251,6 @@
     return result
 
 
-def ritz(gram_k, gram_m, vecs):
-    lower = jnp.linalg.cholesky(gram_m)
-    half = jax.scipy.linalg.solve_triangular(lower, gram_k, lower=True)
-    reduced = jax.scipy.linalg.solve_triangular(lower, half.T, lower=True)
-    bound = jnp.max(jnp.sum(jnp.abs(reduced), axis=1))
-    shifted = jnp.eye(reduced.shape[0], dtype=jnp.float32) - reduced / bound
-    filtered = jnp.dot(shifted, shifted[:, :vecs], precision=lax.Precision.HIGHEST)
-    return jax.scipy.linalg.solve_triangular(lower, filtered, lower=True, trans=1)
-
-
 def local_grams(vectors, k_vectors, mass):
     flat = vectors.reshape(vectors.shape[0], -1)
     k_flat = k_vectors.reshape(vectors.shape[0], -1)
@@ -194,31 +283,7 @@
     square = jnp.triu(gram_k) + jnp.tril(gram_m, -1)
     diagonal = jnp.sum(jnp.where(eye, gram_m, 0.0), axis=0)
     rows = jnp.concatenate([square, jnp.broadcast_to(diagonal[None], (256 - order, order))])
-    total = spread_sum(jnp.pad(rows, ((0, 0), (0, 256 - order))))
-    square = total[:order, :order]
-    diagonal = total[order, :order]
-    high = jnp.triu(square)
-    low = jnp.tril(square, -1)
-    return (high + jnp.triu(square, 1).T, low + low.T + jnp.where(eye, diagonal[None], 0.0))
-
-
-def combined(gram, quotient):
-    vecs = quotient.shape[0]
-    rows = jnp.concatenate(
-        [
-            gram[:vecs],
-            gram[vecs : 2 * vecs] - quotient[:, None] * gram[2 * vecs : 3 * vecs],
-            gram[3 * vecs :],
-        ]
-    )
-    return jnp.concatenate(
-        [
-            rows[:, :vecs],
-            rows[:, vecs : 2 * vecs] - quotient[None, :] * rows[:, 2 * vecs : 3 * vecs],
-            rows[:, 3 * vecs :],
-        ],
-        axis=1,
-    )
+    return spread_sum(jnp.pad(rows, ((0, 0), (0, 256 - order))))
 
 
 def shards(offsets, block, prior):
@@ -260,14 +325,12 @@
     w_part = w_wide[:, 1:-1, 1:-1, :]
     basis = jnp.concatenate([block, u_part, w_part, prior])
     k_basis = jnp.concatenate([k_wide[:, 1:-1, 1:-1, :], applied])
-    gram_k, gram_m = summed_grams(*local_grams(basis, k_basis, mass))
-    quotient = jnp.diagonal(gram_k[:vecs, :vecs]) / jnp.diagonal(gram_m[:vecs, :vecs])
-    search = u_part - quotient[:, None, None, None] * w_part
-    coeffs = ritz(combined(gram_k, quotient), combined(gram_m, quotient), vecs)
+    coeffs, quotient = ritz_call(summed_grams(*local_grams(basis, k_basis, mass)))
+    search = u_part - quotient[:, :1, None, None] * w_part
     scale = jnp.sqrt(jnp.float32(total_a * total_b * depth))
     flat_basis = jnp.concatenate([block, search, prior]).reshape(3 * vecs, -1)
     new_block = scale * lax.dot_general(
-        coeffs, flat_basis, (((0,), (0,)), ((), ())), precision=lax.Precision.HIGHEST
+        coeffs, flat_basis, (((1,), (0,)), ((), ())), precision=lax.Precision.HIGHEST
     )
     return (new_block.reshape(block.shape), search)
 

time: 218 us -> 170 us (0.78)
  other arithmetic: 87.1 us -> 42.4 us
  Pallas kernels: 0 us -> 14.3 us
  blocking collectives: 45.7 us -> 59.2 us
  local copies, waits for them, and re-layouts: 19.3 us -> 10.6 us
  starting transfers between devices: 32.3 us -> 25.6 us
  waiting for transfers between devices: 11.3 us -> 4.77 us
  matrix products: 14.8 us -> 8.28 us
    another operation x13 -> x0, other arithmetic: 50 us -> none  [the longest x7 27.9 us: ritz(): lower = jnp.linalg.cholesky(gram_m)]
    all_to_all x0 -> x1, blocking collectives: none -> 15.2 us  [spread_sum(): lax.all_to_all(jnp.broadcast_to(part[None], (count,) + part.shape), plane...]
    pallas_call x0 -> x1, Pallas kernels: none -> 14.3 us  [ritz_call(): pl.pallas_call(ritz_kernel, out_shape=(jax.ShapeDtypeStruct((VECS, 3 * VE...]
    reduce_sum x9, other arithmetic: 10.9 us -> 22.9 us  [assemble(): entry_value = jnp.sum(gradients[first] * gradients[second], axis=0) * weight]
    all_to_all x1 -> x0, waiting for transfers between devices: 8.23 us -> none  [spread_sum(): lax.all_to_all(jnp.broadcast_to(part[None], (count,) + part.shape), plane...]
    all_to_all x1 -> x0, starting transfers between devices: 6.8 us -> none  [spread_sum(): lax.all_to_all(jnp.broadcast_to(part[None], (count,) + part.shape), plane...]
    another operation x11 -> x0, matrix products: 6.34 us -> none  [the longest x3 2.45 us: ritz(): reduced = jax.scipy.linalg.solve_triangular(lower, half.T, lower=True)]
    unnamed x25 -> x16, local copies, waits for them, and re-layouts: 9.75 us -> 8.07 us
  transfers between devices with their start and end apart: 9 -> 8, of which waited for: 3 -> 2; matrix products, arithmetic and copies ran while one was open for 14% -> 24% of each run, Pallas kernels for 0% -> 0%
where the time goes in v3:
time: 170 us; the launch traced here: 167 us
  blocking collectives  59.2 us (35%)
  other arithmetic  42.4 us (25%)
  starting transfers between devices  25.6 us (15%)
  Pallas kernels  14.3 us (8%)
  local copies, waits for them, and re-layouts  10.6 us (6%)
  matrix products  8.28 us (5%)
  waiting for transfers between devices  4.77 us (3%)
    all_to_all x1, blocking collectives, spread_sum(): lax.all_to_all(jnp.broadcast_to(part[None], (depth,) + part.shape), 'pz',...  28 us
    reduce_sum x9, other arithmetic, assemble(): entry_value = jnp.sum(gradients[first] * gradients[second], axis=0) * weight  22.9 us
    ppermute x4, starting transfers between devices, padded_2(): lax.ppermute(tail, axis, [(i, (i + 1) % count) for i in range(ends)])  18.8 us
    all_to_all x1, blocking collectives, spread_sum(): part = jnp.sum(lax.all_to_all(pieces, plane, 0, 0), axis=0)  16 us
    all_to_all x1, blocking collectives, spread_sum(): lax.all_to_all(jnp.broadcast_to(part[None], (count,) + part.shape), plane...  15.2 us
    pallas_call x1, Pallas kernels, ritz_call(): pl.pallas_call(ritz_kernel, out_shape=(jax.ShapeDtypeStruct((VECS, 3 * VE...  14.3 us
    unnamed x16, local copies, waits for them, and re-layouts  8.07 us
    ppermute x4, starting transfers between devices, padded_2(): lax.ppermute(head, axis, [((i + 1) % count, i) for i in range(ends)])  6.8 us
  transfers between devices with their start and end apart: 8, of which 2 were waited for; matrix products, arithmetic and copies ran while one was open for 24% of the time, Pallas kernels for 0%

profile of v3, /device:TPU:1, one launch (start us, length us, event | category | flops | bytes accessed | tf_op | source)
XLA Modules:
  0.0 166.8 jit_solution(14594879820151580974)
XLA Ops:
  0.6 1.7 copy.29
  4.0 4.0 %collective-permute-start = (f32[51,2,8,128]{3,0,2,1:T(8,128)}, f32[51,2,8,128]{3,0,2,1:T(8,128)S(1)}, u32[]{:S(2)}, u32[]{:S(2)}) collective-permute-start(f32[51,2,8,128]{3,0,2,1:T(8,128)} %get-tuple-element.82), channel_id=1, source_target_pairs={{0,32},{32,64},{64,96},{96,128},{128,160},{160,192},{192,224},{224... | collective-permute-start | bytes 1253384 | tf_op jit(solution)/shard_map/ppermute | solution.py:115
  8.0 1.3 collective-permute-start.1
  11.4 4.0 %collective-permute-start.4 = (f32[48,1,8,128]{3,0,2,1:T(8,128)}, f32[48,1,8,128]{3,0,2,1:T(8,128)S(1)}, u32[]{:S(2)}, u32[]{:S(2)}) collective-permute-start(f32[48,1,8,128]{3,0,2,1:T(8,128)} %get-tuple-element.85), channel_id=1, source_target_pairs={{0,32},{32,64},{64,96},{96,128},{128,160},{160,192},{192,224},{224... | collective-permute-start | bytes 589832 | tf_op jit(solution)/shard_map/ppermute | solution.py:115
  17.1 3.4 %collective-permute-done.4 = f32[48,1,8,128]{3,0,2,1:T(8,128)S(1)} collective-permute-done((f32[48,1,8,128]{3,0,2,1:T(8,128)}, f32[48,1,8,128]{3,0,2,1:T(8,128)S(1)}, u32[]{:S(2)}, u32[]{:S(2)}) %collective-permute-start.4) | collective-permute-done | bytes 196640 | tf_op jit(solution)/shard_map/ppermute | solution.py:115
  20.6 7.2 %collective-permute-start.2 = (f32[51,8,2,128]{3,0,2,1:T(8,128)S(1)}, f32[51,8,2,128]{3,0,2,1:T(8,128)S(1)}, u32[]{:S(2)}, u32[]{:S(2)}) collective-permute-start(f32[51,8,2,128]{3,0,2,1:T(8,128)S(1)} %get-tuple-element.78), channel_id=1, source_target_pairs={{0,1},{1,2},{2,3},{3,4},{4,5},{5,6},{6,7},{7,8},{8,9},{9,10},{10,1... | collective-permute-start | bytes 1253384 | tf_op jit(solution)/shard_map/ppermute | solution.py:115
  27.8 1.9 %collective-permute-start.3 = (f32[51,8,2,128]{3,0,2,1:T(8,128)S(1)}, f32[51,8,2,128]{3,0,2,1:T(8,128)S(1)}, u32[]{:S(2)}, u32[]{:S(2)}) collective-permute-start(f32[51,8,2,128]{3,0,2,1:T(8,128)S(1)} %get-tuple-element.79), channel_id=1, source_target_pairs={{1,0},{2,1},{3,2},{4,3},{5,4},{6,5},{7,6},{8,7},{9,8},{10,9},{11,1... | collective-permute-start | bytes 1253384 | tf_op jit(solution)/shard_map/ppermute | solution.py:117
  30.2 3.6 %collective-permute-start.6 = (f32[48,6,1,128]{3,0,2,1:T(8,128)S(1)}, f32[48,6,1,128]{3,0,2,1:T(8,128)S(1)}, u32[]{:S(2)}, u32[]{:S(2)}) collective-permute-start(f32[48,6,1,128]{3,0,2,1:T(8,128)S(1)} %get-tuple-element.80), channel_id=1, source_target_pairs={{0,1},{1,2},{2,3},{3,4},{4,5},{5,6},{6,7},{7,8},{8,9},{9,10},{10,1... | collective-permute-start | bytes 442376 | tf_op jit(solution)/shard_map/ppermute | solution.py:115
  33.9 2.3 %collective-permute-start.7 = (f32[48,6,1,128]{3,0,2,1:T(8,128)S(1)}, f32[48,6,1,128]{3,0,2,1:T(8,128)S(1)}, u32[]{:S(2)}, u32[]{:S(2)}) collective-permute-start(f32[48,6,1,128]{3,0,2,1:T(8,128)S(1)} %get-tuple-element.81), channel_id=1, source_target_pairs={{1,0},{2,1},{3,2},{4,3},{5,4},{6,5},{7,6},{8,7},{9,8},{10,9},{11,1... | collective-permute-start | bytes 442376 | tf_op jit(solution)/shard_map/ppermute | solution.py:117
  36.2 1.4 collective-permute-done.3
  41.9 1.3 multiply_reduce_fusion.25
  44.1 1.3 multiply_reduce_fusion.38
  48.3 13.6 %multiply_reduce_fusion.39 = (f32[7,11,127]{2,1,0:T(8,128)S(1)}, f32[7,11,127]{2,1,0:T(8,128)S(1)}, f32[7,11,127]{2,1,0:T(8,128)S(1)}, f32[7,11,127]{2,1,0:T(8,1...) fusion(f32[3,7,11,127]{3,0,2,1:T(4,128)S(1)} %get-tuple-element, ...), kind=kLoop, calls=%fused_computation.173 | loop fusion | flops 704088 | bytes 1173480 | tf_op jit(solution)/shard_map/reduce_sum | solution.py:191
  61.9 1.6 multiply_reduce_fusion.19
  67.6 4.4 %broadcast_divide_fusion = (f32[48,6,10,128]{3,0,2,1:T(8,128)S(1)}, f32[48,6,10,128]{3,0,2,1:T(8,128)S(1)}) fusion(f32[6,10,128]{2,1,0:T(8,128)S(1)} %get-tuple-element.72, f32[6,10,128]{2,1,0:T(8,128)S(1)} %get-tuple-element.206, f32[51,8,10,128]{3,0,2,1:T(8,128)S(1)} %get-tuple-element.77, f32[6,10,128]{2,1,0:T(8,128)S(1)} %get-tuple-element.203, ...), kind=kLoop, calls=%fused_computation.96 | loop fusion | flops 11059200 | bytes 16121856 | tf_op jit(solution)/shard_map/div | solution.py:321
  72.2 1.5 copy-done.2
  73.7 2.9 %select_reduce_fusion = (f32[192]{0:T(256)S(1)}, f32[192,192]{0,1:T(8,128)S(1)}) fusion(f32[48,4,8,128]{3,0,2,1:T(8,128)S(1)} %copy-done.2, f32[48,4,8,128]{3,0,2,1:T(8,128)S(1)} %slice.626, f32[48,4,8,128]{3,0,2,1:T(8,128)S(1)} %slice.624, f32[48,4,8,128]{3,0,2,1:T(8,128)S(1)} %copy.29, f32[4,8,128]{2,1,0:T(8,128)S(1)} %slice.654), kind=kOutput, calls=%fused_computation.108 | convolution fusion | flops 1817554688 | bytes 3310336 | tf_op jit(solution)/shard_map/dot_general | solution.py:261
  76.9 5.7 %fusion.20 = f32[144,4,8,128]{3,0,2,1:T(8,128)S(1)} fusion(f32[144,6,10,128]{3,0,2,1:T(8,128)S(1)} %maximum_maximum_fusion, f32[4,8,128]{2,1,0:T(8,128)S(1)} %slice_bitcast_fusion, f32[4,8,128]{2,1,0:T(8,128)S(1)} %slice_bitcast_fusion.1, f32[4,8,128]{2,1,0:T(8,128)S(1)} %slice_bitcast_fusion.2, f32[4,8,128]{2,1,0:T(8,128)S(1)} %slice_bitcast_fusion.3, ...), kind=kLoop, calls=%fused_computation.40 | loop fusion | flops 17104896 | bytes 23543808 | tf_op jit(solution)/shard_map/add | solution.py:242
  82.7 2.7 %fusion.65 = f32[192,192]{0,1:T(8,128)S(1)} fusion(f32[144,4,8,128]{3,0,2,1:T(8,128)S(1)} %fusion.20, f32[48,4,8,128]{3,0,2,1:T(8,128)S(1)} %slice.627, f32[48,4,8,128]{3,0,2,1:T(8,128)S(1)} %copy-done.2, f32[48,4,8,128]{3,0,2,1:T(8,128)S(1)} %slice.626, f32[48,4,8,128]{3,0,2,1:T(8,128)S(1)} %slice.624, f32[48,4,8,128]{3,0,2,1:T(8,128)S(1)} %copy.29, ...), kind=kOutput, calls=%fused_computation.98 | convolution fusion | flops 1815232512 | bytes 6587136 | tf_op jit(solution)/shard_map/dot_general | solution.py:258
  85.8 16.0 %all_to_all.15 = f32[32,8,256]{2,1,0:T(8,128)S(1)} all-to-all(f32[32,8,256]{2,1,0:T(8,128)S(1)} %pad_bitcast_fusion), channel_id=1, replica_groups=mesh['px'=16,'pz'=16,'pc'=2] {'px','pc'}, dimensions={0} | all-to-all | bytes 524288 | tf_op jit(solution)/shard_map/all_to_all | solution.py:272
  101.8 28.0 %all_to_all.16 = f32[16,8,256]{2,1,0:T(8,128)S(1)} all-to-all(f32[16,8,256]{2,1,0:T(8,128)S(1)} %broadcast_in_dim.140), channel_id=1, replica_groups=mesh['px'=16,'pz'=16,'pc'=2] {'pz'}, dimensions={0} | all-to-all | bytes 262144 | tf_op jit(solution)/shard_map/all_to_all | solution.py:274
  129.9 15.2 %all_to_all.17 = f32[32,8,256]{2,1,0:T(8,128)S(1)} all-to-all(f32[32,8,256]{2,1,0:T(8,128)S(1)} %broadcast_in_dim.141), channel_id=1, replica_groups=mesh['px'=16,'pz'=16,'pc'=2] {'px','pc'}, dimensions={0} | all-to-all | bytes 524288 | tf_op jit(solution)/shard_map/all_to_all | solution.py:276
  145.1 14.3 %shard_map.50 = (f32[48,144]{1,0:T(8,128)S(1)}, f32[48,128]{1,0:T(8,128)S(1)}) custom-call(f32[256,256]{1,0:T(8,128)S(1)} %bitcast.177), custom_call_target="tpu_custom_call" | custom-call | tf_op jit(solution)/shard_map/pallas_call | solution.py:95
  162.8 2.7 %fusion.53 = f32[6,8,32,128]{3,1,2,0:T(8,128)S(1)} fusion(f32[48,144]{1,0:T(8,128)S(1)} %get-tuple-element.5, f32[18,8,32,128]{3,2,1,0:T(8,128)S(1)} %bitcast.178), kind=kOutput, calls=%fused_computation.90 | convolution fusion | flops 339935232 | bytes 3173376 | tf_op jit(solution)/shard_map/dot_general | solution.py:332
  (108 shorter events, 23.3 us)
Async XLA Ops:
  0.6 8.6 %copy-start.3 = (f32[48,4,8,128]{3,2,1,0:T(8,128)S(1)}, f32[48,4,8,128]{3,2,1,0:T(8,128)}, u32[]{:S(2)}) copy-start(f32[48,4,8,128]{3,2,1,0:T(8,128)} %param.7) | copy-start | bytes 2359300
  4.0 16.5 %collective-permute-start = (f32[51,2,8,128]{3,0,2,1:T(8,128)}, f32[51,2,8,128]{3,0,2,1:T(8,128)S(1)}, u32[]{:S(2)}, u32[]{:S(2)}) collective-permute-start(f32[51,2,8,128]{3,0,2,1:T(8,128)} %get-tuple-element.82), channel_id=1, source_target_pairs={{0,32},{32,64},{64,96},{96,128},{128,160},{160,192},{192,224},{224... | collective-permute-start | bytes 1253384 | tf_op jit(solution)/shard_map/ppermute | solution.py:115
  8.0 12.5 %collective-permute-start.1 = (f32[51,2,8,128]{3,0,2,1:T(8,128)S(1)}, f32[51,2,8,128]{3,0,2,1:T(8,128)S(1)}, u32[]{:S(2)}, u32[]{:S(2)}) collective-permute-start(f32[51,2,8,128]{3,0,2,1:T(8,128)S(1)} %get-tuple-element.83), channel_id=1, source_target_pairs={{32,0},{64,32},{96,64},{128,96},{160,128},{192,160},{224,192},{256... | collective-permute-start | bytes 1253384 | tf_op jit(solution)/shard_map/ppermute | solution.py:117
  9.7 0.9 copy-start.1
  11.4 9.1 %collective-permute-start.4 = (f32[48,1,8,128]{3,0,2,1:T(8,128)}, f32[48,1,8,128]{3,0,2,1:T(8,128)S(1)}, u32[]{:S(2)}, u32[]{:S(2)}) collective-permute-start(f32[48,1,8,128]{3,0,2,1:T(8,128)} %get-tuple-element.85), channel_id=1, source_target_pairs={{0,32},{32,64},{64,96},{96,128},{128,160},{160,192},{192,224},{224... | collective-permute-start | bytes 589832 | tf_op jit(solution)/shard_map/ppermute | solution.py:115
  15.4 14.8 %collective-permute-start.5 = (f32[48,1,8,128]{3,0,2,1:T(8,128)}, f32[48,1,8,128]{3,0,2,1:T(8,128)S(1)}, u32[]{:S(2)}, u32[]{:S(2)}) collective-permute-start(f32[48,1,8,128]{3,0,2,1:T(8,128)} %get-tuple-element.84), channel_id=1, source_target_pairs={{32,0},{64,32},{96,64},{128,96},{160,128},{192,160},{224,192},{256... | collective-permute-start | bytes 589832 | tf_op jit(solution)/shard_map/ppermute | solution.py:117
  20.6 15.6 %collective-permute-start.2 = (f32[51,8,2,128]{3,0,2,1:T(8,128)S(1)}, f32[51,8,2,128]{3,0,2,1:T(8,128)S(1)}, u32[]{:S(2)}, u32[]{:S(2)}) collective-permute-start(f32[51,8,2,128]{3,0,2,1:T(8,128)S(1)} %get-tuple-element.78), channel_id=1, source_target_pairs={{0,1},{1,2},{2,3},{3,4},{4,5},{5,6},{6,7},{7,8},{8,9},{9,10},{10,1... | collective-permute-start | bytes 1253384 | tf_op jit(solution)/shard_map/ppermute | solution.py:115
  27.8 9.8 %collective-permute-start.3 = (f32[51,8,2,128]{3,0,2,1:T(8,128)S(1)}, f32[51,8,2,128]{3,0,2,1:T(8,128)S(1)}, u32[]{:S(2)}, u32[]{:S(2)}) collective-permute-start(f32[51,8,2,128]{3,0,2,1:T(8,128)S(1)} %get-tuple-element.79), channel_id=1, source_target_pairs={{1,0},{2,1},{3,2},{4,3},{5,4},{6,5},{7,6},{8,7},{9,8},{10,9},{11,1... | collective-permute-start | bytes 1253384 | tf_op jit(solution)/shard_map/ppermute | solution.py:117
  30.2 46.3 %collective-permute-start.6 = (f32[48,6,1,128]{3,0,2,1:T(8,128)S(1)}, f32[48,6,1,128]{3,0,2,1:T(8,128)S(1)}, u32[]{:S(2)}, u32[]{:S(2)}) collective-permute-start(f32[48,6,1,128]{3,0,2,1:T(8,128)S(1)} %get-tuple-element.80), channel_id=1, source_target_pairs={{0,1},{1,2},{2,3},{3,4},{4,5},{5,6},{6,7},{7,8},{8,9},{9,10},{10,1... | collective-permute-start | bytes 442376 | tf_op jit(solution)/shard_map/ppermute | solution.py:115
  33.9 42.7 %collective-permute-start.7 = (f32[48,6,1,128]{3,0,2,1:T(8,128)S(1)}, f32[48,6,1,128]{3,0,2,1:T(8,128)S(1)}, u32[]{:S(2)}, u32[]{:S(2)}) collective-permute-start(f32[48,6,1,128]{3,0,2,1:T(8,128)S(1)} %get-tuple-element.81), channel_id=1, source_target_pairs={{1,0},{2,1},{3,2},{4,3},{5,4},{6,5},{7,6},{8,7},{9,8},{10,9},{11,1... | collective-permute-start | bytes 442376 | tf_op jit(solution)/shard_map/ppermute | solution.py:117
  72.0 4.6 %copy-start = (f32[48,6,10,128]{3,0,2,1:T(8,128)}, f32[48,6,10,128]{3,0,2,1:T(8,128)S(1)}, u32[]{:S(2)}) copy-start(f32[48,6,10,128]{3,0,2,1:T(8,128)S(1)} %get-tuple-element.70) | copy-start | bytes 4423684
  72.0 1.7 %copy-start.2 = (f32[48,4,8,128]{3,0,2,1:T(8,128)S(1)}, f32[48,4,8,128]{3,0,2,1:T(8,128)}, u32[]{:S(2)}) copy-start(f32[48,4,8,128]{3,0,2,1:T(8,128)} %copy-done.1) | copy-start | bytes 2359300

commit v4 on v3

v4 whole, which is shorter than its diff:
```python
import math

import jax
import jax.numpy as jnp
from jax import lax
from jax.experimental import pallas as pl
from jax.experimental.pallas import tpu as pltpu
from jax.sharding import Mesh
from jax.sharding import PartitionSpec as P

VECS = 48
HI = lax.Precision.HIGHEST
FORWARD = [(0, 0, 1), (0, 1, 0), (0, 1, 1), (1, 0, 0), (1, 0, 1), (1, 1, 0), (1, 1, 1)]
VMEM = pltpu.VMEM


def dots(a, b, dims):
    return lax.dot_general(a, b, (dims, ((), ())), precision=HI, preferred_element_type=jnp.float32)


def eliminated(gram):
    order = gram.shape[0]
    third = order // 3
    rows = lax.broadcasted_iota(jnp.int32, gram.shape, 0)
    cols = lax.broadcasted_iota(jnp.int32, gram.shape, 1)
    inverse = jnp.where(rows == cols, 1.0, 0.0).astype(jnp.float32)
    place = lax.broadcasted_iota(jnp.int32, (third, 128), 0)
    done = []
    for j in range(3):
        left = gram[:third]
        right = inverse[:third]
        gram = gram[third:]
        inverse = inverse[third:]
        pivots = jnp.ones((third, 128), jnp.float32)
        for k in range(third):
            c = third * j + k
            column = jnp.broadcast_to(left[:, c : c + 1], (third, 128))
            pivot = column[k : k + 1, :]
            pivots = jnp.where(place == k, pivot, pivots)
            factor = jnp.where(place > k, column * (1.0 / pivot), 0.0)
            factor = jnp.concatenate([factor, factor], axis=1)
            left, right = (
                left - factor * left[k : k + 1, :],
                right - factor * right[k : k + 1, :],
            )
        scale = 1.0 / jnp.sqrt(pivots)
        scale = jnp.concatenate([scale, scale], axis=1)
        left = left * scale
        right = right * scale
        done.append(right)
        if j < 2:
            flipped = left.T[third * (j + 1) : order]
            gram = gram - dots(flipped, left, ((1,), (0,)))
            inverse = inverse - dots(flipped, right, ((1,), (0,)))
    return jnp.concatenate(done, axis=0)


def ritz_core(total):
    vecs = VECS
    order = 3 * vecs
    full = 4 * vecs
    rows = lax.broadcasted_iota(jnp.int32, total.shape, 0)
    cols = lax.broadcasted_iota(jnp.int32, total.shape, 1)
    flipped = total.T
    diagonal = total[full : full + 1, :]
    gram_k = jnp.where(rows <= cols, total, flipped)
    gram_m = jnp.where(rows > cols, total, jnp.where(rows == cols, diagonal, flipped))
    eye = rows == cols
    top = lambda g: jnp.sum(jnp.where(eye, g, 0.0)[:vecs], axis=1, keepdims=True)
    quotient = top(gram_k) / top(gram_m)

    def joined(g):
        mid = g[vecs : 2 * vecs] - quotient * g[2 * vecs : 3 * vecs]
        return jnp.concatenate([g[:vecs], mid, g[3 * vecs : full]], axis=0)

    gram_k = joined(joined(gram_k).T)
    gram_m = joined(joined(gram_m).T)
    gram_m = jnp.concatenate([gram_m, jnp.zeros((order, 256 - order), jnp.float32)], axis=1)
    inverse = eliminated(gram_m)[:, :order]
    half = dots(inverse, gram_k, ((1,), (0,)))
    reduced = dots(half, inverse, ((1,), (1,)))
    bound = jnp.max(jnp.sum(jnp.abs(reduced), axis=1, keepdims=True), axis=0, keepdims=True)
    eye = lax.broadcasted_iota(jnp.int32, (order, order), 0) == lax.broadcasted_iota(
        jnp.int32, (order, order), 1
    )
    shifted = jnp.where(eye, 1.0, 0.0) - reduced / bound
    filtered = dots(shifted[:vecs], shifted, ((1,), (0,)))
    return dots(filtered, inverse, ((1,), (0,))), quotient


def kuhn_tetrahedra():
    orders = [(0, 1, 2), (0, 2, 1), (1, 0, 2), (1, 2, 0), (2, 0, 1), (2, 1, 0)]
    tetrahedra = []
    for ordering in orders:
        corner = [0, 0, 0]
        corners = [(0, 0, 0)]
        for axis_step in ordering:
            corner[axis_step] = 1
            corners.append((corner[0], corner[1], corner[2]))
        tetrahedra.append(corners)
    return tetrahedra


def cross(p, q):
    return (
        p[1] * q[2] - p[2] * q[1],
        p[2] * q[0] - p[0] * q[2],
        p[0] * q[1] - p[1] * q[0],
    )


def dot3(p, q):
    return p[0] * q[0] + p[1] * q[1] + p[2] * q[2]


def shifted_lanes(x, step):
    return pltpu.roll(x, (-step) % x.shape[-1], x.ndim - 1)


def shifted_rows(x, step):
    return pltpu.roll(x, (-step) % x.shape[-2], x.ndim - 2)


def assemble_tables(off_ref, coef_ref, start_a, start_b, total_a, total_b):
    shape = (16, 128)
    row = lax.broadcasted_iota(jnp.int32, shape, 0)
    lane = lax.broadcasted_iota(jnp.int32, shape, 1)
    grid_b = start_b - 2 + row
    valid_bc = (grid_b >= 0) & (grid_b <= total_b - 2) & (row < 11) & (lane < 127)
    coef_ref[...] = jnp.zeros(coef_ref.shape, jnp.float32)

    def plane(a):
        grid_a = (start_a - 2 + a).astype(jnp.float32)
        base = [
            off_ref[0, a] + grid_a,
            off_ref[1, a] + grid_b.astype(jnp.float32),
            off_ref[2, a] + lane.astype(jnp.float32),
        ]
        out = {}
        for db in (0, 1):
            moved = [shifted_rows(p, db) if db else p for p in base]
            for dc in (0, 1):
                out[(db, dc)] = [shifted_lanes(p, dc) if dc else p for p in moved]
        return out

    def add(slot, a, value, b_shift, c_shift):
        if c_shift:
            value = shifted_lanes(value, -1)
        if b_shift == 0:
            value = shifted_rows(value, 1)
        coef_ref[slot, a] = coef_ref[slot, a] + value

    low = plane(0)
    for a in range(7):
        high = plane(a + 1)
        at = lambda corner: (high if corner[0] else low)[(corner[1], corner[2])]
        cell_a = start_a - 2 + a
        inside = valid_bc & (cell_a >= 0) & (cell_a <= total_a - 2)
        sums = {}
        for corners in kuhn_tetrahedra():
            anchor = at(corners[0])
            edges = [tuple(x - y for x, y in zip(at(c), anchor)) for c in corners[1:]]
            g1 = cross(edges[1], edges[2])
            g2 = cross(edges[2], edges[0])
            g3 = cross(edges[0], edges[1])
            g0 = tuple(-(x + y + z) for x, y, z in zip(g1, g2, g3))
            grads = [g0, g1, g2, g3]
            det = jnp.where(inside, jnp.abs(dot3(edges[0], g1)), 1.0)
            weight = jnp.where(inside, 1.0 / (6.0 * det), 0.0)
            for i in range(4):
                for j in range(i, 4):
                    step = tuple(q - p for p, q in zip(corners[i], corners[j]))
                    slot = 7 if i == j else FORWARD.index(step)
                    key = (slot, corners[i])
                    value = dot3(grads[i], grads[j]) * weight
                    sums[key] = sums[key] + value if key in sums else value
            part = jnp.where(inside, det * (1.0 / 24.0), 0.0)
            for corner in corners:
                key = (8, corner)
                sums[key] = sums[key] + part if key in sums else part
        for (slot, corner), value in sums.items():
            table_a = a + corner[0] - 1
            if 0 <= table_a <= 5:
                add(slot, table_a, value, corner[1], corner[2])
        low = high


def gram_kernel(start_ref, own_ref, down_a, up_a, down_b, up_b, c_pp, c_mm, c_pm, c_mp, off_own,
                gram_ref, uw_ref, off_ref, coef_ref, turn_ref, xb_ref, y_ref, acc_ref):
    v = VECS
    for i in range(3):
        for a in range(4):
            off_ref[i, 2 + a, 2:10] = off_own[i, a]
            off_ref[i, 2 + a, 10:12] = down_b[12, i * 8 + a * 2 : i * 8 + a * 2 + 2]
            off_ref[i, 2 + a, 0:2] = up_b[4, i * 8 + a * 2 : i * 8 + a * 2 + 2]
        for a in range(2):
            off_ref[i, 6 + a, 2:10] = down_a[24, i * 16 + a * 8 : i * 16 + a * 8 + 8]
            off_ref[i, a, 2:10] = up_a[8, i * 16 + a * 8 : i * 16 + a * 8 + 8]
            pair = slice(i * 4 + a * 2, i * 4 + a * 2 + 2)
            off_ref[i, 6 + a, 10:12] = c_pp[5, pair]
            off_ref[i, a, 0:2] = c_mm[1, pair]
            off_ref[i, 6 + a, 0:2] = c_pm[1, pair]
            off_ref[i, a, 10:12] = c_mp[1, pair]
    assemble_tables(off_ref, coef_ref, start_ref[0], start_ref[1], start_ref[2], start_ref[3])
    for slot, (da, db, dc) in enumerate(FORWARD):
        if dc:
            for a in range(6):
                turn_ref[slot, a] = shifted_lanes(coef_ref[slot, a], -1)

    def put(a, b, ref, i):
        xb_ref[a + 1, b + 1] = ref[i]

    for a in range(4):
        for b in range(8):
            xb_ref[a + 1, b + 1] = own_ref[a * 8 + b, :v]
            y_ref[a * 9 + b, 2 * v :] = own_ref[a * 8 + b, v:]
    for b in range(8):
        put(4, b, down_a, b)
        put(5, b, down_a, 8 + b)
        y_ref[4 * 9 + b, 2 * v :] = down_a[16 + b]
        put(-1, b, up_a, b)
    for a in range(4):
        put(a, 8, down_b, a * 2)
        put(a, 9, down_b, a * 2 + 1)
        y_ref[a * 9 + 8, 2 * v :] = down_b[8 + a]
        put(a, -1, up_b, a)
    for a in range(2):
        for b in range(2):
            put(4 + a, 8 + b, c_pp, a * 2 + b)
    y_ref[4 * 9 + 8, 2 * v :] = c_pp[4]
    put(-1, -1, c_mm, 0)
    put(4, -1, c_pm, 0)
    put(-1, 8, c_mp, 0)

    def row(ref, slot, a, b):
        return ref[slot, a, pl.ds(b, 1), :]

    def k_block(a, b):
        x = lambda i, j: xb_ref[a + 1 + i, b + 1 + j]
        total = x(0, 0) * row(coef_ref, 7, a + 1, b + 1)
        ahead = None
        behind = None
        for slot, (da, db, dc) in enumerate(FORWARD):
            front = x(da, db) * row(turn_ref if dc else coef_ref, slot, a + 1, b + 1)
            back = x(-da, -db) * row(coef_ref, slot, a + 1 - da, b + 1 - db)
            if dc:
                ahead = front if ahead is None else ahead + front
                behind = back if behind is None else behind + back
            else:
                total = total + front + back
        return total + shifted_lanes(ahead, 1) + shifted_lanes(behind, -1)

    def first(t, carry):
        a = t // 9
        b = t - a * 9
        kb = k_block(a, b)
        diagonal = row(coef_ref, 7, a + 1, b + 1)
        inverse = 1.0 / jnp.where(diagonal == 0.0, 1.0, diagonal)
        y_ref[t, :v] = kb * inverse
        y_ref[t, v : 2 * v] = xb_ref[a + 1, b + 1] * (row(coef_ref, 8, a + 1, b + 1) * inverse)
        return carry

    lax.fori_loop(0, 45, first, 0)

    acc_ref[...] = jnp.zeros(acc_ref.shape, jnp.float32)

    def sides(a, b):
        t = a * 9 + b
        block = xb_ref[a + 1, b + 1]
        y = y_ref[t]
        diagonal = row(coef_ref, 7, a + 1, b + 1)
        mass = row(coef_ref, 8, a + 1, b + 1)
        straight = y * (0.5 * diagonal)
        ahead = None
        for slot, (da, db, dc) in enumerate(FORWARD):
            front = y_ref[t + 9 * da + db] * row(turn_ref if dc else coef_ref, slot, a + 1, b + 1)
            if dc:
                ahead = front if ahead is None else ahead + front
            else:
                straight = straight + front
        ky = straight + shifted_lanes(ahead, 1)
        kb = y[:v] * diagonal
        basis = jnp.concatenate([block, y], axis=0)
        return basis, jnp.concatenate([kb, ky, basis * mass], axis=0)

    def second(t, carry):
        a = t // 4
        b = (t - a * 4) * 2
        x0, r0 = sides(a, b)
        x1, r1 = sides(a, b + 1)
        uw_ref[a * 8 + b] = x0[v : 3 * v]
        uw_ref[a * 8 + b + 1] = x1[v : 3 * v]
        left = jnp.concatenate([r0, r1], axis=1)
        right = jnp.concatenate([x0, x1], axis=1)
        acc_ref[...] += lax.dot_general(
            left, right, (((1,), (1,)), ((), ())), precision=HI,
            preferred_element_type=jnp.float32)
        return carry

    lax.fori_loop(0, 16, second, 0)

    n = 4 * v
    acc = acc_ref[...]
    pad = lambda g: jnp.concatenate(
        [jnp.concatenate([g, jnp.zeros((n, 256 - n), jnp.float32)], axis=1),
         jnp.zeros((256 - n, 256), jnp.float32)], axis=0)
    half = pad(acc[:n])
    gram_m = pad(acc[n:])
    rows = lax.broadcasted_iota(jnp.int32, (256, 256), 0)
    cols = lax.broadcasted_iota(jnp.int32, (256, 256), 1)
    gram_k = jnp.where(rows < v, half, half + half.T)
    diagonal = jnp.sum(jnp.where(rows == cols, gram_m, 0.0), axis=0, keepdims=True)
    square = jnp.where(rows <= cols, gram_k, gram_m)
    gram_ref[...] = jnp.where(rows < n, square, diagonal)


def gram_call(start, own, pieces, off):
    v = VECS
    spec = pl.BlockSpec(memory_space=VMEM)
    return pl.pallas_call(
        gram_kernel,
        out_shape=(
            jax.ShapeDtypeStruct((256, 256), jnp.float32),
            jax.ShapeDtypeStruct((32, 2 * v, 128), jnp.float32),
        ),
        in_specs=[pl.BlockSpec(memory_space=pltpu.SMEM)] + [spec] * (2 + len(pieces)),
        out_specs=(spec, spec),
        scratch_shapes=[
            VMEM((3, 8, 16, 128), jnp.float32),
            VMEM((9, 6, 16, 128), jnp.float32),
            VMEM((7, 6, 16, 128), jnp.float32),
            VMEM((7, 11, v, 128), jnp.float32),
            VMEM((45, 3 * v, 128), jnp.float32),
            VMEM((8 * v, 4 * v), jnp.float32),
        ],
        compiler_params=pltpu.CompilerParams(vmem_limit_bytes=48 * 2**20),
    )(start, own, *pieces, off)


def finish_kernel(scale, total_ref, own_hbm, uw_hbm, new_ref, search_ref, own_ref, uw_ref, sems):
    v = VECS
    copies = [
        pltpu.make_async_copy(own_hbm, own_ref, sems.at[0]),
        pltpu.make_async_copy(uw_hbm, uw_ref, sems.at[1]),
    ]
    for copy in copies:
        copy.start()
    coeffs, quotient = ritz_core(total_ref[...])
    coeffs = coeffs * scale
    quotient = jnp.broadcast_to(quotient, (v, 128))
    for copy in copies:
        copy.wait()
    for t in range(0, 32, 2):
        basis = []
        for i in (t, t + 1):
            search = uw_ref[i, :v] - quotient * uw_ref[i, v:]
            search_ref[pl.ds(i, v, stride=32), :] = search
            basis.append(jnp.concatenate([own_ref[i, :v], search, own_ref[i, v:]], axis=0))
        new = dots(coeffs, jnp.concatenate(basis, axis=1), ((1,), (0,)))
        new_ref[pl.ds(t, v, stride=32), :] = new[:, :128]
        new_ref[pl.ds(t + 1, v, stride=32), :] = new[:, 128:]


def finish_call(scale, total, own, uw):
    v = VECS
    vmem = pl.BlockSpec(memory_space=VMEM)
    hbm = pl.BlockSpec(memory_space=pl.ANY)
    out = jax.ShapeDtypeStruct((v * 32, 128), jnp.float32)
    return pl.pallas_call(
        lambda *refs: finish_kernel(scale, *refs),
        out_shape=(out, out),
        in_specs=[vmem, hbm, hbm],
        out_specs=(vmem, vmem),
        scratch_shapes=[
            VMEM((32, 2 * v, 128), jnp.float32),
            VMEM((32, 2 * v, 128), jnp.float32),
            pltpu.SemaphoreType.DMA((2,)),
        ],
        compiler_params=pltpu.CompilerParams(vmem_limit_bytes=48 * 2**20),
    )(total, own, uw)


def spread_sum(rows):
    plane = ("px", "pc")
    count = lax.axis_size("px") * lax.axis_size("pc")
    depth = lax.axis_size("pz")
    pieces = rows.reshape(count, -1, rows.shape[1])
    part = jnp.sum(lax.all_to_all(pieces, plane, 0, 0), axis=0)
    part = jnp.sum(
        lax.all_to_all(jnp.broadcast_to(part[None], (depth,) + part.shape), "pz", 0, 0), axis=0
    )
    whole = lax.all_to_all(jnp.broadcast_to(part[None], (count,) + part.shape), plane, 0, 0)
    return whole.reshape(rows.shape)


def neighbour(payload, step_a, step_b):
    count_a = lax.axis_size("px")
    count_b = lax.axis_size("pz") * lax.axis_size("pc")
    pairs = []
    for a in range(count_a):
        for b in range(count_b):
            if 0 <= a + step_a < count_a and 0 <= b + step_b < count_b:
                pairs.append(((a + step_a) * count_b + b + step_b, a * count_b + b))
    return lax.ppermute(payload, ("px", "pz", "pc"), pairs)


def shards(offsets, block, prior):
    v = block.shape[0]
    rows_a, rows_b, depth = block.shape[1:]
    total_a = rows_a * lax.axis_size("px")
    total_b = rows_b * lax.axis_size("pz") * lax.axis_size("pc")
    start = jnp.stack(
        [
            lax.axis_index("px") * rows_a,
            lax.axis_index(("pz", "pc")) * rows_b,
            jnp.int32(total_a),
            jnp.int32(total_b),
        ]
    ).astype(jnp.int32)
    own = jnp.concatenate([block, prior]).transpose(1, 2, 0, 3)

    def payload(b_a, b_b, p_a, p_b, o_a, o_b):
        parts = [own[b_a, b_b, :v].reshape(-1, v, depth)]
        if p_a is not None:
            parts.append(own[p_a, p_b, v:].reshape(-1, v, depth))
        rows = offsets[:, o_a, o_b].reshape(-1, depth)
        parts.append(jnp.pad(rows, ((0, v - rows.shape[0]), (0, 0)))[None])
        return jnp.concatenate(parts)

    low, high, every = slice(0, 2), slice(-2, None), slice(None)
    first, last = slice(0, 1), slice(-1, None)
    down_a = neighbour(payload(low, every, first, every, low, every), 1, 0)
    up_a = neighbour(payload(last, every, None, None, high, every), -1, 0)
    down_b = neighbour(payload(every, low, every, first, every, low), 0, 1)
    up_b = neighbour(payload(every, last, None, None, every, high), 0, -1)
    c_pp = neighbour(payload(low, low, first, first, low, low), 1, 1)
    c_mm = neighbour(payload(last, last, None, None, high, high), -1, -1)
    c_pm = neighbour(payload(first, last, None, None, low, high), 1, -1)
    c_mp = neighbour(payload(last, first, None, None, high, low), -1, 1)
    own = own.reshape(rows_a * rows_b, 2 * v, depth)
    pieces = (down_a, up_a, down_b, up_b, c_pp, c_mm, c_pm, c_mp)
    gram, uw = gram_call(start, own, pieces, offsets)
    scale = math.sqrt(total_a * total_b * depth)
    new_block, search = finish_call(scale, spread_sum(gram), own, uw)
    return (new_block.reshape(block.shape), search.reshape(block.shape))


def solution(mesh):
    grid = Mesh(
        mesh.devices.reshape(mesh.shape["px"], mesh.shape["py"] // 2, 2), ("px", "pz", "pc")
    )
    spec = P(None, "px", ("pz", "pc"), None)
    return jax.shard_map(
        shards, mesh=grid, in_specs=(spec, spec, spec), out_specs=(spec, spec), check_vma=False
    )
```

time: 170 us -> 146 us (0.86); the launches traced: 167 us -> 145 us
  other arithmetic: 42.4 us -> 4.34 us
  Pallas kernels: 14.3 us -> 32.9 us
  matrix products: 8.28 us -> 0 us
  blocking collectives: 59.2 us -> 66.1 us
  local copies, waits for them, and re-layouts: 10.6 us -> 14 us
  waiting for transfers between devices: 4.77 us -> 2.1 us
    reduce_sum x10 -> x0, other arithmetic: 23.4 us -> none  [the longest x9 22.9 us: assemble(): entry_value = jnp.sum(gradients[first] * gradients[second], axis=0) * weight]
    pallas_call x1 -> x2, Pallas kernels: 14.3 us -> 32.9 us  [the longest x1 17.7 us: finish_call(): pl.pallas_call(lambda *refs: finish_kernel(scale, *refs), out_shape=(out,...]
    dot_general x3 -> x0, matrix products: 8.28 us -> none  [the longest x1 2.88 us: local_grams(): lax.dot_general(flat, m_flat, (((1,), (1,)), ((), ())), precision=lax.Pre...]
    add x15 -> x0, other arithmetic: 8.02 us -> none  [the longest x1 5.72 us: stiffness_apply(): result + coefs[position] * padded[:, 1 + shift_key[0]:1 + shift_key[0] +...]
    div x2 -> x0, other arithmetic: 4.72 us -> none  [the longest x1 4.37 us: shards(): u_wide = k_wide / diagonal]
    unnamed x16 -> x33, local copies, waits for them, and re-layouts: 8.07 us -> 12.4 us
    all_to_all x1, blocking collectives: 16 us -> 19.8 us  [spread_sum(): part = jnp.sum(lax.all_to_all(pieces, plane, 0, 0), axis=0)]
    sub x13 -> x0, other arithmetic: 3.43 us -> none  [the longest x1 1.29 us: shards(): search = u_part - quotient[:, :1, None, None] * w_part]
  transfers between devices with their start and end apart: 8 -> 8, of which waited for: 2 -> 1; matrix products, arithmetic and copies ran while one was open for 24% -> 3% of each run, Pallas kernels for 0% -> 0%
where the time goes in v4:
time: 146 us; the launch traced here: 145 us
  blocking collectives  66.1 us (45%)
  Pallas kernels  32.9 us (23%)
  starting transfers between devices  24.7 us (17%)
  local copies, waits for them, and re-layouts  14 us (10%)
  other arithmetic  4.34 us (3%)
  waiting for transfers between devices  2.1 us (1%)
    all_to_all x1, blocking collectives, spread_sum(): lax.all_to_all(jnp.broadcast_to(part[None], (depth,) + part.shape), 'pz',...  31.2 us
    ppermute x8, starting transfers between devices, neighbour(): return lax.ppermute(payload, ('px', 'pz', 'pc'), pairs)  24.7 us
    all_to_all x1, blocking collectives, spread_sum(): part = jnp.sum(lax.all_to_all(pieces, plane, 0, 0), axis=0)  19.8 us
    pallas_call x1, Pallas kernels, finish_call(): pl.pallas_call(lambda *refs: finish_kernel(scale, *refs), out_shape=(out,...  17.7 us
    all_to_all x1, blocking collectives, spread_sum(): lax.all_to_all(jnp.broadcast_to(part[None], (count,) + part.shape), plane...  15.1 us
    pallas_call x1, Pallas kernels, gram_call(): pl.pallas_call(gram_kernel, out_shape=(jax.ShapeDtypeStruct((256, 256), j...  15.1 us
    unnamed x33, local copies, waits for them, and re-layouts  12.4 us
    concatenate x8, other arithmetic, payload(): return jnp.concatenate(parts)  4.21 us
  transfers between devices with their start and end apart: 8, of which 1 were waited for; matrix products, arithmetic and copies ran while one was open for 3% of the time, Pallas kernels for 0%

profile of v4, /device:TPU:1, one launch (start us, length us, event | category | flops | bytes accessed | tf_op | source)
XLA Modules:
  0.0 145.0 jit_solution(14609434941541839283)
XLA Ops:
  0.6 0.9 fusion
  1.6 1.6 %copy_dynamic-update-slice_fusion.1 = f32[96,4,8,128]{3,0,2,1:T(8,128)S(1)} fusion(f32[48,4,8,128]{3,2,1,0:T(8,128)} %param.4), kind=kLoop, calls=%fused_computation.1 | loop fusion | bytes 1572864
  3.7 5.9 %collective-permute-start.5 = (f32[2,48,128]{2,1,0:T(8,128)S(1)}, f32[2,48,128]{2,1,0:T(8,128)S(1)}, u32[]{:S(2)}, u32[]{:S(2)}) collective-permute-start(f32[2,48,128]{2,1,0:T(8,128)S(1)} %pad_maximum_fusion.5), channel_id=1, source_target_pairs={{0,33},{1,34},{2,35},{3,36},{4,37},{5,38},{6,39},{7,40},{8,41},{9,... | collective-permute-start | bytes 147464 | tf_op jit(solution)/shard_map/ppermute | solution.py:404
  10.2 1.3 collective-permute-start.6
  12.1 4.3 %collective-permute-start.7 = (f32[2,48,128]{2,1,0:T(8,128)}, f32[2,48,128]{2,1,0:T(8,128)S(1)}, u32[]{:S(2)}, u32[]{:S(2)}) collective-permute-start(f32[2,48,128]{2,1,0:T(8,128)} %pad_maximum_fusion.7), channel_id=1, source_target_pairs={{1,32},{2,33},{3,34},{4,35},{5,36},{6,37},{7,38},{8,39},{9,40},{10... | collective-permute-start | bytes 147464 | tf_op jit(solution)/shard_map/ppermute | solution.py:404
  17.2 1.9 %collective-permute-start.2 = (f32[13,48,128]{2,1,0:T(8,128)}, f32[13,48,128]{2,1,0:T(8,128)S(1)}, u32[]{:S(2)}, u32[]{:S(2)}) collective-permute-start(f32[13,48,128]{2,1,0:T(8,128)} %pad_maximum_fusion.1), channel_id=1, source_target_pairs={{1,0},{2,1},{3,2},{4,3},{5,4},{6,5},{7,6},{8,7},{9,8},{10,9},{11,1... | collective-permute-start | bytes 958472 | tf_op jit(solution)/shard_map/ppermute | solution.py:404
  19.2 0.9 pad_maximum_fusion
  20.1 1.3 collective-permute-start
  22.7 1.3 collective-permute-start.4
  24.6 4.6 %collective-permute-start.1 = (f32[9,48,128]{2,1,0:T(8,128)S(1)}, f32[9,48,128]{2,1,0:T(8,128)S(1)}, u32[]{:S(2)}, u32[]{:S(2)}) collective-permute-start(f32[9,48,128]{2,1,0:T(8,128)S(1)} %pad_maximum_fusion.2), channel_id=1, source_target_pairs={{0,32},{1,33},{2,34},{3,35},{4,36},{5,37},{6,38},{7,39},{8,40},{9,... | collective-permute-start | bytes 663560 | tf_op jit(solution)/shard_map/ppermute | solution.py:404
  30.6 4.2 %collective-permute-start.3 = (f32[5,48,128]{2,1,0:T(8,128)}, f32[5,48,128]{2,1,0:T(8,128)S(1)}, u32[]{:S(2)}, u32[]{:S(2)}) collective-permute-start(f32[5,48,128]{2,1,0:T(8,128)} %pad_maximum_fusion.4), channel_id=1, source_target_pairs={{0,1},{1,2},{2,3},{3,4},{4,5},{5,6},{6,7},{7,8},{8,9},{9,10},{10,1... | collective-permute-start | bytes 368648 | tf_op jit(solution)/shard_map/ppermute | solution.py:404
  34.8 2.1 %collective-permute-done.3.up_b = f32[5,48,128]{2,1,0:T(8,128)S(1)} collective-permute-done((f32[5,48,128]{2,1,0:T(8,128)}, f32[5,48,128]{2,1,0:T(8,128)S(1)}, u32[]{:S(2)}, u32[]{:S(2)}) %collective-permute-start.3) | collective-permute-done | bytes 122912 | tf_op jit(solution)/shard_map/ppermute | solution.py:404
  38.9 0.8 copy-done
  39.7 1.1 copy-done.1
  40.8 0.9 copy-done.4
  41.7 0.9 copy-done.6
  42.7 0.9 copy-done.8
  44.4 0.8 copy-done.12
  45.2 0.8 copy-done.14
  46.0 15.1 %shard_map.50 = (f32[256,256]{1,0:T(8,128)S(1)}, f32[32,96,128]{2,1,0:T(8,128)S(1)}) custom-call(s32[4]{0:T(128)S(1)} %pad_add_fusion.start_ref, f32[32,96,128]{2,1,0:T(8,128)S(1)} %bitcast.50, f32[25,48,128]{2,1,0:T(8,128)S(1)} %copy-done.1, f32[9,48,128]{2,1,0:T(8,128)S(1)} %copy-done.4, f32[13,48,128]{2,1,0:T(8,128)S(1)} %collective-permute-done.2.down_b, ...), custom_call_target="tpu_custom_call" | custom-call | tf_op jit(solution)/shard_map/pallas_call | solution.py:320
  61.1 19.8 %all_to_all.15 = f32[32,8,256]{2,1,0:T(8,128)S(1)} all-to-all(f32[32,8,256]{2,1,0:T(8,128)S(1)} %bitcast.53), channel_id=1, replica_groups=mesh['px'=16,'pz'=16,'pc'=2] {'px','pc'}, dimensions={0} | all-to-all | bytes 524288 | tf_op jit(solution)/shard_map/all_to_all | solution.py:388
  80.9 31.2 %all_to_all.16 = f32[16,8,256]{2,1,0:T(8,128)S(1)} all-to-all(f32[16,8,256]{2,1,0:T(8,128)S(1)} %broadcast_in_dim.44), channel_id=1, replica_groups=mesh['px'=16,'pz'=16,'pc'=2] {'pz'}, dimensions={0} | all-to-all | bytes 262144 | tf_op jit(solution)/shard_map/all_to_all | solution.py:390
  112.2 15.1 %all_to_all.17 = f32[32,8,256]{2,1,0:T(8,128)S(1)} all-to-all(f32[32,8,256]{2,1,0:T(8,128)S(1)} %broadcast_in_dim.45), channel_id=1, replica_groups=mesh['px'=16,'pz'=16,'pc'=2] {'px','pc'}, dimensions={0} | all-to-all | bytes 524288 | tf_op jit(solution)/shard_map/all_to_all | solution.py:392
  127.3 17.7 %shard_map.51 = (f32[1536,128]{1,0:T(8,128)}, f32[1536,128]{1,0:T(8,128)}) custom-call(f32[256,256]{1,0:T(8,128)S(1)} %bitcast.52, f32[32,96,128]{2,1,0:T(8,128)S(1)} %bitcast.51, f32[32,96,128]{2,1,0:T(8,128)S(1)} %get-tuple-element.7.refs_2_), custom_call_target="tpu_custom_call" | custom-call | tf_op jit(solution)/shard_map/pallas_call | solution.py:369
  (63 shorter events, 8.8 us)
Async XLA Ops:
  0.6 2.5 %copy-start.15 = (f32[48,4,8,128]{3,2,1,0:T(8,128)S(1)}, f32[48,4,8,128]{3,2,1,0:T(8,128)}, u32[]{:S(2)}) copy-start(f32[48,4,8,128]{3,2,1,0:T(8,128)} %param.5) | copy-start | bytes 2359300
  1.5 14.8 %copy-start.2 = (f32[3,4,8,128]{3,2,1,0:T(8,128)S(1)}, f32[3,4,8,128]{3,2,1,0:T(8,128)}, u32[]{:S(2)}) copy-start(f32[3,4,8,128]{3,2,1,0:T(8,128)} %off_own.1) | copy-start | bytes 147460
  3.7 18.4 %collective-permute-start.5 = (f32[2,48,128]{2,1,0:T(8,128)S(1)}, f32[2,48,128]{2,1,0:T(8,128)S(1)}, u32[]{:S(2)}, u32[]{:S(2)}) collective-permute-start(f32[2,48,128]{2,1,0:T(8,128)S(1)} %pad_maximum_fusion.5), channel_id=1, source_target_pairs={{0,33},{1,34},{2,35},{3,36},{4,37},{5,38},{6,39},{7,40},{8,41},{9,... | collective-permute-start | bytes 147464 | tf_op jit(solution)/shard_map/ppermute | solution.py:404
  10.2 13.8 %collective-permute-start.6 = (f32[2,48,128]{2,1,0:T(8,128)}, f32[2,48,128]{2,1,0:T(8,128)S(1)}, u32[]{:S(2)}, u32[]{:S(2)}) collective-permute-start(f32[2,48,128]{2,1,0:T(8,128)} %pad_maximum_fusion.6), channel_id=1, source_target_pairs={{32,1},{33,2},{34,3},{35,4},{36,5},{37,6},{38,7},{39,8},{40,9},{41... | collective-permute-start | bytes 147464 | tf_op jit(solution)/shard_map/ppermute | solution.py:404
  12.1 17.8 %collective-permute-start.7 = (f32[2,48,128]{2,1,0:T(8,128)}, f32[2,48,128]{2,1,0:T(8,128)S(1)}, u32[]{:S(2)}, u32[]{:S(2)}) collective-permute-start(f32[2,48,128]{2,1,0:T(8,128)} %pad_maximum_fusion.7), channel_id=1, source_target_pairs={{1,32},{2,33},{3,34},{4,35},{5,36},{6,37},{7,38},{8,39},{9,40},{10... | collective-permute-start | bytes 147464 | tf_op jit(solution)/shard_map/ppermute | solution.py:404
  17.2 21.7 %collective-permute-start.2 = (f32[13,48,128]{2,1,0:T(8,128)}, f32[13,48,128]{2,1,0:T(8,128)S(1)}, u32[]{:S(2)}, u32[]{:S(2)}) collective-permute-start(f32[13,48,128]{2,1,0:T(8,128)} %pad_maximum_fusion.1), channel_id=1, source_target_pairs={{1,0},{2,1},{3,2},{4,3},{5,4},{6,5},{7,6},{8,7},{9,8},{10,9},{11,1... | collective-permute-start | bytes 958472 | tf_op jit(solution)/shard_map/ppermute | solution.py:404
  20.1 18.8 %collective-permute-start = (f32[25,48,128]{2,1,0:T(8,128)}, f32[25,48,128]{2,1,0:T(8,128)S(1)}, u32[]{:S(2)}, u32[]{:S(2)}) collective-permute-start(f32[25,48,128]{2,1,0:T(8,128)} %pad_maximum_fusion), channel_id=1, source_target_pairs={{32,0},{33,1},{34,2},{35,3},{36,4},{37,5},{38,6},{39,7},{40,8},{41... | collective-permute-start | bytes 1843208 | tf_op jit(solution)/shard_map/ppermute | solution.py:404
  22.1 0.6 copy-start.9
  22.7 14.8 %collective-permute-start.4 = (f32[6,48,128]{2,1,0:T(8,128)}, f32[6,48,128]{2,1,0:T(8,128)S(1)}, u32[]{:S(2)}, u32[]{:S(2)}) collective-permute-start(f32[6,48,128]{2,1,0:T(8,128)} %pad_maximum_fusion.3), channel_id=1, source_target_pairs={{33,0},{34,1},{35,2},{36,3},{37,4},{38,5},{39,6},{40,7},{41,8},{42... | collective-permute-start | bytes 442376 | tf_op jit(solution)/shard_map/ppermute | solution.py:404
  24.0 0.6 copy-start.11
  24.6 13.6 %collective-permute-start.1 = (f32[9,48,128]{2,1,0:T(8,128)S(1)}, f32[9,48,128]{2,1,0:T(8,128)S(1)}, u32[]{:S(2)}, u32[]{:S(2)}) collective-permute-start(f32[9,48,128]{2,1,0:T(8,128)S(1)} %pad_maximum_fusion.2), channel_id=1, source_target_pairs={{0,32},{1,33},{2,34},{3,35},{4,36},{5,37},{6,38},{7,39},{8,40},{9,... | collective-permute-start | bytes 663560 | tf_op jit(solution)/shard_map/ppermute | solution.py:404
  30.0 0.6 copy-start.13
  30.6 6.3 %collective-permute-start.3 = (f32[5,48,128]{2,1,0:T(8,128)}, f32[5,48,128]{2,1,0:T(8,128)S(1)}, u32[]{:S(2)}, u32[]{:S(2)}) collective-permute-start(f32[5,48,128]{2,1,0:T(8,128)} %pad_maximum_fusion.4), channel_id=1, source_target_pairs={{0,1},{1,2},{2,3},{3,4},{4,5},{5,6},{6,7},{7,8},{8,9},{9,10},{10,1... | collective-permute-start | bytes 368648 | tf_op jit(solution)/shard_map/ppermute | solution.py:404
  36.9 0.7 copy-start.7
  37.6 0.7 copy-start.5
  38.2 0.7 copy-start.3
  38.9 0.8 copy-start
  39.7 1.1 copy-start.1
  40.8 0.9 copy-start.4
  41.7 0.9 copy-start.6
  42.7 0.9 copy-start.8
  43.6 0.8 copy-start.10
  44.4 0.8 copy-start.12
  45.2 0.8 copy-start.14

commit v5 on v4

--- a/solution.py
+++ b/solution.py
@@ -185,52 +185,119 @@
         low = high
 
 
-def gram_kernel(start_ref, own_ref, down_a, up_a, down_b, up_b, c_pp, c_mm, c_pm, c_mp, off_own,
-                gram_ref, uw_ref, off_ref, coef_ref, turn_ref, xb_ref, y_ref, acc_ref):
+def pack_kernel(block_ref, prior_ref, off_ref, own, down_a, up_a, down_b, up_b, c_pp, c_mm, c_pm, c_mp):
     v = VECS
+    block = lambda a, b: block_ref[pl.ds(a * 8 + b, v, stride=32), :]
+    prior = lambda a, b: prior_ref[pl.ds(a * 8 + b, v, stride=32), :]
+    for a in range(4):
+        for b in range(8):
+            x = block(a, b)
+            y = prior(a, b)
+            own[a, b, :v] = x
+            own[a, b, v:] = y
+            if a < 2:
+                down_a[a * 8 + b] = x
+            if a == 0:
+                down_a[16 + b] = y
+            if a == 3:
+                up_a[b] = x
+            if b < 2:
+                down_b[b * 4 + a] = x
+            if b == 0:
+                down_b[8 + a] = y
+            if b == 7:
+                up_b[a] = x
+            if a < 2 and b < 2:
+                c_pp[a * 2 + b] = x
+            if a == 0 and b == 0:
+                c_pp[4] = y
+            if a == 3 and b == 7:
+                c_mm[0] = x
+            if a == 0 and b == 7:
+                c_pm[0] = x
+            if a == 3 and b == 0:
+                c_mp[0] = x
+    for i in range(3):
+        for a in range(4):
+            down_b[12, i * 8 + a * 2 : i * 8 + a * 2 + 2] = off_ref[i, a, 0:2]
+            up_b[4, i * 8 + a * 2 : i * 8 + a * 2 + 2] = off_ref[i, a, 6:8]
+        for a in range(2):
+            down_a[24, i * 16 + a * 8 : i * 16 + a * 8 + 8] = off_ref[i, a]
+            up_a[8, i * 16 + a * 8 : i * 16 + a * 8 + 8] = off_ref[i, 2 + a]
+            pair = slice(i * 4 + a * 2, i * 4 + a * 2 + 2)
+            c_pp[5, pair] = off_ref[i, a, 0:2]
+            c_mm[1, pair] = off_ref[i, 2 + a, 6:8]
+            c_pm[1, pair] = off_ref[i, a, 6:8]
+            c_mp[1, pair] = off_ref[i, 2 + a, 0:2]
+
+
+def pack_call(block, prior, offsets):
+    v = VECS
+    vmem = pl.BlockSpec(memory_space=VMEM)
+    sizes = [(4, 8, 2 * v, 128)] + [(n, v, 128) for n in (25, 9, 13, 5, 6, 2, 2, 2)]
+    return pl.pallas_call(
+        pack_kernel,
+        out_shape=tuple(jax.ShapeDtypeStruct(s, jnp.float32) for s in sizes),
+        in_specs=[vmem] * 3,
+        out_specs=(vmem,) * len(sizes),
+        compiler_params=pltpu.CompilerParams(vmem_limit_bytes=60 * 2**20),
+    )(block.reshape(-1, 128), prior.reshape(-1, 128), offsets)
+
+
+def gram_kernel(start_ref, own, down_a, up_a, down_b, up_b, c_pp, c_mm, c_pm, c_mp, off_own,
+                gram_ref, uw_ref, edge_ref, off_ref, coef_ref, turn_ref, xb_ref, y_ref, acc_ref,
+                sems):
+    v = VECS
+    moves = [
+        (piece.at[piece.shape[0] - 1], edge_ref.at[i])
+        for i, piece in enumerate((down_a, up_a, down_b, up_b, c_pp, c_mm, c_pm, c_mp))
+    ]
+    third = slice(2 * v, 3 * v)
+    moves += [
+        (own.at[:, :, :v], xb_ref.at[1:5, 1:9]),
+        (down_a.at[0:8], xb_ref.at[5, 1:9]),
+        (down_a.at[8:16], xb_ref.at[6, 1:9]),
+        (up_a.at[0:8], xb_ref.at[0, 1:9]),
+        (down_b.at[0:4], xb_ref.at[1:5, 9]),
+        (down_b.at[4:8], xb_ref.at[1:5, 10]),
+        (up_b.at[0:4], xb_ref.at[1:5, 0]),
+        (c_pp.at[0:2], xb_ref.at[5, 9:11]),
+        (c_pp.at[2:4], xb_ref.at[6, 9:11]),
+        (c_mm.at[0], xb_ref.at[0, 0]),
+        (c_pm.at[0], xb_ref.at[5, 0]),
+        (c_mp.at[0], xb_ref.at[0, 9]),
+        (own.at[:, :, v:], y_ref.at[0:4, 0:8, third]),
+        (down_a.at[16:24], y_ref.at[4, 0:8, third]),
+        (down_b.at[8:12], y_ref.at[0:4, 8, third]),
+        (c_pp.at[4], y_ref.at[4, 8, third]),
+    ]
+    copies = [pltpu.make_async_copy(x, y, sems.at[i]) for i, (x, y) in enumerate(moves)]
+    for copy in copies:
+        copy.start()
+    for copy in copies[:8]:
+        copy.wait()
     for i in range(3):
         for a in range(4):
             off_ref[i, 2 + a, 2:10] = off_own[i, a]
-            off_ref[i, 2 + a, 10:12] = down_b[12, i * 8 + a * 2 : i * 8 + a * 2 + 2]
-            off_ref[i, 2 + a, 0:2] = up_b[4, i * 8 + a * 2 : i * 8 + a * 2 + 2]
+            pair = slice(i * 8 + a * 2, i * 8 + a * 2 + 2)
+            off_ref[i, 2 + a, 10:12] = edge_ref[2, pair]
+            off_ref[i, 2 + a, 0:2] = edge_ref[3, pair]
         for a in range(2):
-            off_ref[i, 6 + a, 2:10] = down_a[24, i * 16 + a * 8 : i * 16 + a * 8 + 8]
-            off_ref[i, a, 2:10] = up_a[8, i * 16 + a * 8 : i * 16 + a * 8 + 8]
+            rows = slice(i * 16 + a * 8, i * 16 + a * 8 + 8)
+            off_ref[i, 6 + a, 2:10] = edge_ref[0, rows]
+            off_ref[i, a, 2:10] = edge_ref[1, rows]
             pair = slice(i * 4 + a * 2, i * 4 + a * 2 + 2)
-            off_ref[i, 6 + a, 10:12] = c_pp[5, pair]
-            off_ref[i, a, 0:2] = c_mm[1, pair]
-            off_ref[i, 6 + a, 0:2] = c_pm[1, pair]
-            off_ref[i, a, 10:12] = c_mp[1, pair]
+            off_ref[i, 6 + a, 10:12] = edge_ref[4, pair]
+            off_ref[i, a, 0:2] = edge_ref[5, pair]
+            off_ref[i, 6 + a, 0:2] = edge_ref[6, pair]
+            off_ref[i, a, 10:12] = edge_ref[7, pair]
     assemble_tables(off_ref, coef_ref, start_ref[0], start_ref[1], start_ref[2], start_ref[3])
     for slot, (da, db, dc) in enumerate(FORWARD):
         if dc:
             for a in range(6):
                 turn_ref[slot, a] = shifted_lanes(coef_ref[slot, a], -1)
-
-    def put(a, b, ref, i):
-        xb_ref[a + 1, b + 1] = ref[i]
-
-    for a in range(4):
-        for b in range(8):
-            xb_ref[a + 1, b + 1] = own_ref[a * 8 + b, :v]
-            y_ref[a * 9 + b, 2 * v :] = own_ref[a * 8 + b, v:]
-    for b in range(8):
-        put(4, b, down_a, b)
-        put(5, b, down_a, 8 + b)
-        y_ref[4 * 9 + b, 2 * v :] = down_a[16 + b]
-        put(-1, b, up_a, b)
-    for a in range(4):
-        put(a, 8, down_b, a * 2)
-        put(a, 9, down_b, a * 2 + 1)
-        y_ref[a * 9 + 8, 2 * v :] = down_b[8 + a]
-        put(a, -1, up_b, a)
-    for a in range(2):
-        for b in range(2):
-            put(4 + a, 8 + b, c_pp, a * 2 + b)
-    y_ref[4 * 9 + 8, 2 * v :] = c_pp[4]
-    put(-1, -1, c_mm, 0)
-    put(4, -1, c_pm, 0)
-    put(-1, 8, c_mp, 0)
+    for copy in copies[8:]:
+        copy.wait()
 
     def row(ref, slot, a, b):
         return ref[slot, a, pl.ds(b, 1), :]
@@ -256,8 +323,8 @@
         kb = k_block(a, b)
         diagonal = row(coef_ref, 7, a + 1, b + 1)
         inverse = 1.0 / jnp.where(diagonal == 0.0, 1.0, diagonal)
-        y_ref[t, :v] = kb * inverse
-        y_ref[t, v : 2 * v] = xb_ref[a + 1, b + 1] * (row(coef_ref, 8, a + 1, b + 1) * inverse)
+        y_ref[a, b, :v] = kb * inverse
+        y_ref[a, b, v : 2 * v] = xb_ref[a + 1, b + 1] * (row(coef_ref, 8, a + 1, b + 1) * inverse)
         return carry
 
     lax.fori_loop(0, 45, first, 0)
@@ -265,15 +332,14 @@
     acc_ref[...] = jnp.zeros(acc_ref.shape, jnp.float32)
 
     def sides(a, b):
-        t = a * 9 + b
         block = xb_ref[a + 1, b + 1]
-        y = y_ref[t]
+        y = y_ref[a, b]
         diagonal = row(coef_ref, 7, a + 1, b + 1)
         mass = row(coef_ref, 8, a + 1, b + 1)
         straight = y * (0.5 * diagonal)
         ahead = None
         for slot, (da, db, dc) in enumerate(FORWARD):
-            front = y_ref[t + 9 * da + db] * row(turn_ref if dc else coef_ref, slot, a + 1, b + 1)
+            front = y_ref[a + da, b + db] * row(turn_ref if dc else coef_ref, slot, a + 1, b + 1)
             if dc:
                 ahead = front if ahead is None else ahead + front
             else:
@@ -323,17 +389,21 @@
             jax.ShapeDtypeStruct((256, 256), jnp.float32),
             jax.ShapeDtypeStruct((32, 2 * v, 128), jnp.float32),
         ),
-        in_specs=[pl.BlockSpec(memory_space=pltpu.SMEM)] + [spec] * (2 + len(pieces)),
+        in_specs=[pl.BlockSpec(memory_space=pltpu.SMEM)]
+        + [pl.BlockSpec(memory_space=pl.ANY)] * (1 + len(pieces))
+        + [spec],
         out_specs=(spec, spec),
         scratch_shapes=[
+            VMEM((8, v, 128), jnp.float32),
             VMEM((3, 8, 16, 128), jnp.float32),
             VMEM((9, 6, 16, 128), jnp.float32),
             VMEM((7, 6, 16, 128), jnp.float32),
             VMEM((7, 11, v, 128), jnp.float32),
-            VMEM((45, 3 * v, 128), jnp.float32),
+            VMEM((5, 9, 3 * v, 128), jnp.float32),
             VMEM((8 * v, 4 * v), jnp.float32),
+            pltpu.SemaphoreType.DMA((24,)),
         ],
-        compiler_params=pltpu.CompilerParams(vmem_limit_bytes=48 * 2**20),
+        compiler_params=pltpu.CompilerParams(vmem_limit_bytes=12 * 2**20),
     )(start, own, *pieces, off)
 
 
@@ -376,7 +446,7 @@
             VMEM((32, 2 * v, 128), jnp.float32),
             pltpu.SemaphoreType.DMA((2,)),
         ],
-        compiler_params=pltpu.CompilerParams(vmem_limit_bytes=48 * 2**20),
+        compiler_params=pltpu.CompilerParams(vmem_limit_bytes=12 * 2**20),
     )(total, own, uw)
 
 
@@ -417,29 +487,19 @@
             jnp.int32(total_b),
         ]
     ).astype(jnp.int32)
-    own = jnp.concatenate([block, prior]).transpose(1, 2, 0, 3)
-
-    def payload(b_a, b_b, p_a, p_b, o_a, o_b):
-        parts = [own[b_a, b_b, :v].reshape(-1, v, depth)]
-        if p_a is not None:
-            parts.append(own[p_a, p_b, v:].reshape(-1, v, depth))
-        rows = offsets[:, o_a, o_b].reshape(-1, depth)
-        parts.append(jnp.pad(rows, ((0, v - rows.shape[0]), (0, 0)))[None])
-        return jnp.concatenate(parts)
-
-    low, high, every = slice(0, 2), slice(-2, None), slice(None)
-    first, last = slice(0, 1), slice(-1, None)
-    down_a = neighbour(payload(low, every, first, every, low, every), 1, 0)
-    up_a = neighbour(payload(last, every, None, None, high, every), -1, 0)
-    down_b = neighbour(payload(every, low, every, first, every, low), 0, 1)
-    up_b = neighbour(payload(every, last, None, None, every, high), 0, -1)
-    c_pp = neighbour(payload(low, low, first, first, low, low), 1, 1)
-    c_mm = neighbour(payload(last, last, None, None, high, high), -1, -1)
-    c_pm = neighbour(payload(first, last, None, None, low, high), 1, -1)
-    c_mp = neighbour(payload(last, first, None, None, high, low), -1, 1)
+    own, down_a, up_a, down_b, up_b, c_pp, c_mm, c_pm, c_mp = pack_call(block, prior, offsets)
+    pieces = (
+        neighbour(down_a, 1, 0),
+        neighbour(up_a, -1, 0),
+        neighbour(down_b, 0, 1),
+        neighbour(up_b, 0, -1),
+        neighbour(c_pp, 1, 1),
+        neighbour(c_mm, -1, -1),
+        neighbour(c_pm, 1, -1),
+        neighbour(c_mp, -1, 1),
+    )
+    gram, uw = gram_call(start, own, pieces, offsets)
     own = own.reshape(rows_a * rows_b, 2 * v, depth)
-    pieces = (down_a, up_a, down_b, up_b, c_pp, c_mm, c_pm, c_mp)
-    gram, uw = gram_call(start, own, pieces, offsets)
     scale = math.sqrt(total_a * total_b * depth)
     new_block, search = finish_call(scale, spread_sum(gram), own, uw)
     return (new_block.reshape(block.shape), search.reshape(block.shape))

time: 146 us -> 132 us (0.904)
  local copies, waits for them, and re-layouts: 14 us -> 1.44 us
  Pallas kernels: 32.9 us -> 38.2 us
  blocking collectives: 66.1 us -> 61.4 us
  other arithmetic: 4.34 us -> 0.13 us
  waiting for transfers between devices: 2.1 us -> 4.18 us
    unnamed x33 -> x6, local copies, waits for them, and re-layouts: 12.4 us -> 1.41 us
    concatenate x8 -> x0, other arithmetic: 4.21 us -> none  [payload(): return jnp.concatenate(parts)]
    pallas_call x0 -> x1, Pallas kernels: none -> 3.75 us  [pack_call(): pl.pallas_call(pack_kernel, out_shape=tuple((jax.ShapeDtypeStruct(s, jnp....]
    all_to_all x1, blocking collectives: 31.2 us -> 28.3 us  [spread_sum(): lax.all_to_all(jnp.broadcast_to(part[None], (depth,) + part.shape), 'pz',...]
    ppermute x8, waiting for transfers between devices: 2.1 us -> 4.18 us  [neighbour(): return lax.ppermute(payload, ('px', 'pz', 'pc'), pairs)]
    all_to_all x1, blocking collectives: 19.8 us -> 18 us  [spread_sum(): part = jnp.sum(lax.all_to_all(pieces, plane, 0, 0), axis=0)]
    pallas_call x1, Pallas kernels: 15.1 us -> 16.8 us  [gram_call(): pl.pallas_call(gram_kernel, out_shape=(jax.ShapeDtypeStruct((256, 256), j...]
  transfers between devices with their start and end apart: 8 -> 8, of which waited for: 1 -> 3; matrix products, arithmetic and copies ran while one was open for 3% -> 0% of each run, Pallas kernels for 0% -> 0%
where the time goes in v5:
time: 132 us; the launch traced here: 131 us
  blocking collectives  61.4 us (47%)
  Pallas kernels  38.2 us (29%)
  starting transfers between devices  25.1 us (19%)
  waiting for transfers between devices  4.18 us (3%)
  local copies, waits for them, and re-layouts  1.44 us (1%)
    all_to_all x1, blocking collectives, spread_sum(): lax.all_to_all(jnp.broadcast_to(part[None], (depth,) + part.shape), 'pz',...  28.3 us
    ppermute x8, starting transfers between devices, neighbour(): return lax.ppermute(payload, ('px', 'pz', 'pc'), pairs)  25.1 us
    all_to_all x1, blocking collectives, spread_sum(): part = jnp.sum(lax.all_to_all(pieces, plane, 0, 0), axis=0)  18 us
    pallas_call x1, Pallas kernels, finish_call(): pl.pallas_call(lambda *refs: finish_kernel(scale, *refs), out_shape=(out,...  17.7 us
    pallas_call x1, Pallas kernels, gram_call(): pl.pallas_call(gram_kernel, out_shape=(jax.ShapeDtypeStruct((256, 256), j...  16.8 us
    all_to_all x1, blocking collectives, spread_sum(): lax.all_to_all(jnp.broadcast_to(part[None], (count,) + part.shape), plane...  15.1 us
    ppermute x8, waiting for transfers between devices, neighbour(): return lax.ppermute(payload, ('px', 'pz', 'pc'), pairs)  4.18 us
    pallas_call x1, Pallas kernels, pack_call(): pl.pallas_call(pack_kernel, out_shape=tuple((jax.ShapeDtypeStruct(s, jnp....  3.75 us
  transfers between devices with their start and end apart: 8, of which 3 were waited for; matrix products, arithmetic and copies ran while one was open for 0% of the time, Pallas kernels for 0%

profile of v5, /device:TPU:1, one launch (start us, length us, event | category | flops | bytes accessed | tf_op | source)
XLA Modules:
  0.0 131.3 jit_solution(5525504232287579915)
XLA Ops:
  0.6 3.7 %shard_map.50 = (f32[4,8,96,128]{3,2,1,0:T(8,128)}, f32[25,48,128]{2,1,0:T(8,128)}, f32[9,48,128]{2,1,0:T(8,128)}, f32[13,48,128]{2,1,0:T(8,128)}, f32[5,48,128]...) custom-call(f32[1536,128]{1,0:T(8,128)} %bitcast.12, ...), custom_call_target="tpu_custom_call" | custom-call | tf_op jit(solution)/shard_map/pallas_call | solution.py:238
  4.4 1.3 collective-permute-start
  5.7 8.8 %collective-permute-start.2 = (f32[13,48,128]{2,1,0:T(8,128)}, f32[13,48,128]{2,1,0:T(8,128)S(1)}, u32[]{:S(2)}, u32[]{:S(2)}) collective-permute-start(f32[13,48,128]{2,1,0:T(8,128)} %get-tuple-element.18), channel_id=1, source_target_pairs={{1,0},{2,1},{3,2},{4,3},{5,4},{6,5},{7,6},{8,7},{9,8},{10,9},{11,1... | collective-permute-start | bytes 958472 | tf_op jit(solution)/shard_map/ppermute | solution.py:474
  14.5 1.3 collective-permute-start.5
  15.8 4.9 %collective-permute-start.1 = (f32[9,48,128]{2,1,0:T(8,128)}, f32[9,48,128]{2,1,0:T(8,128)S(1)}, u32[]{:S(2)}, u32[]{:S(2)}) collective-permute-start(f32[9,48,128]{2,1,0:T(8,128)} %get-tuple-element.17), channel_id=1, source_target_pairs={{0,32},{1,33},{2,34},{3,35},{4,36},{5,37},{6,38},{7,39},{8,40},{9,... | collective-permute-start | bytes 663560 | tf_op jit(solution)/shard_map/ppermute | solution.py:474
  20.7 1.3 collective-permute-start.6
  22.0 0.0 collective-permute-done.5.c_mm
  22.0 4.3 %collective-permute-start.7 = (f32[2,48,128]{2,1,0:T(8,128)}, f32[2,48,128]{2,1,0:T(8,128)S(1)}, u32[]{:S(2)}, u32[]{:S(2)}) collective-permute-start(f32[2,48,128]{2,1,0:T(8,128)} %get-tuple-element.23), channel_id=1, source_target_pairs={{1,32},{2,33},{3,34},{4,35},{5,36},{6,37},{7,38},{8,39},{9,40},{10... | collective-permute-start | bytes 147464 | tf_op jit(solution)/shard_map/ppermute | solution.py:474
  26.3 0.0 collective-permute-done.6.c_pm
  26.3 1.3 collective-permute-start.4
  27.6 0.4 collective-permute-done.7.c_mp
  28.0 2.0 %collective-permute-start.3 = (f32[5,48,128]{2,1,0:T(8,128)}, f32[5,48,128]{2,1,0:T(8,128)S(1)}, u32[]{:S(2)}, u32[]{:S(2)}) collective-permute-start(f32[5,48,128]{2,1,0:T(8,128)} %get-tuple-element.19), channel_id=1, source_target_pairs={{0,1},{1,2},{2,3},{3,4},{4,5},{5,6},{6,7},{7,8},{8,9},{9,10},{10,1... | collective-permute-start | bytes 368648 | tf_op jit(solution)/shard_map/ppermute | solution.py:474
  30.1 0.1 pad_add_fusion.start_ref
  30.1 2.1 %collective-permute-done.3.up_b = f32[5,48,128]{2,1,0:T(8,128)S(1)} collective-permute-done((f32[5,48,128]{2,1,0:T(8,128)}, f32[5,48,128]{2,1,0:T(8,128)S(1)}, u32[]{:S(2)}, u32[]{:S(2)}) %collective-permute-start.3) | collective-permute-done | bytes 122912 | tf_op jit(solution)/shard_map/ppermute | solution.py:474
  32.2 1.6 %collective-permute-done.4.c_pp = f32[6,48,128]{2,1,0:T(8,128)S(1)} collective-permute-done((f32[6,48,128]{2,1,0:T(8,128)}, f32[6,48,128]{2,1,0:T(8,128)S(1)}, u32[]{:S(2)}, u32[]{:S(2)}) %collective-permute-start.4) | collective-permute-done | bytes 147488 | tf_op jit(solution)/shard_map/ppermute | solution.py:474
  33.9 0.0 collective-permute-done.1.up_a
  33.9 0.0 collective-permute-done.2.down_b
  33.9 0.0 collective-permute-done.down_a
  33.9 1.4 %copy-done = f32[4,8,96,128]{3,2,1,0:T(8,128)S(1)} copy-done((f32[4,8,96,128]{3,2,1,0:T(8,128)S(1)}, f32[4,8,96,128]{3,2,1,0:T(8,128)}, u32[]{:S(2)}) %copy-start) | copy-done | bytes 1572888
  35.3 16.8 %shard_map.51 = (f32[256,256]{1,0:T(8,128)S(1)}, f32[32,96,128]{2,1,0:T(8,128)S(1)}) custom-call(s32[4]{0:T(128)S(1)} %pad_add_fusion.start_ref, f32[4,8,96,128]{3,2,1,0:T(8,128)S(1)} %copy-done, f32[25,48,128]{2,1,0:T(8,128)S(1)} %collective-permute-done.down_a, f32[9,48,128]{2,1,0:T(8,128)S(1)} %collective-permute-done.1.up_a, ...), custom_call_target="tpu_custom_call" | custom-call | tf_op jit(solution)/shard_map/pallas_call | solution.py:386
  52.1 18.0 %all_to_all.15 = f32[32,8,256]{2,1,0:T(8,128)S(1)} all-to-all(f32[32,8,256]{2,1,0:T(8,128)S(1)} %bitcast.11), channel_id=1, replica_groups=mesh['px'=16,'pz'=16,'pc'=2] {'px','pc'}, dimensions={0} | all-to-all | bytes 524288 | tf_op jit(solution)/shard_map/all_to_all | solution.py:458
  70.1 28.3 %all_to_all.16 = f32[16,8,256]{2,1,0:T(8,128)S(1)} all-to-all(f32[16,8,256]{2,1,0:T(8,128)S(1)} %broadcast_in_dim.4), channel_id=1, replica_groups=mesh['px'=16,'pz'=16,'pc'=2] {'pz'}, dimensions={0} | all-to-all | bytes 262144 | tf_op jit(solution)/shard_map/all_to_all | solution.py:460
  98.5 15.1 %all_to_all.17 = f32[32,8,256]{2,1,0:T(8,128)S(1)} all-to-all(f32[32,8,256]{2,1,0:T(8,128)S(1)} %broadcast_in_dim.5), channel_id=1, replica_groups=mesh['px'=16,'pz'=16,'pc'=2] {'px','pc'}, dimensions={0} | all-to-all | bytes 524288 | tf_op jit(solution)/shard_map/all_to_all | solution.py:462
  113.6 17.7 %shard_map.52 = (f32[1536,128]{1,0:T(8,128)}, f32[1536,128]{1,0:T(8,128)}) custom-call(f32[256,256]{1,0:T(8,128)S(1)} %bitcast.10, f32[32,96,128]{2,1,0:T(8,128)S(1)} %bitcast.9, f32[32,96,128]{2,1,0:T(8,128)S(1)} %get-tuple-element.25.refs_2_), custom_call_target="tpu_custom_call" | custom-call | tf_op jit(solution)/shard_map/pallas_call | solution.py:439
  (9 shorter events, 0.1 us)
Async XLA Ops:
  0.6 33.2 %copy-start.2 = (f32[3,4,8,128]{3,2,1,0:T(8,128)S(1)}, f32[3,4,8,128]{3,2,1,0:T(8,128)}, u32[]{:S(2)}) copy-start(f32[3,4,8,128]{3,2,1,0:T(8,128)} %off_own.1) | copy-start | bytes 147460
  4.4 29.5 %collective-permute-start = (f32[25,48,128]{2,1,0:T(8,128)}, f32[25,48,128]{2,1,0:T(8,128)S(1)}, u32[]{:S(2)}, u32[]{:S(2)}) collective-permute-start(f32[25,48,128]{2,1,0:T(8,128)} %get-tuple-element.16), channel_id=1, source_target_pairs={{32,0},{33,1},{34,2},{35,3},{36,4},{37,5},{38,6},{39,7},{40,8},{41... | collective-permute-start | bytes 1843208 | tf_op jit(solution)/shard_map/ppermute | solution.py:474
  5.7 28.2 %collective-permute-start.2 = (f32[13,48,128]{2,1,0:T(8,128)}, f32[13,48,128]{2,1,0:T(8,128)S(1)}, u32[]{:S(2)}, u32[]{:S(2)}) collective-permute-start(f32[13,48,128]{2,1,0:T(8,128)} %get-tuple-element.18), channel_id=1, source_target_pairs={{1,0},{2,1},{3,2},{4,3},{5,4},{6,5},{7,6},{8,7},{9,8},{10,9},{11,1... | collective-permute-start | bytes 958472 | tf_op jit(solution)/shard_map/ppermute | solution.py:474
  14.5 7.5 %collective-permute-start.5 = (f32[2,48,128]{2,1,0:T(8,128)}, f32[2,48,128]{2,1,0:T(8,128)S(1)}, u32[]{:S(2)}, u32[]{:S(2)}) collective-permute-start(f32[2,48,128]{2,1,0:T(8,128)} %get-tuple-element.21), channel_id=1, source_target_pairs={{0,33},{1,34},{2,35},{3,36},{4,37},{5,38},{6,39},{7,40},{8,41},{9,... | collective-permute-start | bytes 147464 | tf_op jit(solution)/shard_map/ppermute | solution.py:474
  15.8 18.1 %collective-permute-start.1 = (f32[9,48,128]{2,1,0:T(8,128)}, f32[9,48,128]{2,1,0:T(8,128)S(1)}, u32[]{:S(2)}, u32[]{:S(2)}) collective-permute-start(f32[9,48,128]{2,1,0:T(8,128)} %get-tuple-element.17), channel_id=1, source_target_pairs={{0,32},{1,33},{2,34},{3,35},{4,36},{5,37},{6,38},{7,39},{8,40},{9,... | collective-permute-start | bytes 663560 | tf_op jit(solution)/shard_map/ppermute | solution.py:474
  20.7 5.6 %collective-permute-start.6 = (f32[2,48,128]{2,1,0:T(8,128)}, f32[2,48,128]{2,1,0:T(8,128)S(1)}, u32[]{:S(2)}, u32[]{:S(2)}) collective-permute-start(f32[2,48,128]{2,1,0:T(8,128)} %get-tuple-element.22), channel_id=1, source_target_pairs={{32,1},{33,2},{34,3},{35,4},{36,5},{37,6},{38,7},{39,8},{40,9},{41... | collective-permute-start | bytes 147464 | tf_op jit(solution)/shard_map/ppermute | solution.py:474
  22.0 6.0 %collective-permute-start.7 = (f32[2,48,128]{2,1,0:T(8,128)}, f32[2,48,128]{2,1,0:T(8,128)S(1)}, u32[]{:S(2)}, u32[]{:S(2)}) collective-permute-start(f32[2,48,128]{2,1,0:T(8,128)} %get-tuple-element.23), channel_id=1, source_target_pairs={{1,32},{2,33},{3,34},{4,35},{5,36},{6,37},{7,38},{8,39},{9,40},{10... | collective-permute-start | bytes 147464 | tf_op jit(solution)/shard_map/ppermute | solution.py:474
  26.3 7.6 %collective-permute-start.4 = (f32[6,48,128]{2,1,0:T(8,128)}, f32[6,48,128]{2,1,0:T(8,128)S(1)}, u32[]{:S(2)}, u32[]{:S(2)}) collective-permute-start(f32[6,48,128]{2,1,0:T(8,128)} %get-tuple-element.20), channel_id=1, source_target_pairs={{33,0},{34,1},{35,2},{36,3},{37,4},{38,5},{39,6},{40,7},{41,8},{42... | collective-permute-start | bytes 442376 | tf_op jit(solution)/shard_map/ppermute | solution.py:474
  28.0 4.2 %collective-permute-start.3 = (f32[5,48,128]{2,1,0:T(8,128)}, f32[5,48,128]{2,1,0:T(8,128)S(1)}, u32[]{:S(2)}, u32[]{:S(2)}) collective-permute-start(f32[5,48,128]{2,1,0:T(8,128)} %get-tuple-element.19), channel_id=1, source_target_pairs={{0,1},{1,2},{2,3},{3,4},{4,5},{5,6},{6,7},{7,8},{8,9},{9,10},{10,1... | collective-permute-start | bytes 368648 | tf_op jit(solution)/shard_map/ppermute | solution.py:474
  33.9 1.4 %copy-start = (f32[4,8,96,128]{3,2,1,0:T(8,128)S(1)}, f32[4,8,96,128]{3,2,1,0:T(8,128)}, u32[]{:S(2)}) copy-start(f32[4,8,96,128]{3,2,1,0:T(8,128)} %get-tuple-element.15.own) | copy-start | bytes 4718596
  52.1 61.5 %copy-start.1 = (f32[4,8,96,128]{3,2,1,0:T(8,128)S(1)}, f32[4,8,96,128]{3,2,1,0:T(8,128)}, u32[]{:S(2)}) copy-start(f32[4,8,96,128]{3,2,1,0:T(8,128)} %get-tuple-element.15.own) | copy-start | bytes 4718596

commit v6 on v5

--- a/solution.py
+++ b/solution.py
@@ -16,6 +16,19 @@
 
 def dots(a, b, dims):
     return lax.dot_general(a, b, (dims, ((), ())), precision=HI, preferred_element_type=jnp.float32)
+
+
+def split(x):
+    high = x.astype(jnp.bfloat16)
+    return high, (x - high.astype(jnp.float32)).astype(jnp.bfloat16)
+
+
+def split_dots(a, b, dims):
+    (a_high, a_low), (b_high, b_low) = split(a), split(b)
+    one = lambda x, y: lax.dot_general(
+        x, y, (dims, ((), ())), preferred_element_type=jnp.float32
+    )
+    return one(a_high, b_high) + (one(a_high, b_low) + one(a_low, b_high))
 
 
 def eliminated(gram):
@@ -32,16 +45,28 @@
         gram = gram[third:]
         inverse = inverse[third:]
         pivots = jnp.ones((third, 128), jnp.float32)
-        for k in range(third):
+        for k in range(0, third, 2):
             c = third * j + k
-            column = jnp.broadcast_to(left[:, c : c + 1], (third, 128))
-            pivot = column[k : k + 1, :]
-            pivots = jnp.where(place == k, pivot, pivots)
-            factor = jnp.where(place > k, column * (1.0 / pivot), 0.0)
-            factor = jnp.concatenate([factor, factor], axis=1)
+            first = jnp.broadcast_to(left[:, c : c + 1], (third, 128))
+            second = jnp.broadcast_to(left[:, c + 1 : c + 2], (third, 128))
+            p = first[k : k + 1, :]
+            r = second[k : k + 1, :]
+            s = second[k + 1 : k + 2, :]
+            det = p * s - r * r
+            inv = 1.0 / det
+            ratio = r / p
+            sp = s * inv
+            rp = r * inv
+            pp = p * inv
+            one = jnp.where(place > k + 1, first * sp - second * rp, 0.0)
+            one = jnp.where(place == k + 1, ratio, one)
+            two = jnp.where(place > k + 1, second * pp - first * rp, 0.0)
+            pivots = jnp.where(place == k, p, jnp.where(place == k + 1, s - r * ratio, pivots))
+            one = jnp.concatenate([one, one], axis=1)
+            two = jnp.concatenate([two, two], axis=1)
             left, right = (
-                left - factor * left[k : k + 1, :],
-                right - factor * right[k : k + 1, :],
+                left - one * left[k : k + 1, :] - two * left[k + 1 : k + 2, :],
+                right - one * right[k : k + 1, :] - two * right[k + 1 : k + 2, :],
             )
         scale = 1.0 / jnp.sqrt(pivots)
         scale = jnp.concatenate([scale, scale], axis=1)
@@ -185,16 +210,17 @@
         low = high
 
 
-def pack_kernel(block_ref, prior_ref, off_ref, own, down_a, up_a, down_b, up_b, c_pp, c_mm, c_pm, c_mp):
+def pack_kernel(block_ref, prior_ref, off_ref, down_a, up_a, down_b, up_b, c_pp, c_mm, c_pm, c_mp):
     v = VECS
     block = lambda a, b: block_ref[pl.ds(a * 8 + b, v, stride=32), :]
     prior = lambda a, b: prior_ref[pl.ds(a * 8 + b, v, stride=32), :]
     for a in range(4):
         for b in range(8):
+            if a in (2,) and b not in (0, 1, 7):
+                continue
             x = block(a, b)
-            y = prior(a, b)
-            own[a, b, :v] = x
-            own[a, b, v:] = y
+            if a == 0 or b == 0:
+                y = prior(a, b)
             if a < 2:
                 down_a[a * 8 + b] = x
             if a == 0:
@@ -234,7 +260,7 @@
 def pack_call(block, prior, offsets):
     v = VECS
     vmem = pl.BlockSpec(memory_space=VMEM)
-    sizes = [(4, 8, 2 * v, 128)] + [(n, v, 128) for n in (25, 9, 13, 5, 6, 2, 2, 2)]
+    sizes = [(n, v, 128) for n in (25, 9, 13, 5, 6, 2, 2, 2)]
     return pl.pallas_call(
         pack_kernel,
         out_shape=tuple(jax.ShapeDtypeStruct(s, jnp.float32) for s in sizes),
@@ -244,8 +270,8 @@
     )(block.reshape(-1, 128), prior.reshape(-1, 128), offsets)
 
 
-def gram_kernel(start_ref, own, down_a, up_a, down_b, up_b, c_pp, c_mm, c_pm, c_mp, off_own,
-                gram_ref, uw_ref, edge_ref, off_ref, coef_ref, turn_ref, xb_ref, y_ref, acc_ref,
+def gram_kernel(start_ref, block_hbm, prior_hbm, down_a, up_a, down_b, up_b, c_pp, c_mm, c_pm, c_mp, off_own,
+                gram_ref, basis_hbm, block_ref, prior_ref, edge_ref, off_ref, coef_ref, turn_ref, xb_ref, y_ref, acc_ref,
                 sems):
     v = VECS
     moves = [
@@ -253,8 +279,8 @@
         for i, piece in enumerate((down_a, up_a, down_b, up_b, c_pp, c_mm, c_pm, c_mp))
     ]
     third = slice(2 * v, 3 * v)
+    moves += [(block_hbm, block_ref), (prior_hbm, prior_ref)]
     moves += [
-        (own.at[:, :, :v], xb_ref.at[1:5, 1:9]),
         (down_a.at[0:8], xb_ref.at[5, 1:9]),
         (down_a.at[8:16], xb_ref.at[6, 1:9]),
         (up_a.at[0:8], xb_ref.at[0, 1:9]),
@@ -266,7 +292,6 @@
         (c_mm.at[0], xb_ref.at[0, 0]),
         (c_pm.at[0], xb_ref.at[5, 0]),
         (c_mp.at[0], xb_ref.at[0, 9]),
-        (own.at[:, :, v:], y_ref.at[0:4, 0:8, third]),
         (down_a.at[16:24], y_ref.at[4, 0:8, third]),
         (down_b.at[8:12], y_ref.at[0:4, 8, third]),
         (c_pp.at[4], y_ref.at[4, 8, third]),
@@ -274,6 +299,13 @@
     copies = [pltpu.make_async_copy(x, y, sems.at[i]) for i, (x, y) in enumerate(moves)]
     for copy in copies:
         copy.start()
+    for copy in copies[8:10]:
+        copy.wait()
+    for a in range(4):
+        for b in range(8):
+            rows = pl.ds(a * 8 + b, v, stride=32)
+            xb_ref[a + 1, b + 1] = block_ref[rows, :]
+            y_ref[a, b, third] = prior_ref[rows, :]
     for copy in copies[:8]:
         copy.wait()
     for i in range(3):
@@ -296,7 +328,7 @@
         if dc:
             for a in range(6):
                 turn_ref[slot, a] = shifted_lanes(coef_ref[slot, a], -1)
-    for copy in copies[8:]:
+    for copy in copies[10:]:
         copy.wait()
 
     def row(ref, slot, a, b):
@@ -327,7 +359,15 @@
         y_ref[a, b, v : 2 * v] = xb_ref[a + 1, b + 1] * (row(coef_ref, 8, a + 1, b + 1) * inverse)
         return carry
 
-    lax.fori_loop(0, 45, first, 0)
+    lax.fori_loop(0, 45, first, 0, unroll=3)
+    results = [
+        pltpu.make_async_copy(x, basis_hbm.at[:, :, rows], sems.at[24 + i])
+        for i, (x, rows) in enumerate(
+            ((xb_ref.at[1:5, 1:9], slice(0, v)), (y_ref.at[0:4, 0:8], slice(v, 4 * v)))
+        )
+    ]
+    for copy in results:
+        copy.start()
 
     acc_ref[...] = jnp.zeros(acc_ref.shape, jnp.float32)
 
@@ -354,13 +394,9 @@
         b = (t - a * 4) * 2
         x0, r0 = sides(a, b)
         x1, r1 = sides(a, b + 1)
-        uw_ref[a * 8 + b] = x0[v : 3 * v]
-        uw_ref[a * 8 + b + 1] = x1[v : 3 * v]
         left = jnp.concatenate([r0, r1], axis=1)
         right = jnp.concatenate([x0, x1], axis=1)
-        acc_ref[...] += lax.dot_general(
-            left, right, (((1,), (1,)), ((), ())), precision=HI,
-            preferred_element_type=jnp.float32)
+        acc_ref[...] += split_dots(left, right, ((1,), (1,)))
         return carry
 
     lax.fori_loop(0, 16, second, 0)
@@ -378,22 +414,26 @@
     diagonal = jnp.sum(jnp.where(rows == cols, gram_m, 0.0), axis=0, keepdims=True)
     square = jnp.where(rows <= cols, gram_k, gram_m)
     gram_ref[...] = jnp.where(rows < n, square, diagonal)
-
-
-def gram_call(start, own, pieces, off):
+    for copy in results:
+        copy.wait()
+
+
+def gram_call(start, block, prior, pieces, off):
     v = VECS
     spec = pl.BlockSpec(memory_space=VMEM)
     return pl.pallas_call(
         gram_kernel,
         out_shape=(
             jax.ShapeDtypeStruct((256, 256), jnp.float32),
-            jax.ShapeDtypeStruct((32, 2 * v, 128), jnp.float32),
+            jax.ShapeDtypeStruct((4, 8, 4 * v, 128), jnp.float32),
         ),
         in_specs=[pl.BlockSpec(memory_space=pltpu.SMEM)]
-        + [pl.BlockSpec(memory_space=pl.ANY)] * (1 + len(pieces))
+        + [pl.BlockSpec(memory_space=pl.ANY)] * (2 + len(pieces))
         + [spec],
-        out_specs=(spec, spec),
+        out_specs=(spec, pl.BlockSpec(memory_space=pl.ANY)),
         scratch_shapes=[
+            VMEM((32 * v, 128), jnp.float32),
+            VMEM((32 * v, 128), jnp.float32),
             VMEM((8, v, 128), jnp.float32),
             VMEM((3, 8, 16, 128), jnp.float32),
             VMEM((9, 6, 16, 128), jnp.float32),
@@ -401,53 +441,44 @@
             VMEM((7, 11, v, 128), jnp.float32),
             VMEM((5, 9, 3 * v, 128), jnp.float32),
             VMEM((8 * v, 4 * v), jnp.float32),
-            pltpu.SemaphoreType.DMA((24,)),
+            pltpu.SemaphoreType.DMA((26,)),
         ],
-        compiler_params=pltpu.CompilerParams(vmem_limit_bytes=12 * 2**20),
-    )(start, own, *pieces, off)
-
-
-def finish_kernel(scale, total_ref, own_hbm, uw_hbm, new_ref, search_ref, own_ref, uw_ref, sems):
+        compiler_params=pltpu.CompilerParams(vmem_limit_bytes=52 * 2**20),
+    )(start, block.reshape(-1, 128), prior.reshape(-1, 128), *pieces, off)
+
+
+def finish_kernel(scale, total_ref, basis_hbm, new_ref, search_ref, basis_ref, sem):
     v = VECS
-    copies = [
-        pltpu.make_async_copy(own_hbm, own_ref, sems.at[0]),
-        pltpu.make_async_copy(uw_hbm, uw_ref, sems.at[1]),
-    ]
-    for copy in copies:
-        copy.start()
+    load = pltpu.make_async_copy(basis_hbm, basis_ref, sem)
+    load.start()
     coeffs, quotient = ritz_core(total_ref[...])
     coeffs = coeffs * scale
     quotient = jnp.broadcast_to(quotient, (v, 128))
-    for copy in copies:
-        copy.wait()
+    load.wait()
     for t in range(0, 32, 2):
         basis = []
         for i in (t, t + 1):
-            search = uw_ref[i, :v] - quotient * uw_ref[i, v:]
+            x = basis_ref[i // 8, i % 8]
+            search = x[v : 2 * v] - quotient * x[2 * v : 3 * v]
             search_ref[pl.ds(i, v, stride=32), :] = search
-            basis.append(jnp.concatenate([own_ref[i, :v], search, own_ref[i, v:]], axis=0))
-        new = dots(coeffs, jnp.concatenate(basis, axis=1), ((1,), (0,)))
+            basis.append(jnp.concatenate([x[:v], search, x[3 * v :]], axis=0))
+        new = split_dots(coeffs, jnp.concatenate(basis, axis=1), ((1,), (0,)))
         new_ref[pl.ds(t, v, stride=32), :] = new[:, :128]
         new_ref[pl.ds(t + 1, v, stride=32), :] = new[:, 128:]
 
 
-def finish_call(scale, total, own, uw):
+def finish_call(scale, total, basis):
     v = VECS
     vmem = pl.BlockSpec(memory_space=VMEM)
-    hbm = pl.BlockSpec(memory_space=pl.ANY)
     out = jax.ShapeDtypeStruct((v * 32, 128), jnp.float32)
     return pl.pallas_call(
         lambda *refs: finish_kernel(scale, *refs),
         out_shape=(out, out),
-        in_specs=[vmem, hbm, hbm],
+        in_specs=[vmem, pl.BlockSpec(memory_space=pl.ANY)],
         out_specs=(vmem, vmem),
-        scratch_shapes=[
-            VMEM((32, 2 * v, 128), jnp.float32),
-            VMEM((32, 2 * v, 128), jnp.float32),
-            pltpu.SemaphoreType.DMA((2,)),
-        ],
-        compiler_params=pltpu.CompilerParams(vmem_limit_bytes=12 * 2**20),
-    )(total, own, uw)
+        scratch_shapes=[VMEM((4, 8, 4 * v, 128), jnp.float32), pltpu.SemaphoreType.DMA],
+        compiler_params=pltpu.CompilerParams(vmem_limit_bytes=60 * 2**20),
+    )(total, basis)
 
 
 def spread_sum(rows):
@@ -475,7 +506,6 @@
 
 
 def shards(offsets, block, prior):
-    v = block.shape[0]
     rows_a, rows_b, depth = block.shape[1:]
     total_a = rows_a * lax.axis_size("px")
     total_b = rows_b * lax.axis_size("pz") * lax.axis_size("pc")
@@ -487,7 +517,7 @@
             jnp.int32(total_b),
         ]
     ).astype(jnp.int32)
-    own, down_a, up_a, down_b, up_b, c_pp, c_mm, c_pm, c_mp = pack_call(block, prior, offsets)
+    down_a, up_a, down_b, up_b, c_pp, c_mm, c_pm, c_mp = pack_call(block, prior, offsets)
     pieces = (
         neighbour(down_a, 1, 0),
         neighbour(up_a, -1, 0),
@@ -498,10 +528,9 @@
         neighbour(c_pm, 1, -1),
         neighbour(c_mp, -1, 1),
     )
-    gram, uw = gram_call(start, own, pieces, offsets)
-    own = own.reshape(rows_a * rows_b, 2 * v, depth)
+    gram, basis = gram_call(start, block, prior, pieces, offsets)
     scale = math.sqrt(total_a * total_b * depth)
-    new_block, search = finish_call(scale, spread_sum(gram), own, uw)
+    new_block, search = finish_call(scale, spread_sum(gram), basis)
     return (new_block.reshape(block.shape), search.reshape(block.shape))
 
 

time: 132 us -> 122 us (0.924)
  Pallas kernels: 38.2 us -> 29 us
    pallas_call x1, Pallas kernels: 17.7 us -> 12.9 us  [finish_call(): pl.pallas_call(lambda *refs: finish_kernel(scale, *refs), out_shape=(out,...]
    pallas_call x1, Pallas kernels: 16.8 us -> 13 us  [gram_call(): pl.pallas_call(gram_kernel, out_shape=(jax.ShapeDtypeStruct((256, 256), j...]
where the time goes in v6:
time: 122 us; the launch traced here: 121 us
  blocking collectives  61.4 us (50%)
  Pallas kernels  29 us (24%)
  starting transfers between devices  25.1 us (21%)
  waiting for transfers between devices  4.18 us (3%)
    all_to_all x1, blocking collectives, spread_sum(): lax.all_to_all(jnp.broadcast_to(part[None], (depth,) + part.shape), 'pz',...  28.3 us
    ppermute x8, starting transfers between devices, neighbour(): return lax.ppermute(payload, ('px', 'pz', 'pc'), pairs)  25.1 us
    all_to_all x1, blocking collectives, spread_sum(): part = jnp.sum(lax.all_to_all(pieces, plane, 0, 0), axis=0)  17.8 us
    all_to_all x1, blocking collectives, spread_sum(): lax.all_to_all(jnp.broadcast_to(part[None], (count,) + part.shape), plane...  15.3 us
    pallas_call x1, Pallas kernels, gram_call(): pl.pallas_call(gram_kernel, out_shape=(jax.ShapeDtypeStruct((256, 256), j...  13 us
    pallas_call x1, Pallas kernels, finish_call(): pl.pallas_call(lambda *refs: finish_kernel(scale, *refs), out_shape=(out,...  12.9 us
    ppermute x8, waiting for transfers between devices, neighbour(): return lax.ppermute(payload, ('px', 'pz', 'pc'), pairs)  4.18 us
    pallas_call x1, Pallas kernels, pack_call(): pl.pallas_call(pack_kernel, out_shape=tuple((jax.ShapeDtypeStruct(s, jnp....  2.99 us
  transfers between devices with their start and end apart: 8, of which 3 were waited for; matrix products, arithmetic and copies ran while one was open for 0% of the time, Pallas kernels for 0%

profile of v6, /device:TPU:1, one launch (start us, length us, event | category | flops | bytes accessed | tf_op | source)
XLA Modules:
  0.0 121.4 jit_solution(135587903829850679)
XLA Ops:
  0.6 3.0 %shard_map.50 = (f32[25,48,128]{2,1,0:T(8,128)}, f32[9,48,128]{2,1,0:T(8,128)}, f32[13,48,128]{2,1,0:T(8,128)}, f32[5,48,128]{2,1,0:T(8,128)}, f32[6,48,128]{2,1...) custom-call(f32[1536,128]{1,0:T(8,128)} %bitcast.9, f32[1536,128]{1,0:T(8,128)} %bitcast.11, ...), custom_call_target="tpu_custom_call" | custom-call | tf_op jit(solution)/shard_map/pallas_call | solution.py:264
  3.6 1.3 %collective-permute-start = (f32[25,48,128]{2,1,0:T(8,128)}, f32[25,48,128]{2,1,0:T(8,128)S(1)}, u32[]{:S(2)}, u32[]{:S(2)}) collective-permute-start(f32[25,48,128]{2,1,0:T(8,128)} %get-tuple-element.14), channel_id=1, source_target_pairs={{32,0},{33,1},{34,2},{35,3},{36,4},{37,5},{38,6},{39,7},{40,8},{41... | collective-permute-start | bytes 1843208 | tf_op jit(solution)/shard_map/ppermute | solution.py:505
  4.9 8.8 %collective-permute-start.2 = (f32[13,48,128]{2,1,0:T(8,128)}, f32[13,48,128]{2,1,0:T(8,128)S(1)}, u32[]{:S(2)}, u32[]{:S(2)}) collective-permute-start(f32[13,48,128]{2,1,0:T(8,128)} %get-tuple-element.16), channel_id=1, source_target_pairs={{1,0},{2,1},{3,2},{4,3},{5,4},{6,5},{7,6},{8,7},{9,8},{10,9},{11,1... | collective-permute-start | bytes 958472 | tf_op jit(solution)/shard_map/ppermute | solution.py:505
  13.7 1.3 %collective-permute-start.5 = (f32[2,48,128]{2,1,0:T(8,128)}, f32[2,48,128]{2,1,0:T(8,128)S(1)}, u32[]{:S(2)}, u32[]{:S(2)}) collective-permute-start(f32[2,48,128]{2,1,0:T(8,128)} %get-tuple-element.19), channel_id=1, source_target_pairs={{0,33},{1,34},{2,35},{3,36},{4,37},{5,38},{6,39},{7,40},{8,41},{9,... | collective-permute-start | bytes 147464 | tf_op jit(solution)/shard_map/ppermute | solution.py:505
  15.0 4.9 %collective-permute-start.1 = (f32[9,48,128]{2,1,0:T(8,128)}, f32[9,48,128]{2,1,0:T(8,128)S(1)}, u32[]{:S(2)}, u32[]{:S(2)}) collective-permute-start(f32[9,48,128]{2,1,0:T(8,128)} %get-tuple-element.15), channel_id=1, source_target_pairs={{0,32},{1,33},{2,34},{3,35},{4,36},{5,37},{6,38},{7,39},{8,40},{9,... | collective-permute-start | bytes 663560 | tf_op jit(solution)/shard_map/ppermute | solution.py:505
  19.9 1.3 %collective-permute-start.6 = (f32[2,48,128]{2,1,0:T(8,128)}, f32[2,48,128]{2,1,0:T(8,128)S(1)}, u32[]{:S(2)}, u32[]{:S(2)}) collective-permute-start(f32[2,48,128]{2,1,0:T(8,128)} %get-tuple-element.20), channel_id=1, source_target_pairs={{32,1},{33,2},{34,3},{35,4},{36,5},{37,6},{38,7},{39,8},{40,9},{41... | collective-permute-start | bytes 147464 | tf_op jit(solution)/shard_map/ppermute | solution.py:505
  21.2 0.0 collective-permute-done.5.c_mm
  21.2 4.3 %collective-permute-start.7 = (f32[2,48,128]{2,1,0:T(8,128)}, f32[2,48,128]{2,1,0:T(8,128)S(1)}, u32[]{:S(2)}, u32[]{:S(2)}) collective-permute-start(f32[2,48,128]{2,1,0:T(8,128)} %get-tuple-element.21), channel_id=1, source_target_pairs={{1,32},{2,33},{3,34},{4,35},{5,36},{6,37},{7,38},{8,39},{9,40},{10... | collective-permute-start | bytes 147464 | tf_op jit(solution)/shard_map/ppermute | solution.py:505
  25.5 0.0 collective-permute-done.6.c_pm
  25.5 1.3 %collective-permute-start.4 = (f32[6,48,128]{2,1,0:T(8,128)}, f32[6,48,128]{2,1,0:T(8,128)S(1)}, u32[]{:S(2)}, u32[]{:S(2)}) collective-permute-start(f32[6,48,128]{2,1,0:T(8,128)} %get-tuple-element.18), channel_id=1, source_target_pairs={{33,0},{34,1},{35,2},{36,3},{37,4},{38,5},{39,6},{40,7},{41,8},{42... | collective-permute-start | bytes 442376 | tf_op jit(solution)/shard_map/ppermute | solution.py:505
  26.8 0.4 collective-permute-done.7.c_mp
  27.2 2.0 %collective-permute-start.3 = (f32[5,48,128]{2,1,0:T(8,128)}, f32[5,48,128]{2,1,0:T(8,128)S(1)}, u32[]{:S(2)}, u32[]{:S(2)}) collective-permute-start(f32[5,48,128]{2,1,0:T(8,128)} %get-tuple-element.17), channel_id=1, source_target_pairs={{0,1},{1,2},{2,3},{3,4},{4,5},{5,6},{6,7},{7,8},{8,9},{9,10},{10,1... | collective-permute-start | bytes 368648 | tf_op jit(solution)/shard_map/ppermute | solution.py:505
  29.3 0.1 pad_add_fusion.start_ref
  29.4 2.1 %collective-permute-done.3.up_b = f32[5,48,128]{2,1,0:T(8,128)S(1)} collective-permute-done((f32[5,48,128]{2,1,0:T(8,128)}, f32[5,48,128]{2,1,0:T(8,128)S(1)}, u32[]{:S(2)}, u32[]{:S(2)}) %collective-permute-start.3) | collective-permute-done | bytes 122912 | tf_op jit(solution)/shard_map/ppermute | solution.py:505
  31.5 1.6 %collective-permute-done.4.c_pp = f32[6,48,128]{2,1,0:T(8,128)S(1)} collective-permute-done((f32[6,48,128]{2,1,0:T(8,128)}, f32[6,48,128]{2,1,0:T(8,128)S(1)}, u32[]{:S(2)}, u32[]{:S(2)}) %collective-permute-start.4) | collective-permute-done | bytes 147488 | tf_op jit(solution)/shard_map/ppermute | solution.py:505
  33.1 0.0 collective-permute-done.1.up_a
  33.1 0.0 collective-permute-done.2.down_b
  33.1 0.0 copy-start
  33.1 0.8 copy-done
  33.9 13.0 %shard_map.51 = (f32[256,256]{1,0:T(8,128)S(1)}, f32[4,8,192,128]{3,2,1,0:T(8,128)}) custom-call(s32[4]{0:T(128)S(1)} %pad_add_fusion.start_ref, f32[1536,128]{1,0:T(8,128)} %bitcast.10, f32[1536,128]{1,0:T(8,128)} %bitcast.12, f32[25,48,128]{2,1,0:T(8,128)S(1)} %collective-permute-done.down_a, f32[9,48,128]{2,1,0:T(8,128)S(1)} %collective-permute-done.1.up_a, ...), custom_call_target="tpu_custom_call" | custom-call | tf_op jit(solution)/shard_map/pallas_call | solution.py:424
  47.0 17.8 %all_to_all.15 = f32[32,8,256]{2,1,0:T(8,128)S(1)} all-to-all(f32[32,8,256]{2,1,0:T(8,128)S(1)} %bitcast.8), channel_id=1, replica_groups=mesh['px'=16,'pz'=16,'pc'=2] {'px','pc'}, dimensions={0} | all-to-all | bytes 524288 | tf_op jit(solution)/shard_map/all_to_all | solution.py:489
  64.8 28.3 %all_to_all.16 = f32[16,8,256]{2,1,0:T(8,128)S(1)} all-to-all(f32[16,8,256]{2,1,0:T(8,128)S(1)} %broadcast_in_dim.4), channel_id=1, replica_groups=mesh['px'=16,'pz'=16,'pc'=2] {'pz'}, dimensions={0} | all-to-all | bytes 262144 | tf_op jit(solution)/shard_map/all_to_all | solution.py:491
  93.2 15.3 %all_to_all.17 = f32[32,8,256]{2,1,0:T(8,128)} all-to-all(f32[32,8,256]{2,1,0:T(8,128)S(1)} %broadcast_in_dim.5), channel_id=1, replica_groups=mesh['px'=16,'pz'=16,'pc'=2] {'px','pc'}, dimensions={0} | all-to-all | bytes 524288 | tf_op jit(solution)/shard_map/all_to_all | solution.py:493
  108.5 12.9 %shard_map.52 = (f32[1536,128]{1,0:T(8,128)}, f32[1536,128]{1,0:T(8,128)}) custom-call(f32[256,256]{1,0:T(8,128)} %bitcast.13, f32[4,8,192,128]{3,2,1,0:T(8,128)} %get-tuple-element.23.refs_1_), custom_call_target="tpu_custom_call" | custom-call | tf_op jit(solution)/shard_map/pallas_call | solution.py:474
  (5 shorter events, 0.1 us)
Async XLA Ops:
  3.6 29.5 %collective-permute-start = (f32[25,48,128]{2,1,0:T(8,128)}, f32[25,48,128]{2,1,0:T(8,128)S(1)}, u32[]{:S(2)}, u32[]{:S(2)}) collective-permute-start(f32[25,48,128]{2,1,0:T(8,128)} %get-tuple-element.14), channel_id=1, source_target_pairs={{32,0},{33,1},{34,2},{35,3},{36,4},{37,5},{38,6},{39,7},{40,8},{41... | collective-permute-start | bytes 1843208 | tf_op jit(solution)/shard_map/ppermute | solution.py:505
  4.9 28.2 %collective-permute-start.2 = (f32[13,48,128]{2,1,0:T(8,128)}, f32[13,48,128]{2,1,0:T(8,128)S(1)}, u32[]{:S(2)}, u32[]{:S(2)}) collective-permute-start(f32[13,48,128]{2,1,0:T(8,128)} %get-tuple-element.16), channel_id=1, source_target_pairs={{1,0},{2,1},{3,2},{4,3},{5,4},{6,5},{7,6},{8,7},{9,8},{10,9},{11,1... | collective-permute-start | bytes 958472 | tf_op jit(solution)/shard_map/ppermute | solution.py:505
  13.7 7.5 %collective-permute-start.5 = (f32[2,48,128]{2,1,0:T(8,128)}, f32[2,48,128]{2,1,0:T(8,128)S(1)}, u32[]{:S(2)}, u32[]{:S(2)}) collective-permute-start(f32[2,48,128]{2,1,0:T(8,128)} %get-tuple-element.19), channel_id=1, source_target_pairs={{0,33},{1,34},{2,35},{3,36},{4,37},{5,38},{6,39},{7,40},{8,41},{9,... | collective-permute-start | bytes 147464 | tf_op jit(solution)/shard_map/ppermute | solution.py:505
  15.0 18.1 %collective-permute-start.1 = (f32[9,48,128]{2,1,0:T(8,128)}, f32[9,48,128]{2,1,0:T(8,128)S(1)}, u32[]{:S(2)}, u32[]{:S(2)}) collective-permute-start(f32[9,48,128]{2,1,0:T(8,128)} %get-tuple-element.15), channel_id=1, source_target_pairs={{0,32},{1,33},{2,34},{3,35},{4,36},{5,37},{6,38},{7,39},{8,40},{9,... | collective-permute-start | bytes 663560 | tf_op jit(solution)/shard_map/ppermute | solution.py:505
  19.9 5.6 %collective-permute-start.6 = (f32[2,48,128]{2,1,0:T(8,128)}, f32[2,48,128]{2,1,0:T(8,128)S(1)}, u32[]{:S(2)}, u32[]{:S(2)}) collective-permute-start(f32[2,48,128]{2,1,0:T(8,128)} %get-tuple-element.20), channel_id=1, source_target_pairs={{32,1},{33,2},{34,3},{35,4},{36,5},{37,6},{38,7},{39,8},{40,9},{41... | collective-permute-start | bytes 147464 | tf_op jit(solution)/shard_map/ppermute | solution.py:505
  21.2 6.0 %collective-permute-start.7 = (f32[2,48,128]{2,1,0:T(8,128)}, f32[2,48,128]{2,1,0:T(8,128)S(1)}, u32[]{:S(2)}, u32[]{:S(2)}) collective-permute-start(f32[2,48,128]{2,1,0:T(8,128)} %get-tuple-element.21), channel_id=1, source_target_pairs={{1,32},{2,33},{3,34},{4,35},{5,36},{6,37},{7,38},{8,39},{9,40},{10... | collective-permute-start | bytes 147464 | tf_op jit(solution)/shard_map/ppermute | solution.py:505
  25.5 7.6 %collective-permute-start.4 = (f32[6,48,128]{2,1,0:T(8,128)}, f32[6,48,128]{2,1,0:T(8,128)S(1)}, u32[]{:S(2)}, u32[]{:S(2)}) collective-permute-start(f32[6,48,128]{2,1,0:T(8,128)} %get-tuple-element.18), channel_id=1, source_target_pairs={{33,0},{34,1},{35,2},{36,3},{37,4},{38,5},{39,6},{40,7},{41,8},{42... | collective-permute-start | bytes 442376 | tf_op jit(solution)/shard_map/ppermute | solution.py:505
  27.2 4.2 %collective-permute-start.3 = (f32[5,48,128]{2,1,0:T(8,128)}, f32[5,48,128]{2,1,0:T(8,128)S(1)}, u32[]{:S(2)}, u32[]{:S(2)}) collective-permute-start(f32[5,48,128]{2,1,0:T(8,128)} %get-tuple-element.17), channel_id=1, source_target_pairs={{0,1},{1,2},{2,3},{3,4},{4,5},{5,6},{6,7},{7,8},{8,9},{9,10},{10,1... | collective-permute-start | bytes 368648 | tf_op jit(solution)/shard_map/ppermute | solution.py:505
  33.1 0.8 copy-start

commit v7 on v6

--- a/solution.py
+++ b/solution.py
@@ -29,6 +29,19 @@
         x, y, (dims, ((), ())), preferred_element_type=jnp.float32
     )
     return one(a_high, b_high) + (one(a_high, b_low) + one(a_low, b_high))
+
+
+def pair_factors(first, second, k, place, pivots):
+    p = first[k : k + 1, :]
+    r = second[k : k + 1, :]
+    s = second[k + 1 : k + 2, :]
+    inv = 1.0 / (p * s - r * r)
+    ratio = r / p
+    one = jnp.where(place > k + 1, first * (s * inv) - second * (r * inv), 0.0)
+    one = jnp.where(place == k + 1, ratio, one)
+    two = jnp.where(place > k + 1, second * (p * inv) - first * (r * inv), 0.0)
+    pivots = jnp.where(place == k, p, jnp.where(place == k + 1, s - r * ratio, pivots))
+    return one, two, pivots
 
 
 def eliminated(gram):
@@ -45,29 +58,23 @@
         gram = gram[third:]
         inverse = inverse[third:]
         pivots = jnp.ones((third, 128), jnp.float32)
-        for k in range(0, third, 2):
+        for k in range(0, third, 4):
             c = third * j + k
-            first = jnp.broadcast_to(left[:, c : c + 1], (third, 128))
-            second = jnp.broadcast_to(left[:, c + 1 : c + 2], (third, 128))
-            p = first[k : k + 1, :]
-            r = second[k : k + 1, :]
-            s = second[k + 1 : k + 2, :]
-            det = p * s - r * r
-            inv = 1.0 / det
-            ratio = r / p
-            sp = s * inv
-            rp = r * inv
-            pp = p * inv
-            one = jnp.where(place > k + 1, first * sp - second * rp, 0.0)
-            one = jnp.where(place == k + 1, ratio, one)
-            two = jnp.where(place > k + 1, second * pp - first * rp, 0.0)
-            pivots = jnp.where(place == k, p, jnp.where(place == k + 1, s - r * ratio, pivots))
-            one = jnp.concatenate([one, one], axis=1)
-            two = jnp.concatenate([two, two], axis=1)
-            left, right = (
-                left - one * left[k : k + 1, :] - two * left[k + 1 : k + 2, :],
-                right - one * right[k : k + 1, :] - two * right[k + 1 : k + 2, :],
-            )
+            columns = [
+                jnp.broadcast_to(left[:, c + i : c + i + 1], (third, 128)) for i in range(4)
+            ]
+            one, two, pivots = pair_factors(columns[0], columns[1], k, place, pivots)
+            columns = [
+                x - one * x[k : k + 1, :] - two * x[k + 1 : k + 2, :] for x in columns[2:]
+            ]
+            three, four, pivots = pair_factors(columns[0], columns[1], k + 2, place, pivots)
+            one, two, three, four = [
+                jnp.concatenate([x, x], axis=1) for x in (one, two, three, four)
+            ]
+            left = left - one * left[k : k + 1, :] - two * left[k + 1 : k + 2, :]
+            right = right - one * right[k : k + 1, :] - two * right[k + 1 : k + 2, :]
+            left = left - three * left[k + 2 : k + 3, :] - four * left[k + 3 : k + 4, :]
+            right = right - three * right[k + 2 : k + 3, :] - four * right[k + 3 : k + 4, :]
         scale = 1.0 / jnp.sqrt(pivots)
         scale = jnp.concatenate([scale, scale], axis=1)
         left = left * scale
@@ -210,13 +217,22 @@
         low = high
 
 
-def pack_kernel(block_ref, prior_ref, off_ref, down_a, up_a, down_b, up_b, c_pp, c_mm, c_pm, c_mp):
+DOWN_B = [(0, 0), (0, 1), (1, 0), (1, 1)]
+REST_B = [(2, 0), (2, 1), (3, 1), (3, 0)]
+UP_B = {0: 0, 3: 2, 1: 3, 2: 4}
+
+
+def place_b(a, b):
+    return DOWN_B.index((a, b)) if (a, b) in DOWN_B else 9 + REST_B.index((a, b))
+
+
+def pack_kernel(block_ref, prior_ref, off_ref, down_a, up_a, down_b, up_b):
     v = VECS
     block = lambda a, b: block_ref[pl.ds(a * 8 + b, v, stride=32), :]
     prior = lambda a, b: prior_ref[pl.ds(a * 8 + b, v, stride=32), :]
     for a in range(4):
         for b in range(8):
-            if a in (2,) and b not in (0, 1, 7):
+            if a == 2 and b not in (0, 1, 7):
                 continue
             x = block(a, b)
             if a == 0 or b == 0:
@@ -228,39 +244,24 @@
             if a == 3:
                 up_a[b] = x
             if b < 2:
-                down_b[b * 4 + a] = x
+                down_b[place_b(a, b)] = x
             if b == 0:
-                down_b[8 + a] = y
+                down_b[4 if a == 0 else 5 + a] = y
             if b == 7:
-                up_b[a] = x
-            if a < 2 and b < 2:
-                c_pp[a * 2 + b] = x
-            if a == 0 and b == 0:
-                c_pp[4] = y
-            if a == 3 and b == 7:
-                c_mm[0] = x
-            if a == 0 and b == 7:
-                c_pm[0] = x
-            if a == 3 and b == 0:
-                c_mp[0] = x
+                up_b[UP_B[a]] = x
     for i in range(3):
         for a in range(4):
-            down_b[12, i * 8 + a * 2 : i * 8 + a * 2 + 2] = off_ref[i, a, 0:2]
-            up_b[4, i * 8 + a * 2 : i * 8 + a * 2 + 2] = off_ref[i, a, 6:8]
+            down_b[5, i * 8 + a * 2 : i * 8 + a * 2 + 2] = off_ref[i, a, 0:2]
+            up_b[1, i * 8 + a * 2 : i * 8 + a * 2 + 2] = off_ref[i, a, 6:8]
         for a in range(2):
             down_a[24, i * 16 + a * 8 : i * 16 + a * 8 + 8] = off_ref[i, a]
             up_a[8, i * 16 + a * 8 : i * 16 + a * 8 + 8] = off_ref[i, 2 + a]
-            pair = slice(i * 4 + a * 2, i * 4 + a * 2 + 2)
-            c_pp[5, pair] = off_ref[i, a, 0:2]
-            c_mm[1, pair] = off_ref[i, 2 + a, 6:8]
-            c_pm[1, pair] = off_ref[i, a, 6:8]
-            c_mp[1, pair] = off_ref[i, 2 + a, 0:2]
 
 
 def pack_call(block, prior, offsets):
     v = VECS
     vmem = pl.BlockSpec(memory_space=VMEM)
-    sizes = [(n, v, 128) for n in (25, 9, 13, 5, 6, 2, 2, 2)]
+    sizes = [(n, v, 128) for n in (25, 9, 13, 5)]
     return pl.pallas_call(
         pack_kernel,
         out_shape=tuple(jax.ShapeDtypeStruct(s, jnp.float32) for s in sizes),
@@ -270,31 +271,36 @@
     )(block.reshape(-1, 128), prior.reshape(-1, 128), offsets)
 
 
-def gram_kernel(start_ref, block_hbm, prior_hbm, down_a, up_a, down_b, up_b, c_pp, c_mm, c_pm, c_mp, off_own,
+def gram_kernel(start_ref, block_hbm, prior_hbm, down_a, up_a, down_b, up_b, down_c, up_c, off_own,
                 gram_ref, basis_hbm, block_ref, prior_ref, edge_ref, off_ref, coef_ref, turn_ref, xb_ref, y_ref, acc_ref,
                 sems):
     v = VECS
-    moves = [
-        (piece.at[piece.shape[0] - 1], edge_ref.at[i])
-        for i, piece in enumerate((down_a, up_a, down_b, up_b, c_pp, c_mm, c_pm, c_mp))
-    ]
+    edges = (down_a.at[24], up_a.at[8], down_b.at[5], up_b.at[1],
+             down_c.at[5], up_c.at[3], down_c.at[7], up_c.at[1])
+    moves = [(piece, edge_ref.at[i]) for i, piece in enumerate(edges)]
     third = slice(2 * v, 3 * v)
     moves += [(block_hbm, block_ref), (prior_hbm, prior_ref)]
     moves += [
         (down_a.at[0:8], xb_ref.at[5, 1:9]),
         (down_a.at[8:16], xb_ref.at[6, 1:9]),
         (up_a.at[0:8], xb_ref.at[0, 1:9]),
-        (down_b.at[0:4], xb_ref.at[1:5, 9]),
-        (down_b.at[4:8], xb_ref.at[1:5, 10]),
-        (up_b.at[0:4], xb_ref.at[1:5, 0]),
-        (c_pp.at[0:2], xb_ref.at[5, 9:11]),
-        (c_pp.at[2:4], xb_ref.at[6, 9:11]),
-        (c_mm.at[0], xb_ref.at[0, 0]),
-        (c_pm.at[0], xb_ref.at[5, 0]),
-        (c_mp.at[0], xb_ref.at[0, 9]),
+        (down_b.at[0:2], xb_ref.at[1, 9:11]),
+        (down_b.at[2:4], xb_ref.at[2, 9:11]),
+        (down_b.at[9:11], xb_ref.at[3, 9:11]),
+        (down_b.at[11], xb_ref.at[4, 10]),
+        (down_b.at[12], xb_ref.at[4, 9]),
+        (up_b.at[0], xb_ref.at[1, 0]),
+        (up_b.at[3:5], xb_ref.at[2:4, 0]),
+        (up_b.at[2], xb_ref.at[4, 0]),
+        (down_c.at[0:2], xb_ref.at[5, 9:11]),
+        (down_c.at[2:4], xb_ref.at[6, 9:11]),
+        (up_c.at[2], xb_ref.at[0, 0]),
+        (down_c.at[6], xb_ref.at[5, 0]),
+        (up_c.at[0], xb_ref.at[0, 9]),
         (down_a.at[16:24], y_ref.at[4, 0:8, third]),
-        (down_b.at[8:12], y_ref.at[0:4, 8, third]),
-        (c_pp.at[4], y_ref.at[4, 8, third]),
+        (down_b.at[4], y_ref.at[0, 8, third]),
+        (down_b.at[6:9], y_ref.at[1:4, 8, third]),
+        (down_c.at[4], y_ref.at[4, 8, third]),
     ]
     copies = [pltpu.make_async_copy(x, y, sems.at[i]) for i, (x, y) in enumerate(moves)]
     for copy in copies:
@@ -318,11 +324,12 @@
             rows = slice(i * 16 + a * 8, i * 16 + a * 8 + 8)
             off_ref[i, 6 + a, 2:10] = edge_ref[0, rows]
             off_ref[i, a, 2:10] = edge_ref[1, rows]
-            pair = slice(i * 4 + a * 2, i * 4 + a * 2 + 2)
-            off_ref[i, 6 + a, 10:12] = edge_ref[4, pair]
-            off_ref[i, a, 0:2] = edge_ref[5, pair]
-            off_ref[i, 6 + a, 0:2] = edge_ref[6, pair]
-            off_ref[i, a, 10:12] = edge_ref[7, pair]
+            low = slice(i * 8 + a * 2, i * 8 + a * 2 + 2)
+            high = slice(i * 8 + a * 2 + 4, i * 8 + a * 2 + 6)
+            off_ref[i, 6 + a, 10:12] = edge_ref[4, low]
+            off_ref[i, a, 0:2] = edge_ref[5, high]
+            off_ref[i, 6 + a, 0:2] = edge_ref[6, low]
+            off_ref[i, a, 10:12] = edge_ref[7, high]
     assemble_tables(off_ref, coef_ref, start_ref[0], start_ref[1], start_ref[2], start_ref[3])
     for slot, (da, db, dc) in enumerate(FORWARD):
         if dc:
@@ -359,9 +366,9 @@
         y_ref[a, b, v : 2 * v] = xb_ref[a + 1, b + 1] * (row(coef_ref, 8, a + 1, b + 1) * inverse)
         return carry
 
-    lax.fori_loop(0, 45, first, 0, unroll=3)
+    lax.fori_loop(0, 45, first, 0, unroll=9)
     results = [
-        pltpu.make_async_copy(x, basis_hbm.at[:, :, rows], sems.at[24 + i])
+        pltpu.make_async_copy(x, basis_hbm.at[:, :, rows], sems.at[30 + i])
         for i, (x, rows) in enumerate(
             ((xb_ref.at[1:5, 1:9], slice(0, v)), (y_ref.at[0:4, 0:8], slice(v, 4 * v)))
         )
@@ -399,7 +406,7 @@
         acc_ref[...] += split_dots(left, right, ((1,), (1,)))
         return carry
 
-    lax.fori_loop(0, 16, second, 0)
+    lax.fori_loop(0, 16, second, 0, unroll=4)
 
     n = 4 * v
     acc = acc_ref[...]
@@ -441,7 +448,7 @@
             VMEM((7, 11, v, 128), jnp.float32),
             VMEM((5, 9, 3 * v, 128), jnp.float32),
             VMEM((8 * v, 4 * v), jnp.float32),
-            pltpu.SemaphoreType.DMA((26,)),
+            pltpu.SemaphoreType.DMA((32,)),
         ],
         compiler_params=pltpu.CompilerParams(vmem_limit_bytes=52 * 2**20),
     )(start, block.reshape(-1, 128), prior.reshape(-1, 128), *pieces, off)
@@ -517,17 +524,14 @@
             jnp.int32(total_b),
         ]
     ).astype(jnp.int32)
-    down_a, up_a, down_b, up_b, c_pp, c_mm, c_pm, c_mp = pack_call(block, prior, offsets)
-    pieces = (
-        neighbour(down_a, 1, 0),
-        neighbour(up_a, -1, 0),
-        neighbour(down_b, 0, 1),
-        neighbour(up_b, 0, -1),
-        neighbour(c_pp, 1, 1),
-        neighbour(c_mm, -1, -1),
-        neighbour(c_pm, 1, -1),
-        neighbour(c_mp, -1, 1),
-    )
+    down_a, up_a, down_b, up_b = pack_call(block, prior, offsets)
+    down_b = neighbour(down_b, 0, 1)
+    up_b = neighbour(up_b, 0, -1)
+    down_a = neighbour(down_a, 1, 0)
+    up_a = neighbour(up_a, -1, 0)
+    down_c = neighbour(jnp.concatenate([down_b[:6], up_b[:2]]), 1, 0)
+    up_c = neighbour(jnp.concatenate([down_b[12:], down_b[5:6], up_b[2:3], up_b[1:2]]), -1, 0)
+    pieces = (down_a, up_a, down_b, up_b, down_c, up_c)
     gram, basis = gram_call(start, block, prior, pieces, offsets)
     scale = math.sqrt(total_a * total_b * depth)
     new_block, search = finish_call(scale, spread_sum(gram), basis)

time: 122 us -> 118 us (0.967)
  waiting for transfers between devices: 4.18 us -> 15 us
  starting transfers between devices: 25.1 us -> 18 us
  Pallas kernels: 29 us -> 24.7 us
  blocking collectives: 61.4 us -> 57.9 us
    ppermute x8 -> x6, waiting for transfers between devices: 4.18 us -> 15 us  [neighbour(): return lax.ppermute(payload, ('px', 'pz', 'pc'), pairs)]
    ppermute x8 -> x6, starting transfers between devices: 25.1 us -> 18 us  [neighbour(): return lax.ppermute(payload, ('px', 'pz', 'pc'), pairs)]
    all_to_all x1, blocking collectives: 17.8 us -> 14.5 us  [spread_sum(): part = jnp.sum(lax.all_to_all(pieces, plane, 0, 0), axis=0)]
    pallas_call x1, Pallas kernels: 12.9 us -> 10.7 us  [finish_call(): pl.pallas_call(lambda *refs: finish_kernel(scale, *refs), out_shape=(out,...]
    pallas_call x1, Pallas kernels: 13 us -> 11 us  [gram_call(): pl.pallas_call(gram_kernel, out_shape=(jax.ShapeDtypeStruct((256, 256), j...]
  transfers between devices with their start and end apart: 8 -> 6, of which waited for: 3 -> 3; matrix products, arithmetic and copies ran while one was open for 0% -> 0% of each run, Pallas kernels for 0% -> 0%
where the time goes in v7:
time: 118 us; the launch traced here: 117 us
  blocking collectives  57.9 us (49%)
  Pallas kernels  24.7 us (21%)
  starting transfers between devices  18 us (15%)
  waiting for transfers between devices  15 us (13%)
    all_to_all x1, blocking collectives, spread_sum(): lax.all_to_all(jnp.broadcast_to(part[None], (depth,) + part.shape), 'pz',...  28.1 us
    ppermute x6, starting transfers between devices, neighbour(): return lax.ppermute(payload, ('px', 'pz', 'pc'), pairs)  18 us
    all_to_all x1, blocking collectives, spread_sum(): lax.all_to_all(jnp.broadcast_to(part[None], (count,) + part.shape), plane...  15.3 us
    ppermute x6, waiting for transfers between devices, neighbour(): return lax.ppermute(payload, ('px', 'pz', 'pc'), pairs)  15 us
    all_to_all x1, blocking collectives, spread_sum(): part = jnp.sum(lax.all_to_all(pieces, plane, 0, 0), axis=0)  14.5 us
    pallas_call x1, Pallas kernels, gram_call(): pl.pallas_call(gram_kernel, out_shape=(jax.ShapeDtypeStruct((256, 256), j...  11 us
    pallas_call x1, Pallas kernels, finish_call(): pl.pallas_call(lambda *refs: finish_kernel(scale, *refs), out_shape=(out,...  10.7 us
    pallas_call x1, Pallas kernels, pack_call(): pl.pallas_call(pack_kernel, out_shape=tuple((jax.ShapeDtypeStruct(s, jnp....  2.94 us
  transfers between devices with their start and end apart: 6, of which 3 were waited for; matrix products, arithmetic and copies ran while one was open for 0% of the time, Pallas kernels for 0%

profile of v7, /device:TPU:1, one launch (start us, length us, event | category | flops | bytes accessed | tf_op | source)
XLA Modules:
  0.0 117.4 jit_solution(15881786620425792497)
XLA Ops:
  0.6 2.9 %shard_map.50 = (f32[25,48,128]{2,1,0:T(8,128)}, f32[9,48,128]{2,1,0:T(8,128)}, f32[13,48,128]{2,1,0:T(8,128)}, f32[5,48,128]{2,1,0:T(8,128)}) custom-call(f32[1536,128]{1,0:T(8,128)} %bitcast.9, f32[1536,128]{1,0:T(8,128)} %bitcast.11, f32[3,4,8,128]{3,2,1,0:T(8,128)} %off_own.1), custom_call_target="tpu_custom_call" | custom-call | tf_op jit(solution)/shard_map/pallas_call | solution.py:265
  3.6 4.9 %collective-permute-start.3 = (f32[5,48,128]{2,1,0:T(8,128)}, f32[5,48,128]{2,1,0:T(8,128)S(1)}, u32[]{:S(2)}, u32[]{:S(2)}) collective-permute-start(f32[5,48,128]{2,1,0:T(8,128)} %get-tuple-element.13), channel_id=1, source_target_pairs={{0,1},{1,2},{2,3},{3,4},{4,5},{5,6},{6,7},{7,8},{8,9},{9,10},{10,1... | collective-permute-start | bytes 368648 | tf_op jit(solution)/shard_map/ppermute | solution.py:512
  8.5 5.1 %collective-permute-start.2 = (f32[13,48,128]{2,1,0:T(8,128)}, f32[13,48,128]{2,1,0:T(8,128)S(1)}, u32[]{:S(2)}, u32[]{:S(2)}) collective-permute-start(f32[13,48,128]{2,1,0:T(8,128)} %get-tuple-element.12), channel_id=1, source_target_pairs={{1,0},{2,1},{3,2},{4,3},{5,4},{6,5},{7,6},{8,7},{9,8},{10,9},{11,1... | collective-permute-start | bytes 958472 | tf_op jit(solution)/shard_map/ppermute | solution.py:512
  13.7 1.3 %collective-permute-start.1 = (f32[9,48,128]{2,1,0:T(8,128)}, f32[9,48,128]{2,1,0:T(8,128)S(1)}, u32[]{:S(2)}, u32[]{:S(2)}) collective-permute-start(f32[9,48,128]{2,1,0:T(8,128)} %get-tuple-element.11), channel_id=1, source_target_pairs={{0,32},{1,33},{2,34},{3,35},{4,36},{5,37},{6,38},{7,39},{8,40},{9,... | collective-permute-start | bytes 663560 | tf_op jit(solution)/shard_map/ppermute | solution.py:512
  15.0 1.3 %collective-permute-start = (f32[25,48,128]{2,1,0:T(8,128)}, f32[25,48,128]{2,1,0:T(8,128)S(1)}, u32[]{:S(2)}, u32[]{:S(2)}) collective-permute-start(f32[25,48,128]{2,1,0:T(8,128)} %get-tuple-element.10), channel_id=1, source_target_pairs={{32,0},{33,1},{34,2},{35,3},{36,4},{37,5},{38,6},{39,7},{40,8},{41... | collective-permute-start | bytes 1843208 | tf_op jit(solution)/shard_map/ppermute | solution.py:512
  16.3 0.0 collective-permute-done.3.up_b
  16.3 0.7 collective-permute-done.2.down_b
  17.1 1.3 %collective-permute-start.4 = (f32[8,48,128]{2,1,0:T(8,128)S(1)}, f32[8,48,128]{2,1,0:T(8,128)S(1)}, u32[]{:S(2)}, u32[]{:S(2)}) collective-permute-start(f32[8,48,128]{2,1,0:T(8,128)S(1)} %pad_maximum_fusion), channel_id=1, source_target_pairs={{32,0},{33,1},{34,2},{35,3},{36,4},{37,5},{38,6},{39,7},{40,8},{41... | collective-permute-start | bytes 589832 | tf_op jit(solution)/shard_map/ppermute | solution.py:512
  18.4 4.0 %collective-permute-start.5 = (f32[4,48,128]{2,1,0:T(8,128)S(1)}, f32[4,48,128]{2,1,0:T(8,128)S(1)}, u32[]{:S(2)}, u32[]{:S(2)}) collective-permute-start(f32[4,48,128]{2,1,0:T(8,128)S(1)} %pad_maximum_fusion.1), channel_id=1, source_target_pairs={{0,32},{1,33},{2,34},{3,35},{4,36},{5,37},{6,38},{7,39},{8,40},{9,... | collective-permute-start | bytes 294920 | tf_op jit(solution)/shard_map/ppermute | solution.py:512
  22.4 0.1 pad_add_fusion.start_ref
  22.5 0.0 collective-permute-done.1.up_a
  22.5 2.5 %collective-permute-done.5.up_c = f32[4,48,128]{2,1,0:T(8,128)S(1)} collective-permute-done((f32[4,48,128]{2,1,0:T(8,128)S(1)}, f32[4,48,128]{2,1,0:T(8,128)S(1)}, u32[]{:S(2)}, u32[]{:S(2)}) %collective-permute-start.5) | collective-permute-done | bytes 98336 | tf_op jit(solution)/shard_map/ppermute | solution.py:512
  25.0 11.8 %collective-permute-done.4.down_c = f32[8,48,128]{2,1,0:T(8,128)S(1)} collective-permute-done((f32[8,48,128]{2,1,0:T(8,128)S(1)}, f32[8,48,128]{2,1,0:T(8,128)S(1)}, u32[]{:S(2)}, u32[]{:S(2)}) %collective-permute-start.4) | collective-permute-done | bytes 196640 | tf_op jit(solution)/shard_map/ppermute | solution.py:512
  36.8 0.0 collective-permute-done.down_a
  36.8 0.0 copy-start
  36.8 0.8 copy-done
  37.6 11.0 %shard_map.51 = (f32[256,256]{1,0:T(8,128)S(1)}, f32[4,8,192,128]{3,2,1,0:T(8,128)}) custom-call(s32[4]{0:T(128)S(1)} %pad_add_fusion.start_ref, f32[1536,128]{1,0:T(8,128)} %bitcast.10, f32[1536,128]{1,0:T(8,128)} %bitcast.12, f32[25,48,128]{2,1,0:T(8,128)S(1)} %collective-permute-done.down_a, f32[9,48,128]{2,1,0:T(8,128)S(1)} %collective-permute-done.1.up_a, ...), custom_call_target="tpu_custom_call" | custom-call | tf_op jit(solution)/shard_map/pallas_call | solution.py:431
  48.7 14.5 %all_to_all.15 = f32[32,8,256]{2,1,0:T(8,128)S(1)} all-to-all(f32[32,8,256]{2,1,0:T(8,128)S(1)} %bitcast.8), channel_id=1, replica_groups=mesh['px'=16,'pz'=16,'pc'=2] {'px','pc'}, dimensions={0} | all-to-all | bytes 524288 | tf_op jit(solution)/shard_map/all_to_all | solution.py:496
  63.2 28.1 %all_to_all.16 = f32[16,8,256]{2,1,0:T(8,128)S(1)} all-to-all(f32[16,8,256]{2,1,0:T(8,128)S(1)} %broadcast_in_dim.4), channel_id=1, replica_groups=mesh['px'=16,'pz'=16,'pc'=2] {'pz'}, dimensions={0} | all-to-all | bytes 262144 | tf_op jit(solution)/shard_map/all_to_all | solution.py:498
  91.4 15.3 %all_to_all.17 = f32[32,8,256]{2,1,0:T(8,128)} all-to-all(f32[32,8,256]{2,1,0:T(8,128)S(1)} %broadcast_in_dim.5), channel_id=1, replica_groups=mesh['px'=16,'pz'=16,'pc'=2] {'px','pc'}, dimensions={0} | all-to-all | bytes 524288 | tf_op jit(solution)/shard_map/all_to_all | solution.py:500
  106.7 10.7 %shard_map.52 = (f32[1536,128]{1,0:T(8,128)}, f32[1536,128]{1,0:T(8,128)}) custom-call(f32[256,256]{1,0:T(8,128)} %bitcast.13, f32[4,8,192,128]{3,2,1,0:T(8,128)} %get-tuple-element.15.refs_1_), custom_call_target="tpu_custom_call" | custom-call | tf_op jit(solution)/shard_map/pallas_call | solution.py:481
  (10 shorter events, 0.1 us)
Async XLA Ops:
  3.6 12.7 %collective-permute-start.3 = (f32[5,48,128]{2,1,0:T(8,128)}, f32[5,48,128]{2,1,0:T(8,128)S(1)}, u32[]{:S(2)}, u32[]{:S(2)}) collective-permute-start(f32[5,48,128]{2,1,0:T(8,128)} %get-tuple-element.13), channel_id=1, source_target_pairs={{0,1},{1,2},{2,3},{3,4},{4,5},{5,6},{6,7},{7,8},{8,9},{9,10},{10,1... | collective-permute-start | bytes 368648 | tf_op jit(solution)/shard_map/ppermute | solution.py:512
  8.5 8.5 %collective-permute-start.2 = (f32[13,48,128]{2,1,0:T(8,128)}, f32[13,48,128]{2,1,0:T(8,128)S(1)}, u32[]{:S(2)}, u32[]{:S(2)}) collective-permute-start(f32[13,48,128]{2,1,0:T(8,128)} %get-tuple-element.12), channel_id=1, source_target_pairs={{1,0},{2,1},{3,2},{4,3},{5,4},{6,5},{7,6},{8,7},{9,8},{10,9},{11,1... | collective-permute-start | bytes 958472 | tf_op jit(solution)/shard_map/ppermute | solution.py:512
  13.7 8.9 %collective-permute-start.1 = (f32[9,48,128]{2,1,0:T(8,128)}, f32[9,48,128]{2,1,0:T(8,128)S(1)}, u32[]{:S(2)}, u32[]{:S(2)}) collective-permute-start(f32[9,48,128]{2,1,0:T(8,128)} %get-tuple-element.11), channel_id=1, source_target_pairs={{0,32},{1,33},{2,34},{3,35},{4,36},{5,37},{6,38},{7,39},{8,40},{9,... | collective-permute-start | bytes 663560 | tf_op jit(solution)/shard_map/ppermute | solution.py:512
  15.0 21.9 %collective-permute-start = (f32[25,48,128]{2,1,0:T(8,128)}, f32[25,48,128]{2,1,0:T(8,128)S(1)}, u32[]{:S(2)}, u32[]{:S(2)}) collective-permute-start(f32[25,48,128]{2,1,0:T(8,128)} %get-tuple-element.10), channel_id=1, source_target_pairs={{32,0},{33,1},{34,2},{35,3},{36,4},{37,5},{38,6},{39,7},{40,8},{41... | collective-permute-start | bytes 1843208 | tf_op jit(solution)/shard_map/ppermute | solution.py:512
  17.1 19.8 %collective-permute-start.4 = (f32[8,48,128]{2,1,0:T(8,128)S(1)}, f32[8,48,128]{2,1,0:T(8,128)S(1)}, u32[]{:S(2)}, u32[]{:S(2)}) collective-permute-start(f32[8,48,128]{2,1,0:T(8,128)S(1)} %pad_maximum_fusion), channel_id=1, source_target_pairs={{32,0},{33,1},{34,2},{35,3},{36,4},{37,5},{38,6},{39,7},{40,8},{41... | collective-permute-start | bytes 589832 | tf_op jit(solution)/shard_map/ppermute | solution.py:512
  18.4 6.6 %collective-permute-start.5 = (f32[4,48,128]{2,1,0:T(8,128)S(1)}, f32[4,48,128]{2,1,0:T(8,128)S(1)}, u32[]{:S(2)}, u32[]{:S(2)}) collective-permute-start(f32[4,48,128]{2,1,0:T(8,128)S(1)} %pad_maximum_fusion.1), channel_id=1, source_target_pairs={{0,32},{1,33},{2,34},{3,35},{4,36},{5,37},{6,38},{7,39},{8,40},{9,... | collective-permute-start | bytes 294920 | tf_op jit(solution)/shard_map/ppermute | solution.py:512
  36.8 0.8 copy-start

commit v8 on v7

--- a/solution.py
+++ b/solution.py
@@ -217,13 +217,8 @@
         low = high
 
 
-DOWN_B = [(0, 0), (0, 1), (1, 0), (1, 1)]
-REST_B = [(2, 0), (2, 1), (3, 1), (3, 0)]
-UP_B = {0: 0, 3: 2, 1: 3, 2: 4}
-
-
-def place_b(a, b):
-    return DOWN_B.index((a, b)) if (a, b) in DOWN_B else 9 + REST_B.index((a, b))
+DOWN_A = [(0, 0), (0, 1), (1, 0), (1, 1), None, None, (0, 7)]
+DOWN_A += [(0, b) for b in range(2, 7)] + [(1, b) for b in range(2, 8)]
 
 
 def pack_kernel(block_ref, prior_ref, off_ref, down_a, up_a, down_b, up_b):
@@ -238,24 +233,24 @@
             if a == 0 or b == 0:
                 y = prior(a, b)
             if a < 2:
-                down_a[a * 8 + b] = x
+                down_a[DOWN_A.index((a, b))] = x
             if a == 0:
-                down_a[16 + b] = y
+                down_a[17 + b if b else 4] = y
             if a == 3:
-                up_a[b] = x
+                up_a[0 if b == 0 else 2 if b == 7 else 2 + b] = x
             if b < 2:
-                down_b[place_b(a, b)] = x
+                down_b[b * 4 + a] = x
             if b == 0:
-                down_b[4 if a == 0 else 5 + a] = y
+                down_b[8 + a] = y
             if b == 7:
-                up_b[UP_B[a]] = x
+                up_b[a] = x
     for i in range(3):
         for a in range(4):
-            down_b[5, i * 8 + a * 2 : i * 8 + a * 2 + 2] = off_ref[i, a, 0:2]
-            up_b[1, i * 8 + a * 2 : i * 8 + a * 2 + 2] = off_ref[i, a, 6:8]
+            down_b[12, i * 8 + a * 2 : i * 8 + a * 2 + 2] = off_ref[i, a, 0:2]
+            up_b[4, i * 8 + a * 2 : i * 8 + a * 2 + 2] = off_ref[i, a, 6:8]
         for a in range(2):
-            down_a[24, i * 16 + a * 8 : i * 16 + a * 8 + 8] = off_ref[i, a]
-            up_a[8, i * 16 + a * 8 : i * 16 + a * 8 + 8] = off_ref[i, 2 + a]
+            down_a[5, i * 16 + a * 8 : i * 16 + a * 8 + 8] = off_ref[i, a]
+            up_a[1, i * 16 + a * 8 : i * 16 + a * 8 + 8] = off_ref[i, 2 + a]
 
 
 def pack_call(block, prior, offsets):
@@ -275,31 +270,31 @@
                 gram_ref, basis_hbm, block_ref, prior_ref, edge_ref, off_ref, coef_ref, turn_ref, xb_ref, y_ref, acc_ref,
                 sems):
     v = VECS
-    edges = (down_a.at[24], up_a.at[8], down_b.at[5], up_b.at[1],
-             down_c.at[5], up_c.at[3], down_c.at[7], up_c.at[1])
+    edges = (down_a.at[5], up_a.at[1], down_b.at[12], up_b.at[4],
+             down_c.at[5], up_c.at[3], up_c.at[1], down_c.at[7])
     moves = [(piece, edge_ref.at[i]) for i, piece in enumerate(edges)]
     third = slice(2 * v, 3 * v)
     moves += [(block_hbm, block_ref), (prior_hbm, prior_ref)]
     moves += [
-        (down_a.at[0:8], xb_ref.at[5, 1:9]),
-        (down_a.at[8:16], xb_ref.at[6, 1:9]),
-        (up_a.at[0:8], xb_ref.at[0, 1:9]),
-        (down_b.at[0:2], xb_ref.at[1, 9:11]),
-        (down_b.at[2:4], xb_ref.at[2, 9:11]),
-        (down_b.at[9:11], xb_ref.at[3, 9:11]),
-        (down_b.at[11], xb_ref.at[4, 10]),
-        (down_b.at[12], xb_ref.at[4, 9]),
-        (up_b.at[0], xb_ref.at[1, 0]),
-        (up_b.at[3:5], xb_ref.at[2:4, 0]),
-        (up_b.at[2], xb_ref.at[4, 0]),
+        (down_a.at[0:2], xb_ref.at[5, 1:3]),
+        (down_a.at[2:4], xb_ref.at[6, 1:3]),
+        (down_a.at[6], xb_ref.at[5, 8]),
+        (down_a.at[7:12], xb_ref.at[5, 3:8]),
+        (down_a.at[12:18], xb_ref.at[6, 3:9]),
+        (up_a.at[0], xb_ref.at[0, 1]),
+        (up_a.at[2], xb_ref.at[0, 8]),
+        (up_a.at[3:9], xb_ref.at[0, 2:8]),
+        (down_b.at[0:4], xb_ref.at[1:5, 9]),
+        (down_b.at[4:8], xb_ref.at[1:5, 10]),
+        (up_b.at[0:4], xb_ref.at[1:5, 0]),
         (down_c.at[0:2], xb_ref.at[5, 9:11]),
         (down_c.at[2:4], xb_ref.at[6, 9:11]),
+        (down_c.at[6], xb_ref.at[0, 9]),
+        (up_c.at[0], xb_ref.at[5, 0]),
         (up_c.at[2], xb_ref.at[0, 0]),
-        (down_c.at[6], xb_ref.at[5, 0]),
-        (up_c.at[0], xb_ref.at[0, 9]),
-        (down_a.at[16:24], y_ref.at[4, 0:8, third]),
-        (down_b.at[4], y_ref.at[0, 8, third]),
-        (down_b.at[6:9], y_ref.at[1:4, 8, third]),
+        (down_a.at[4], y_ref.at[4, 0, third]),
+        (down_a.at[18:25], y_ref.at[4, 1:8, third]),
+        (down_b.at[8:12], y_ref.at[0:4, 8, third]),
         (down_c.at[4], y_ref.at[4, 8, third]),
     ]
     copies = [pltpu.make_async_copy(x, y, sems.at[i]) for i, (x, y) in enumerate(moves)]
@@ -324,12 +319,12 @@
             rows = slice(i * 16 + a * 8, i * 16 + a * 8 + 8)
             off_ref[i, 6 + a, 2:10] = edge_ref[0, rows]
             off_ref[i, a, 2:10] = edge_ref[1, rows]
-            low = slice(i * 8 + a * 2, i * 8 + a * 2 + 2)
-            high = slice(i * 8 + a * 2 + 4, i * 8 + a * 2 + 6)
+            low = slice(i * 16 + a * 8, i * 16 + a * 8 + 2)
+            high = slice(i * 16 + a * 8 + 6, i * 16 + a * 8 + 8)
             off_ref[i, 6 + a, 10:12] = edge_ref[4, low]
             off_ref[i, a, 0:2] = edge_ref[5, high]
-            off_ref[i, 6 + a, 0:2] = edge_ref[6, low]
-            off_ref[i, a, 10:12] = edge_ref[7, high]
+            off_ref[i, 6 + a, 0:2] = edge_ref[6, high]
+            off_ref[i, a, 10:12] = edge_ref[7, low]
     assemble_tables(off_ref, coef_ref, start_ref[0], start_ref[1], start_ref[2], start_ref[3])
     for slot, (da, db, dc) in enumerate(FORWARD):
         if dc:
@@ -529,8 +524,8 @@
     up_b = neighbour(up_b, 0, -1)
     down_a = neighbour(down_a, 1, 0)
     up_a = neighbour(up_a, -1, 0)
-    down_c = neighbour(jnp.concatenate([down_b[:6], up_b[:2]]), 1, 0)
-    up_c = neighbour(jnp.concatenate([down_b[12:], down_b[5:6], up_b[2:3], up_b[1:2]]), -1, 0)
+    down_c = neighbour(jnp.concatenate([down_a[:6], up_a[:2]]), 0, 1)
+    up_c = neighbour(jnp.concatenate([down_a[6:7], down_a[5:6], up_a[2:3], up_a[1:2]]), 0, -1)
     pieces = (down_a, up_a, down_b, up_b, down_c, up_c)
     gram, basis = gram_call(start, block, prior, pieces, offsets)
     scale = math.sqrt(total_a * total_b * depth)

time: 118 us -> 115 us (0.975)
  waiting for transfers between devices: 15 us -> 1.55 us
  starting transfers between devices: 18 us -> 24.4 us
  blocking collectives: 57.9 us -> 61.9 us
    ppermute x6, waiting for transfers between devices: 15 us -> 1.55 us  [neighbour(): return lax.ppermute(payload, ('px', 'pz', 'pc'), pairs)]
    ppermute x6, starting transfers between devices: 18 us -> 24.4 us  [neighbour(): return lax.ppermute(payload, ('px', 'pz', 'pc'), pairs)]
    all_to_all x1, blocking collectives: 14.5 us -> 17.7 us  [spread_sum(): part = jnp.sum(lax.all_to_all(pieces, plane, 0, 0), axis=0)]
  transfers between devices with their start and end apart: 6 -> 6, of which waited for: 3 -> 1; matrix products, arithmetic and copies ran while one was open for 0% -> 0% of each run, Pallas kernels for 0% -> 0%
where the time goes in v8:
time: 115 us; the launch traced here: 114 us
  blocking collectives  61.9 us (54%)
  Pallas kernels  24.6 us (21%)
  starting transfers between devices  24.4 us (21%)
  waiting for transfers between devices  1.55 us (1%)
    all_to_all x1, blocking collectives, spread_sum(): lax.all_to_all(jnp.broadcast_to(part[None], (depth,) + part.shape), 'pz',...  28.9 us
    ppermute x6, starting transfers between devices, neighbour(): return lax.ppermute(payload, ('px', 'pz', 'pc'), pairs)  24.4 us
    all_to_all x1, blocking collectives, spread_sum(): part = jnp.sum(lax.all_to_all(pieces, plane, 0, 0), axis=0)  17.7 us
    all_to_all x1, blocking collectives, spread_sum(): lax.all_to_all(jnp.broadcast_to(part[None], (count,) + part.shape), plane...  15.3 us
    pallas_call x1, Pallas kernels, gram_call(): pl.pallas_call(gram_kernel, out_shape=(jax.ShapeDtypeStruct((256, 256), j...  10.9 us
    pallas_call x1, Pallas kernels, finish_call(): pl.pallas_call(lambda *refs: finish_kernel(scale, *refs), out_shape=(out,...  10.7 us
    pallas_call x1, Pallas kernels, pack_call(): pl.pallas_call(pack_kernel, out_shape=tuple((jax.ShapeDtypeStruct(s, jnp....  2.94 us
  transfers between devices with their start and end apart: 6, of which 1 were waited for; matrix products, arithmetic and copies ran while one was open for 0% of the time, Pallas kernels for 0%

profile of v8, /device:TPU:1, one launch (start us, length us, event | category | flops | bytes accessed | tf_op | source)
XLA Modules:
  0.0 114.3 jit_solution(13559872377223038190)
XLA Ops:
  0.6 2.9 %shard_map.50 = (f32[25,48,128]{2,1,0:T(8,128)}, f32[9,48,128]{2,1,0:T(8,128)}, f32[13,48,128]{2,1,0:T(8,128)}, f32[5,48,128]{2,1,0:T(8,128)}) custom-call(f32[1536,128]{1,0:T(8,128)} %bitcast.9, f32[1536,128]{1,0:T(8,128)} %bitcast.11, f32[3,4,8,128]{3,2,1,0:T(8,128)} %off_own.1), custom_call_target="tpu_custom_call" | custom-call | tf_op jit(solution)/shard_map/pallas_call | solution.py:260
  3.6 1.3 %collective-permute-start = (f32[25,48,128]{2,1,0:T(8,128)}, f32[25,48,128]{2,1,0:T(8,128)S(1)}, u32[]{:S(2)}, u32[]{:S(2)}) collective-permute-start(f32[25,48,128]{2,1,0:T(8,128)} %get-tuple-element.10), channel_id=1, source_target_pairs={{32,0},{33,1},{34,2},{35,3},{36,4},{37,5},{38,6},{39,7},{40,8},{41... | collective-permute-start | bytes 1843208 | tf_op jit(solution)/shard_map/ppermute | solution.py:507
  4.9 4.6 %collective-permute-start.1 = (f32[9,48,128]{2,1,0:T(8,128)}, f32[9,48,128]{2,1,0:T(8,128)S(1)}, u32[]{:S(2)}, u32[]{:S(2)}) collective-permute-start(f32[9,48,128]{2,1,0:T(8,128)} %get-tuple-element.11), channel_id=1, source_target_pairs={{0,32},{1,33},{2,34},{3,35},{4,36},{5,37},{6,38},{7,39},{8,40},{9,... | collective-permute-start | bytes 663560 | tf_op jit(solution)/shard_map/ppermute | solution.py:507
  9.4 4.9 %collective-permute-start.3 = (f32[5,48,128]{2,1,0:T(8,128)}, f32[5,48,128]{2,1,0:T(8,128)S(1)}, u32[]{:S(2)}, u32[]{:S(2)}) collective-permute-start(f32[5,48,128]{2,1,0:T(8,128)} %get-tuple-element.13), channel_id=1, source_target_pairs={{0,1},{1,2},{2,3},{3,4},{4,5},{5,6},{6,7},{7,8},{8,9},{9,10},{10,1... | collective-permute-start | bytes 368648 | tf_op jit(solution)/shard_map/ppermute | solution.py:507
  14.4 5.1 %collective-permute-start.2 = (f32[13,48,128]{2,1,0:T(8,128)}, f32[13,48,128]{2,1,0:T(8,128)S(1)}, u32[]{:S(2)}, u32[]{:S(2)}) collective-permute-start(f32[13,48,128]{2,1,0:T(8,128)} %get-tuple-element.12), channel_id=1, source_target_pairs={{1,0},{2,1},{3,2},{4,3},{5,4},{6,5},{7,6},{8,7},{9,8},{10,9},{11,1... | collective-permute-start | bytes 958472 | tf_op jit(solution)/shard_map/ppermute | solution.py:507
  19.5 0.0 collective-permute-done.1.up_a
  19.6 0.0 collective-permute-done.down_a
  19.6 5.0 %collective-permute-start.4 = (f32[8,48,128]{2,1,0:T(8,128)S(1)}, f32[8,48,128]{2,1,0:T(8,128)S(1)}, u32[]{:S(2)}, u32[]{:S(2)}) collective-permute-start(f32[8,48,128]{2,1,0:T(8,128)S(1)} %pad_maximum_fusion), channel_id=1, source_target_pairs={{1,0},{2,1},{3,2},{4,3},{5,4},{6,5},{7,6},{8,7},{9,8},{10,9},{11,1... | collective-permute-start | bytes 589832 | tf_op jit(solution)/shard_map/ppermute | solution.py:507
  24.7 3.5 %collective-permute-start.5 = (f32[4,48,128]{2,1,0:T(8,128)S(1)}, f32[4,48,128]{2,1,0:T(8,128)S(1)}, u32[]{:S(2)}, u32[]{:S(2)}) collective-permute-start(f32[4,48,128]{2,1,0:T(8,128)S(1)} %pad_maximum_fusion.1), channel_id=1, source_target_pairs={{0,1},{1,2},{2,3},{3,4},{4,5},{5,6},{6,7},{7,8},{8,9},{9,10},{10,1... | collective-permute-start | bytes 294920 | tf_op jit(solution)/shard_map/ppermute | solution.py:507
  28.2 0.1 pad_add_fusion.start_ref
  28.3 0.0 collective-permute-done.3.up_b
  28.3 0.0 collective-permute-done.2.down_b
  28.3 1.5 %collective-permute-done.5.up_c = f32[4,48,128]{2,1,0:T(8,128)S(1)} collective-permute-done((f32[4,48,128]{2,1,0:T(8,128)S(1)}, f32[4,48,128]{2,1,0:T(8,128)S(1)}, u32[]{:S(2)}, u32[]{:S(2)}) %collective-permute-start.5) | collective-permute-done | bytes 98336 | tf_op jit(solution)/shard_map/ppermute | solution.py:507
  29.8 0.0 collective-permute-done.4.down_c
  29.8 0.0 copy-start
  29.8 0.8 copy-done
  30.6 10.9 %shard_map.51 = (f32[256,256]{1,0:T(8,128)S(1)}, f32[4,8,192,128]{3,2,1,0:T(8,128)}) custom-call(s32[4]{0:T(128)S(1)} %pad_add_fusion.start_ref, f32[1536,128]{1,0:T(8,128)} %bitcast.10, f32[1536,128]{1,0:T(8,128)} %bitcast.12, f32[25,48,128]{2,1,0:T(8,128)S(1)} %collective-permute-done.down_a, f32[9,48,128]{2,1,0:T(8,128)S(1)} %collective-permute-done.1.up_a, ...), custom_call_target="tpu_custom_call" | custom-call | tf_op jit(solution)/shard_map/pallas_call | solution.py:426
  41.5 17.7 %all_to_all.15 = f32[32,8,256]{2,1,0:T(8,128)S(1)} all-to-all(f32[32,8,256]{2,1,0:T(8,128)S(1)} %bitcast.8), channel_id=1, replica_groups=mesh['px'=16,'pz'=16,'pc'=2] {'px','pc'}, dimensions={0} | all-to-all | bytes 524288 | tf_op jit(solution)/shard_map/all_to_all | solution.py:491
  59.3 28.9 %all_to_all.16 = f32[16,8,256]{2,1,0:T(8,128)S(1)} all-to-all(f32[16,8,256]{2,1,0:T(8,128)S(1)} %broadcast_in_dim.4), channel_id=1, replica_groups=mesh['px'=16,'pz'=16,'pc'=2] {'pz'}, dimensions={0} | all-to-all | bytes 262144 | tf_op jit(solution)/shard_map/all_to_all | solution.py:493
  88.3 15.3 %all_to_all.17 = f32[32,8,256]{2,1,0:T(8,128)} all-to-all(f32[32,8,256]{2,1,0:T(8,128)S(1)} %broadcast_in_dim.5), channel_id=1, replica_groups=mesh['px'=16,'pz'=16,'pc'=2] {'px','pc'}, dimensions={0} | all-to-all | bytes 524288 | tf_op jit(solution)/shard_map/all_to_all | solution.py:495
  103.5 10.7 %shard_map.52 = (f32[1536,128]{1,0:T(8,128)}, f32[1536,128]{1,0:T(8,128)}) custom-call(f32[256,256]{1,0:T(8,128)} %bitcast.13, f32[4,8,192,128]{3,2,1,0:T(8,128)} %get-tuple-element.15.refs_1_), custom_call_target="tpu_custom_call" | custom-call | tf_op jit(solution)/shard_map/pallas_call | solution.py:476
  (10 shorter events, 0.1 us)
Async XLA Ops:
  3.6 16.0 %collective-permute-start = (f32[25,48,128]{2,1,0:T(8,128)}, f32[25,48,128]{2,1,0:T(8,128)S(1)}, u32[]{:S(2)}, u32[]{:S(2)}) collective-permute-start(f32[25,48,128]{2,1,0:T(8,128)} %get-tuple-element.10), channel_id=1, source_target_pairs={{32,0},{33,1},{34,2},{35,3},{36,4},{37,5},{38,6},{39,7},{40,8},{41... | collective-permute-start | bytes 1843208 | tf_op jit(solution)/shard_map/ppermute | solution.py:507
  4.9 14.7 %collective-permute-start.1 = (f32[9,48,128]{2,1,0:T(8,128)}, f32[9,48,128]{2,1,0:T(8,128)S(1)}, u32[]{:S(2)}, u32[]{:S(2)}) collective-permute-start(f32[9,48,128]{2,1,0:T(8,128)} %get-tuple-element.11), channel_id=1, source_target_pairs={{0,32},{1,33},{2,34},{3,35},{4,36},{5,37},{6,38},{7,39},{8,40},{9,... | collective-permute-start | bytes 663560 | tf_op jit(solution)/shard_map/ppermute | solution.py:507
  9.4 18.8 %collective-permute-start.3 = (f32[5,48,128]{2,1,0:T(8,128)}, f32[5,48,128]{2,1,0:T(8,128)S(1)}, u32[]{:S(2)}, u32[]{:S(2)}) collective-permute-start(f32[5,48,128]{2,1,0:T(8,128)} %get-tuple-element.13), channel_id=1, source_target_pairs={{0,1},{1,2},{2,3},{3,4},{4,5},{5,6},{6,7},{7,8},{8,9},{9,10},{10,1... | collective-permute-start | bytes 368648 | tf_op jit(solution)/shard_map/ppermute | solution.py:507
  14.4 13.9 %collective-permute-start.2 = (f32[13,48,128]{2,1,0:T(8,128)}, f32[13,48,128]{2,1,0:T(8,128)S(1)}, u32[]{:S(2)}, u32[]{:S(2)}) collective-permute-start(f32[13,48,128]{2,1,0:T(8,128)} %get-tuple-element.12), channel_id=1, source_target_pairs={{1,0},{2,1},{3,2},{4,3},{5,4},{6,5},{7,6},{8,7},{9,8},{10,9},{11,1... | collective-permute-start | bytes 958472 | tf_op jit(solution)/shard_map/ppermute | solution.py:507
  19.6 10.2 %collective-permute-start.4 = (f32[8,48,128]{2,1,0:T(8,128)S(1)}, f32[8,48,128]{2,1,0:T(8,128)S(1)}, u32[]{:S(2)}, u32[]{:S(2)}) collective-permute-start(f32[8,48,128]{2,1,0:T(8,128)S(1)} %pad_maximum_fusion), channel_id=1, source_target_pairs={{1,0},{2,1},{3,2},{4,3},{5,4},{6,5},{7,6},{8,7},{9,8},{10,9},{11,1... | collective-permute-start | bytes 589832 | tf_op jit(solution)/shard_map/ppermute | solution.py:507
  24.7 5.1 %collective-permute-start.5 = (f32[4,48,128]{2,1,0:T(8,128)S(1)}, f32[4,48,128]{2,1,0:T(8,128)S(1)}, u32[]{:S(2)}, u32[]{:S(2)}) collective-permute-start(f32[4,48,128]{2,1,0:T(8,128)S(1)} %pad_maximum_fusion.1), channel_id=1, source_target_pairs={{0,1},{1,2},{2,3},{3,4},{4,5},{5,6},{6,7},{7,8},{8,9},{9,10},{10,1... | collective-permute-start | bytes 294920 | tf_op jit(solution)/shard_map/ppermute | solution.py:507
  29.8 0.8 copy-start

commit v9 on v8

--- a/solution.py
+++ b/solution.py
@@ -266,8 +266,8 @@
     )(block.reshape(-1, 128), prior.reshape(-1, 128), offsets)
 
 
-def gram_kernel(start_ref, block_hbm, prior_hbm, down_a, up_a, down_b, up_b, down_c, up_c, off_own,
-                gram_ref, basis_hbm, block_ref, prior_ref, edge_ref, off_ref, coef_ref, turn_ref, xb_ref, y_ref, acc_ref,
+def gram_kernel(start_ref, block_hbm, prior_hbm, down_a, up_a, down_b, up_b, down_c, up_c, off_hbm,
+                gram_ref, basis_hbm, block_ref, prior_ref, off_own, edge_ref, off_ref, coef_ref, turn_ref, xb_ref, y_ref, acc_ref,
                 sems):
     v = VECS
     edges = (down_a.at[5], up_a.at[1], down_b.at[12], up_b.at[4],
@@ -298,6 +298,8 @@
         (down_c.at[4], y_ref.at[4, 8, third]),
     ]
     copies = [pltpu.make_async_copy(x, y, sems.at[i]) for i, (x, y) in enumerate(moves)]
+    own_offsets = pltpu.make_async_copy(off_hbm, off_own, sems.at[32])
+    own_offsets.start()
     for copy in copies:
         copy.start()
     for copy in copies[8:10]:
@@ -307,6 +309,7 @@
             rows = pl.ds(a * 8 + b, v, stride=32)
             xb_ref[a + 1, b + 1] = block_ref[rows, :]
             y_ref[a, b, third] = prior_ref[rows, :]
+    own_offsets.wait()
     for copy in copies[:8]:
         copy.wait()
     for i in range(3):
@@ -401,7 +404,7 @@
         acc_ref[...] += split_dots(left, right, ((1,), (1,)))
         return carry
 
-    lax.fori_loop(0, 16, second, 0, unroll=4)
+    lax.fori_loop(0, 16, second, 0, unroll=8)
 
     n = 4 * v
     acc = acc_ref[...]
@@ -430,12 +433,12 @@
             jax.ShapeDtypeStruct((4, 8, 4 * v, 128), jnp.float32),
         ),
         in_specs=[pl.BlockSpec(memory_space=pltpu.SMEM)]
-        + [pl.BlockSpec(memory_space=pl.ANY)] * (2 + len(pieces))
-        + [spec],
+        + [pl.BlockSpec(memory_space=pl.ANY)] * (3 + len(pieces)),
         out_specs=(spec, pl.BlockSpec(memory_space=pl.ANY)),
         scratch_shapes=[
             VMEM((32 * v, 128), jnp.float32),
             VMEM((32 * v, 128), jnp.float32),
+            VMEM((3, 4, 8, 128), jnp.float32),
             VMEM((8, v, 128), jnp.float32),
             VMEM((3, 8, 16, 128), jnp.float32),
             VMEM((9, 6, 16, 128), jnp.float32),
@@ -443,7 +446,7 @@
             VMEM((7, 11, v, 128), jnp.float32),
             VMEM((5, 9, 3 * v, 128), jnp.float32),
             VMEM((8 * v, 4 * v), jnp.float32),
-            pltpu.SemaphoreType.DMA((32,)),
+            pltpu.SemaphoreType.DMA((33,)),
         ],
         compiler_params=pltpu.CompilerParams(vmem_limit_bytes=52 * 2**20),
     )(start, block.reshape(-1, 128), prior.reshape(-1, 128), *pieces, off)

time: 115 us -> 114 us (level)
  no operation moved by 1% of the time
where the time goes in v9:
time: 114 us
  blocking collectives  61.9 us (54%)
  starting transfers between devices  24.4 us (21%)
  Pallas kernels  24.2 us (21%)
  waiting for transfers between devices  1.55 us (1%)
    all_to_all x1, blocking collectives, spread_sum(): lax.all_to_all(jnp.broadcast_to(part[None], (depth,) + part.shape), 'pz',...  28.9 us
    ppermute x6, starting transfers between devices, neighbour(): return lax.ppermute(payload, ('px', 'pz', 'pc'), pairs)  24.4 us
    all_to_all x1, blocking collectives, spread_sum(): part = jnp.sum(lax.all_to_all(pieces, plane, 0, 0), axis=0)  17.7 us
    all_to_all x1, blocking collectives, spread_sum(): lax.all_to_all(jnp.broadcast_to(part[None], (count,) + part.shape), plane...  15.3 us
    pallas_call x1, Pallas kernels, finish_call(): pl.pallas_call(lambda *refs: finish_kernel(scale, *refs), out_shape=(out,...  10.7 us
    pallas_call x1, Pallas kernels, gram_call(): pl.pallas_call(gram_kernel, out_shape=(jax.ShapeDtypeStruct((256, 256), j...  10.5 us
    pallas_call x1, Pallas kernels, pack_call(): pl.pallas_call(pack_kernel, out_shape=tuple((jax.ShapeDtypeStruct(s, jnp....  2.94 us
  transfers between devices with their start and end apart: 6, of which 1 were waited for; matrix products, arithmetic and copies ran while one was open for 0% of the time, Pallas kernels for 0%

profile of v9, /device:TPU:1, one launch (start us, length us, event | category | flops | bytes accessed | tf_op | source)
XLA Modules:
  0.0 114.0 jit_solution(13602790220999886318)
XLA Ops:
  0.6 2.9 %shard_map.50 = (f32[25,48,128]{2,1,0:T(8,128)}, f32[9,48,128]{2,1,0:T(8,128)}, f32[13,48,128]{2,1,0:T(8,128)}, f32[5,48,128]{2,1,0:T(8,128)}) custom-call(f32[1536,128]{1,0:T(8,128)} %bitcast.9, f32[1536,128]{1,0:T(8,128)} %bitcast.11, f32[3,4,8,128]{3,2,1,0:T(8,128)} %off_hbm.1), custom_call_target="tpu_custom_call" | custom-call | tf_op jit(solution)/shard_map/pallas_call | solution.py:260
  3.6 1.3 %collective-permute-start = (f32[25,48,128]{2,1,0:T(8,128)}, f32[25,48,128]{2,1,0:T(8,128)S(1)}, u32[]{:S(2)}, u32[]{:S(2)}) collective-permute-start(f32[25,48,128]{2,1,0:T(8,128)} %get-tuple-element.10), channel_id=1, source_target_pairs={{32,0},{33,1},{34,2},{35,3},{36,4},{37,5},{38,6},{39,7},{40,8},{41... | collective-permute-start | bytes 1843208 | tf_op jit(solution)/shard_map/ppermute | solution.py:510
  4.9 4.6 %collective-permute-start.1 = (f32[9,48,128]{2,1,0:T(8,128)}, f32[9,48,128]{2,1,0:T(8,128)S(1)}, u32[]{:S(2)}, u32[]{:S(2)}) collective-permute-start(f32[9,48,128]{2,1,0:T(8,128)} %get-tuple-element.11), channel_id=1, source_target_pairs={{0,32},{1,33},{2,34},{3,35},{4,36},{5,37},{6,38},{7,39},{8,40},{9,... | collective-permute-start | bytes 663560 | tf_op jit(solution)/shard_map/ppermute | solution.py:510
  9.4 4.9 %collective-permute-start.3 = (f32[5,48,128]{2,1,0:T(8,128)}, f32[5,48,128]{2,1,0:T(8,128)S(1)}, u32[]{:S(2)}, u32[]{:S(2)}) collective-permute-start(f32[5,48,128]{2,1,0:T(8,128)} %get-tuple-element.13), channel_id=1, source_target_pairs={{0,1},{1,2},{2,3},{3,4},{4,5},{5,6},{6,7},{7,8},{8,9},{9,10},{10,1... | collective-permute-start | bytes 368648 | tf_op jit(solution)/shard_map/ppermute | solution.py:510
  14.4 5.1 %collective-permute-start.2 = (f32[13,48,128]{2,1,0:T(8,128)}, f32[13,48,128]{2,1,0:T(8,128)S(1)}, u32[]{:S(2)}, u32[]{:S(2)}) collective-permute-start(f32[13,48,128]{2,1,0:T(8,128)} %get-tuple-element.12), channel_id=1, source_target_pairs={{1,0},{2,1},{3,2},{4,3},{5,4},{6,5},{7,6},{8,7},{9,8},{10,9},{11,1... | collective-permute-start | bytes 958472 | tf_op jit(solution)/shard_map/ppermute | solution.py:510
  19.5 0.0 collective-permute-done.1.up_a
  19.6 0.0 collective-permute-done.down_a
  19.6 5.0 %collective-permute-start.4 = (f32[8,48,128]{2,1,0:T(8,128)S(1)}, f32[8,48,128]{2,1,0:T(8,128)S(1)}, u32[]{:S(2)}, u32[]{:S(2)}) collective-permute-start(f32[8,48,128]{2,1,0:T(8,128)S(1)} %pad_maximum_fusion), channel_id=1, source_target_pairs={{1,0},{2,1},{3,2},{4,3},{5,4},{6,5},{7,6},{8,7},{9,8},{10,9},{11,1... | collective-permute-start | bytes 589832 | tf_op jit(solution)/shard_map/ppermute | solution.py:510
  24.7 3.5 %collective-permute-start.5 = (f32[4,48,128]{2,1,0:T(8,128)S(1)}, f32[4,48,128]{2,1,0:T(8,128)S(1)}, u32[]{:S(2)}, u32[]{:S(2)}) collective-permute-start(f32[4,48,128]{2,1,0:T(8,128)S(1)} %pad_maximum_fusion.1), channel_id=1, source_target_pairs={{0,1},{1,2},{2,3},{3,4},{4,5},{5,6},{6,7},{7,8},{8,9},{9,10},{10,1... | collective-permute-start | bytes 294920 | tf_op jit(solution)/shard_map/ppermute | solution.py:510
  28.2 0.1 pad_add_fusion.start_ref
  28.3 0.0 collective-permute-done.3.up_b
  28.3 0.0 collective-permute-done.2.down_b
  28.3 1.5 %collective-permute-done.5.up_c = f32[4,48,128]{2,1,0:T(8,128)S(1)} collective-permute-done((f32[4,48,128]{2,1,0:T(8,128)S(1)}, f32[4,48,128]{2,1,0:T(8,128)S(1)}, u32[]{:S(2)}, u32[]{:S(2)}) %collective-permute-start.5) | collective-permute-done | bytes 98336 | tf_op jit(solution)/shard_map/ppermute | solution.py:510
  29.8 0.0 collective-permute-done.4.down_c
  29.8 0.0 copy-start
  29.8 0.8 copy-done
  30.6 10.5 %shard_map.51 = (f32[256,256]{1,0:T(8,128)S(1)}, f32[4,8,192,128]{3,2,1,0:T(8,128)}) custom-call(s32[4]{0:T(128)S(1)} %pad_add_fusion.start_ref, f32[1536,128]{1,0:T(8,128)} %bitcast.10, f32[1536,128]{1,0:T(8,128)} %bitcast.12, f32[25,48,128]{2,1,0:T(8,128)S(1)} %collective-permute-done.down_a, f32[9,48,128]{2,1,0:T(8,128)S(1)} %collective-permute-done.1.up_a, ...), custom_call_target="tpu_custom_call" | custom-call | tf_op jit(solution)/shard_map/pallas_call | solution.py:429
  41.1 17.7 %all_to_all.15 = f32[32,8,256]{2,1,0:T(8,128)S(1)} all-to-all(f32[32,8,256]{2,1,0:T(8,128)S(1)} %bitcast.8), channel_id=1, replica_groups=mesh['px'=16,'pz'=16,'pc'=2] {'px','pc'}, dimensions={0} | all-to-all | bytes 524288 | tf_op jit(solution)/shard_map/all_to_all | solution.py:494
  58.9 28.9 %all_to_all.16 = f32[16,8,256]{2,1,0:T(8,128)S(1)} all-to-all(f32[16,8,256]{2,1,0:T(8,128)S(1)} %broadcast_in_dim.4), channel_id=1, replica_groups=mesh['px'=16,'pz'=16,'pc'=2] {'pz'}, dimensions={0} | all-to-all | bytes 262144 | tf_op jit(solution)/shard_map/all_to_all | solution.py:496
  87.8 15.3 %all_to_all.17 = f32[32,8,256]{2,1,0:T(8,128)} all-to-all(f32[32,8,256]{2,1,0:T(8,128)S(1)} %broadcast_in_dim.5), channel_id=1, replica_groups=mesh['px'=16,'pz'=16,'pc'=2] {'px','pc'}, dimensions={0} | all-to-all | bytes 524288 | tf_op jit(solution)/shard_map/all_to_all | solution.py:498
  103.1 10.7 %shard_map.52 = (f32[1536,128]{1,0:T(8,128)}, f32[1536,128]{1,0:T(8,128)}) custom-call(f32[256,256]{1,0:T(8,128)} %bitcast.13, f32[4,8,192,128]{3,2,1,0:T(8,128)} %get-tuple-element.15.refs_1_), custom_call_target="tpu_custom_call" | custom-call | tf_op jit(solution)/shard_map/pallas_call | solution.py:479
  (10 shorter events, 0.1 us)
Async XLA Ops:
  3.6 16.0 %collective-permute-start = (f32[25,48,128]{2,1,0:T(8,128)}, f32[25,48,128]{2,1,0:T(8,128)S(1)}, u32[]{:S(2)}, u32[]{:S(2)}) collective-permute-start(f32[25,48,128]{2,1,0:T(8,128)} %get-tuple-element.10), channel_id=1, source_target_pairs={{32,0},{33,1},{34,2},{35,3},{36,4},{37,5},{38,6},{39,7},{40,8},{41... | collective-permute-start | bytes 1843208 | tf_op jit(solution)/shard_map/ppermute | solution.py:510
  4.9 14.7 %collective-permute-start.1 = (f32[9,48,128]{2,1,0:T(8,128)}, f32[9,48,128]{2,1,0:T(8,128)S(1)}, u32[]{:S(2)}, u32[]{:S(2)}) collective-permute-start(f32[9,48,128]{2,1,0:T(8,128)} %get-tuple-element.11), channel_id=1, source_target_pairs={{0,32},{1,33},{2,34},{3,35},{4,36},{5,37},{6,38},{7,39},{8,40},{9,... | collective-permute-start | bytes 663560 | tf_op jit(solution)/shard_map/ppermute | solution.py:510
  9.4 18.8 %collective-permute-start.3 = (f32[5,48,128]{2,1,0:T(8,128)}, f32[5,48,128]{2,1,0:T(8,128)S(1)}, u32[]{:S(2)}, u32[]{:S(2)}) collective-permute-start(f32[5,48,128]{2,1,0:T(8,128)} %get-tuple-element.13), channel_id=1, source_target_pairs={{0,1},{1,2},{2,3},{3,4},{4,5},{5,6},{6,7},{7,8},{8,9},{9,10},{10,1... | collective-permute-start | bytes 368648 | tf_op jit(solution)/shard_map/ppermute | solution.py:510
  14.4 13.9 %collective-permute-start.2 = (f32[13,48,128]{2,1,0:T(8,128)}, f32[13,48,128]{2,1,0:T(8,128)S(1)}, u32[]{:S(2)}, u32[]{:S(2)}) collective-permute-start(f32[13,48,128]{2,1,0:T(8,128)} %get-tuple-element.12), channel_id=1, source_target_pairs={{1,0},{2,1},{3,2},{4,3},{5,4},{6,5},{7,6},{8,7},{9,8},{10,9},{11,1... | collective-permute-start | bytes 958472 | tf_op jit(solution)/shard_map/ppermute | solution.py:510
  19.6 10.2 %collective-permute-start.4 = (f32[8,48,128]{2,1,0:T(8,128)S(1)}, f32[8,48,128]{2,1,0:T(8,128)S(1)}, u32[]{:S(2)}, u32[]{:S(2)}) collective-permute-start(f32[8,48,128]{2,1,0:T(8,128)S(1)} %pad_maximum_fusion), channel_id=1, source_target_pairs={{1,0},{2,1},{3,2},{4,3},{5,4},{6,5},{7,6},{8,7},{9,8},{10,9},{11,1... | collective-permute-start | bytes 589832 | tf_op jit(solution)/shard_map/ppermute | solution.py:510
  24.7 5.1 %collective-permute-start.5 = (f32[4,48,128]{2,1,0:T(8,128)S(1)}, f32[4,48,128]{2,1,0:T(8,128)S(1)}, u32[]{:S(2)}, u32[]{:S(2)}) collective-permute-start(f32[4,48,128]{2,1,0:T(8,128)S(1)} %pad_maximum_fusion.1), channel_id=1, source_target_pairs={{0,1},{1,2},{2,3},{3,4},{4,5},{5,6},{6,7},{7,8},{8,9},{9,10},{10,1... | collective-permute-start | bytes 294920 | tf_op jit(solution)/shard_map/ppermute | solution.py:510
  29.8 0.8 copy-start
